TPU v7x, 32 devices: a whole 2x2x4 slice. The times are simulated.
32 devices in a mesh: expert: 2 (over x), fsdp: 16 (over z, y, core).
Axes of the slice: x: 2, y: 2, z: 4, core: 2. Of those that a mesh axis runs over, the one named last changes fastest.
Arguments:
- inputs: bfloat16 [31360, 512], P(('expert', 'fsdp')), may hold values from -6 to 6
- cotangent: bfloat16 [31360, 512], P(('expert', 'fsdp')), may hold values from -6 to 6
- routes: int32 [31360, 2], P(('expert', 'fsdp')), may hold values from 0 to 7, as said below
- slots: int32 [31360, 2], P(('expert', 'fsdp')), may hold values from -1 to 257, as said below
- qkv_weight: bfloat16 [512, 1536], P('fsdp'), may hold values from -0.25 to 0.25
- out_weight: bfloat16 [512, 512], P('fsdp'), may hold values from -0.75 to 0.75
- router_weight: bfloat16 [512, 8], P('fsdp'), may hold values from -0.1875 to 0.1875
- norm1_gain: bfloat16 [512], P('fsdp'), may hold values from 0.5 to 1.5
- norm1_shift: bfloat16 [512], P('fsdp'), may hold values from -1 to 1
- norm2_gain: bfloat16 [512], P('fsdp'), may hold values from 0.5 to 1.5
- norm2_shift: bfloat16 [512], P('fsdp'), may hold values from -1 to 1
- expert_up: bfloat16 [8, 512, 2048], P('expert', 'fsdp'), may hold values from -0.25 to 0.25
- expert_down: bfloat16 [8, 2048, 512], P('expert', 'fsdp'), may hold values from -0.875 to 0.875
Outputs:
- output: bfloat16 [31360, 512], P(('expert', 'fsdp'))
- input_grad: float32 [31360, 512], P(('expert', 'fsdp'))
- qkv_grad: float32 [512, 1536], P('fsdp')
- out_grad: float32 [512, 512], P('fsdp')
- router_grad: float32 [512, 8], P('fsdp')
- norm1_gain_grad: float32 [512], P('fsdp')
- norm1_shift_grad: float32 [512], P('fsdp')
- norm2_gain_grad: float32 [512], P('fsdp')
- norm2_shift_grad: float32 [512], P('fsdp')
- up_grad: float32 [8, 512, 2048], P('expert', 'fsdp')
- down_grad: float32 [8, 2048, 512], P('expert', 'fsdp')
Inputs may be any that keep to these rules, and one draw needn't show every extreme that they name: `routes`: each row names two different experts. Within the 980 rows of one device and for each expert, the kept routes hold slots 0, 1, 2, ... once each without gaps, all first routes (column 0) before second ones, each column in one order of priority over the device's patches; a route with slot -1 is dropped and so is every later route to that expert. In every device's rows some expert fills all 258 slots.
All inputs are finite; a program needn't handle non-finite values.
Results may differ from a plain program's by a relative error of at most 0.024.
Values may be sent and summed in bfloat16 or wider, within the bound.
A program may use at most 192 MiB of HBM per device.

v0:
```python
import jax
import jax.numpy as jnp
from jax import lax
from jax.sharding import PartitionSpec as P

HEADS = 8
HEAD_DIM = 64
PATCHES = 49


EPS = 1e-06
ROOT_HALF = 0.7071067811865476
DENSITY_SCALE = 0.3989422804014327


def inner_rows(left, right):
    return lax.dot_general(
        left, right, (((0,), (0,)), ((), ())), preferred_element_type=jnp.float32
    )


def against_rows(left, right):
    return lax.dot_general(
        left, right, (((1,), (1,)), ((), ())), preferred_element_type=jnp.float32
    )


def norm_forward(values):
    center = jnp.mean(values, axis=-1, keepdims=True)
    offset = values - center
    spread = jnp.mean(offset * offset, axis=-1, keepdims=True)
    inverse = lax.rsqrt(spread + EPS)
    return (offset * inverse, inverse)


def norm_backward(upstream, normed, inverse, gain):
    scaled = upstream * gain
    inner = (
        scaled
        - jnp.mean(scaled, axis=-1, keepdims=True)
        - normed * jnp.mean(scaled * normed, axis=-1, keepdims=True)
    )
    return (inverse * inner, jnp.sum(upstream * normed, axis=0), jnp.sum(upstream, axis=0))


def attention_scores(queries, keys_all):
    return jnp.einsum(
        "iqhd,ikhd->ihqk", queries, keys_all, preferred_element_type=jnp.float32
    ) * HEAD_DIM ** (-0.5)


def expert_forward(operands):
    expert_rows, up_matrix, down_matrix = operands
    hidden = jnp.dot(expert_rows, up_matrix, preferred_element_type=jnp.float32)
    active = jax.nn.gelu(hidden, approximate=False).astype(jnp.bfloat16)
    return jnp.dot(active, down_matrix, preferred_element_type=jnp.float32).astype(jnp.bfloat16)


def expert_backward(operands):
    expert_rows, grad_rows, up_matrix, down_matrix = operands
    hidden = jnp.dot(expert_rows, up_matrix, preferred_element_type=jnp.float32)
    active = jax.nn.gelu(hidden, approximate=False).astype(jnp.bfloat16)
    down_part = inner_rows(active, grad_rows)
    grad_active = against_rows(grad_rows, down_matrix)
    slope = 0.5 * (1.0 + lax.erf(hidden * ROOT_HALF)) + hidden * DENSITY_SCALE * jnp.exp(
        -0.5 * hidden * hidden
    )
    grad_hidden = (grad_active * slope).astype(jnp.bfloat16)
    up_part = inner_rows(expert_rows, grad_hidden)
    grad_input = against_rows(grad_hidden, up_matrix).astype(jnp.bfloat16)
    return (up_part, down_part, grad_input)


def on_device(
    inputs,
    cotangent,
    routes,
    slots,
    qkv_weight,
    out_weight,
    router_weight,
    norm1_gain,
    norm1_shift,
    norm2_gain,
    norm2_shift,
    expert_up,
    expert_down,
):
    rows_dev = inputs.shape[0]
    images = rows_dev // PATCHES
    model_width = inputs.shape[1]
    experts = expert_up.shape[0] * lax.axis_size("expert")
    capacity = (42 * rows_dev + 20 * experts - 1) // (20 * experts)
    triple_weight, out_full, router_full, gain_one, shift_one, gain_two, shift_two = (
        lax.all_gather(qkv_weight, "fsdp", axis=0, tiled=True),
        lax.all_gather(out_weight, "fsdp", axis=0, tiled=True),
        lax.all_gather(router_weight, "fsdp", axis=0, tiled=True),
        lax.all_gather(norm1_gain, "fsdp", axis=0, tiled=True),
        lax.all_gather(norm1_shift, "fsdp", axis=0, tiled=True),
        lax.all_gather(norm2_gain, "fsdp", axis=0, tiled=True),
        lax.all_gather(norm2_shift, "fsdp", axis=0, tiled=True),
    )
    up_full, down_full = (
        lax.all_gather(expert_up, "fsdp", axis=1, tiled=True),
        lax.all_gather(expert_down, "fsdp", axis=1, tiled=True),
    )
    hidden_in = inputs.astype(jnp.float32)
    normed_one, inverse_one = norm_forward(hidden_in)
    act_one = (normed_one * gain_one.astype(jnp.float32) + shift_one.astype(jnp.float32)).astype(
        jnp.bfloat16
    )
    triple = jnp.dot(act_one, triple_weight, preferred_element_type=jnp.float32).astype(
        jnp.bfloat16
    )
    triple = triple.reshape(images, PATCHES, 3, HEADS, HEAD_DIM)
    queries = triple[:, :, 0]
    keys_all = triple[:, :, 1]
    values = triple[:, :, 2]
    scores = attention_scores(queries, keys_all)
    log_total = jax.nn.logsumexp(scores, axis=-1, keepdims=True)
    weights = jnp.exp(scores - log_total).astype(jnp.bfloat16)
    attended = jnp.einsum("ihqk,ikhd->iqhd", weights, values, preferred_element_type=jnp.float32)
    attended = attended.reshape(rows_dev, model_width).astype(jnp.bfloat16)
    hidden_mid = hidden_in + jnp.dot(attended, out_full, preferred_element_type=jnp.float32)
    normed_two, inverse_two = norm_forward(hidden_mid)
    act_two = (normed_two * gain_two.astype(jnp.float32) + shift_two.astype(jnp.float32)).astype(
        jnp.bfloat16
    )
    logits = jnp.dot(act_two, router_full, preferred_element_type=jnp.float32)
    router_probs = jax.nn.softmax(logits, axis=-1)
    expert_ids = jnp.arange(experts, dtype=jnp.int32)
    chosen = (routes[:, :, None] == expert_ids).astype(jnp.float32)
    gate_values = jnp.sum(chosen * router_probs[:, None, :], axis=2)
    gate_first = gate_values[:, 0:1]
    gate_second = gate_values[:, 1:2]
    slot_ids = jnp.where(slots >= 0, routes * capacity + slots, -1)
    columns = jnp.arange(experts * capacity, dtype=jnp.int32)
    picks = (jnp.transpose(slot_ids).reshape(2 * rows_dev, 1) == columns).astype(jnp.bfloat16)
    doubled = jnp.concatenate([act_two, act_two], axis=0)
    sent = inner_rows(picks, doubled).astype(jnp.bfloat16).reshape(experts, capacity, model_width)
    arrived = lax.all_to_all(sent, "expert", split_axis=0, concat_axis=1, tiled=True)
    produced = lax.map(expert_forward, (arrived, up_full, down_full))
    returned = lax.all_to_all(produced, "expert", split_axis=1, concat_axis=0, tiled=True)
    selected = jnp.dot(
        picks, returned.reshape(experts * capacity, model_width), preferred_element_type=jnp.float32
    )
    selected_first = selected[:rows_dev]
    selected_second = selected[rows_dev:]
    output = (hidden_mid + gate_first * selected_first + gate_second * selected_second).astype(
        jnp.bfloat16
    )
    grad_out = cotangent.astype(jnp.float32)
    grad_selected = jnp.concatenate([gate_first * grad_out, gate_second * grad_out], axis=0).astype(
        jnp.bfloat16
    )
    grad_gate_first = jnp.sum(grad_out * selected_first, axis=-1, keepdims=True)
    grad_gate_second = jnp.sum(grad_out * selected_second, axis=-1, keepdims=True)
    grad_returned = (
        inner_rows(picks, grad_selected)
        .astype(jnp.bfloat16)
        .reshape(experts, capacity, model_width)
    )
    up_back, down_back = (
        lax.all_gather(expert_up, "fsdp", axis=1, tiled=True),
        lax.all_gather(expert_down, "fsdp", axis=1, tiled=True),
    )
    grad_arrived = lax.all_to_all(grad_returned, "expert", split_axis=0, concat_axis=1, tiled=True)
    up_part, down_part, grad_dispatched = lax.map(
        expert_backward, (arrived, grad_arrived, up_back, down_back)
    )
    grad_sent = lax.all_to_all(grad_dispatched, "expert", split_axis=1, concat_axis=0, tiled=True)
    up_grad, down_grad = (
        lax.psum_scatter(
            up_part.astype(jnp.bfloat16), "fsdp", scatter_dimension=1, tiled=True
        ).astype(jnp.float32),
        lax.psum_scatter(
            down_part.astype(jnp.bfloat16), "fsdp", scatter_dimension=1, tiled=True
        ).astype(jnp.float32),
    )
    triple_back, out_back, router_back, gain_one_back, gain_two_back = (
        lax.all_gather(qkv_weight, "fsdp", axis=0, tiled=True),
        lax.all_gather(out_weight, "fsdp", axis=0, tiled=True),
        lax.all_gather(router_weight, "fsdp", axis=0, tiled=True),
        lax.all_gather(norm1_gain, "fsdp", axis=0, tiled=True),
        lax.all_gather(norm2_gain, "fsdp", axis=0, tiled=True),
    )
    gathered_grad = jnp.dot(
        picks,
        grad_sent.reshape(experts * capacity, model_width),
        preferred_element_type=jnp.float32,
    )
    grad_probs = chosen[:, 0, :] * grad_gate_first + chosen[:, 1, :] * grad_gate_second
    grad_logits = (
        router_probs * (grad_probs - jnp.sum(grad_probs * router_probs, axis=-1, keepdims=True))
    ).astype(jnp.bfloat16)
    router_part = inner_rows(act_two, grad_logits)
    grad_act_two = (
        gathered_grad[:rows_dev] + gathered_grad[rows_dev:] + against_rows(grad_logits, router_back)
    )
    grad_mid_norm, gain_two_part, shift_two_part = norm_backward(
        grad_act_two, normed_two, inverse_two, gain_two_back.astype(jnp.float32)
    )
    grad_mid = grad_out + grad_mid_norm
    grad_branch = grad_mid.astype(jnp.bfloat16)
    out_part = inner_rows(attended, grad_branch)
    grad_attended = (
        against_rows(grad_branch, out_back)
        .astype(jnp.bfloat16)
        .reshape(images, PATCHES, HEADS, HEAD_DIM)
    )
    probs_again = jnp.exp(attention_scores(queries, keys_all) - log_total)
    weights_again = probs_again.astype(jnp.bfloat16)
    grad_weights = jnp.einsum(
        "iqhd,ikhd->ihqk", grad_attended, values, preferred_element_type=jnp.float32
    )
    grad_values = jnp.einsum(
        "ihqk,iqhd->ikhd", weights_again, grad_attended, preferred_element_type=jnp.float32
    )
    grad_scores = (
        probs_again * (grad_weights - jnp.sum(grad_weights * probs_again, axis=-1, keepdims=True))
    ).astype(jnp.bfloat16)
    grad_queries = jnp.einsum(
        "ihqk,ikhd->iqhd", grad_scores, keys_all, preferred_element_type=jnp.float32
    ) * HEAD_DIM ** (-0.5)
    grad_keys = jnp.einsum(
        "ihqk,iqhd->ikhd", grad_scores, queries, preferred_element_type=jnp.float32
    ) * HEAD_DIM ** (-0.5)
    grad_triple = (
        jnp.stack([grad_queries, grad_keys, grad_values], axis=2)
        .astype(jnp.bfloat16)
        .reshape(rows_dev, 3 * model_width)
    )
    triple_part = inner_rows(act_one, grad_triple)
    grad_act_one = against_rows(grad_triple, triple_back)
    grad_in_norm, gain_one_part, shift_one_part = norm_backward(
        grad_act_one, normed_one, inverse_one, gain_one_back.astype(jnp.float32)
    )
    input_grad = grad_mid + grad_in_norm
    totals = (
        lax.psum(triple_part.astype(jnp.bfloat16), "expert").astype(jnp.float32),
        lax.psum(out_part.astype(jnp.bfloat16), "expert").astype(jnp.float32),
        lax.psum(router_part.astype(jnp.bfloat16), "expert").astype(jnp.float32),
        lax.psum(gain_one_part.astype(jnp.bfloat16), "expert").astype(jnp.float32),
        lax.psum(shift_one_part.astype(jnp.bfloat16), "expert").astype(jnp.float32),
        lax.psum(gain_two_part.astype(jnp.bfloat16), "expert").astype(jnp.float32),
        lax.psum(shift_two_part.astype(jnp.bfloat16), "expert").astype(jnp.float32),
    )
    shares = (
        lax.psum_scatter(
            totals[0].astype(jnp.bfloat16), "fsdp", scatter_dimension=0, tiled=True
        ).astype(jnp.float32),
        lax.psum_scatter(
            totals[1].astype(jnp.bfloat16), "fsdp", scatter_dimension=0, tiled=True
        ).astype(jnp.float32),
        lax.psum_scatter(
            totals[2].astype(jnp.bfloat16), "fsdp", scatter_dimension=0, tiled=True
        ).astype(jnp.float32),
        lax.psum_scatter(
            totals[3].astype(jnp.bfloat16), "fsdp", scatter_dimension=0, tiled=True
        ).astype(jnp.float32),
        lax.psum_scatter(
            totals[4].astype(jnp.bfloat16), "fsdp", scatter_dimension=0, tiled=True
        ).astype(jnp.float32),
        lax.psum_scatter(
            totals[5].astype(jnp.bfloat16), "fsdp", scatter_dimension=0, tiled=True
        ).astype(jnp.float32),
        lax.psum_scatter(
            totals[6].astype(jnp.bfloat16), "fsdp", scatter_dimension=0, tiled=True
        ).astype(jnp.float32),
    )
    return (
        output,
        input_grad,
        shares[0],
        shares[1],
        shares[2],
        shares[3],
        shares[4],
        shares[5],
        shares[6],
        up_grad,
        down_grad,
    )


def solution(mesh):
    in_specs = (
        P(("expert", "fsdp"), None),
        P(("expert", "fsdp"), None),
        P(("expert", "fsdp"), None),
        P(("expert", "fsdp"), None),
        P("fsdp", None),
        P("fsdp", None),
        P("fsdp", None),
        P("fsdp"),
        P("fsdp"),
        P("fsdp"),
        P("fsdp"),
        P("expert", "fsdp", None),
        P("expert", "fsdp", None),
    )
    out_specs = (
        P(("expert", "fsdp"), None),
        P(("expert", "fsdp"), None),
        P("fsdp", None),
        P("fsdp", None),
        P("fsdp", None),
        P("fsdp"),
        P("fsdp"),
        P("fsdp"),
        P("fsdp"),
        P("expert", "fsdp", None),
        P("expert", "fsdp", None),
    )
    return jax.shard_map(
        on_device, mesh=mesh, in_specs=in_specs, out_specs=out_specs, check_vma=False
    )
```

profile of v0, /device:TPU:28, one launch (start us, length us, event | category | flops | bytes accessed | tf_op | source)
XLA Modules:
  0.0 980.0 jit_solution(15997492674302908760)
XLA Ops:
  14.8 26.6 %all-reduce.9 = (bf16[512]{0:T(512)(128)(2,1)S(1)}, bf16[512]{0:T(512)(128)(2,1)S(1)}, bf16[512]{0:T(512)(128)(2,1)S(1)}, bf16[512]{0:T(512)(128)(2,1)S(1)}) all-reduce(bf16[512]{0:T(512)(128)(2,1)S(1)} %dynamic-update-slice.1, bf16[512]{0:T(512)(128)(2,1)S(1)} %dynamic-update-slice, ...), channel_id=1, replica_groups=mesh['expert'=2,'fsdp'=16] {'fsdp'}, use_global_device_ids=true, to_apply=%add.1 | all-reduce | flops 2048 | bytes 8192
  45.5 25.4 %all_gather.37 = bf16[512,512]{1,0:T(8,128)(2,1)S(1)} all-gather(bf16[32,512]{1,0:T(8,128)(2,1)} %param.22), channel_id=1, replica_groups=mesh['expert'=2,'fsdp'=16] {'fsdp'}, dimensions={0}, use_global_device_ids=true | all-gather | bytes 557056 | tf_op jit(solution)/shard_map/all_gather | solution.py:96
  76.3 8.4 reshape.117
  102.0 6.9 fusion.191
  115.5 26.5 %all-to-all-done = bf16[8,258,512]{2,1,0:T(8,128)(2,1)S(1)} async-done(((bf16[8,258,512]{2,1,0:T(8,128)(2,1)}), bf16[8,258,512]{2,1,0:T(8,128)(2,1)S(1)}, u32[]{:S(2)}, u32[]{:S(2)}) %all-to-all-start) | async-done | bytes 2113568 | tf_op jit(solution)/shard_map/all_to_all | solution.py:141
  146.4 54.5 %all-gather.9.cloned.1.call-done = bf16[4,2048,512]{2,1,0:T(8,128)(2,1)} async-done(((bf16[4,128,512]{2,1,0:T(8,128)(2,1)}), bf16[4,2048,512]{2,1,0:T(8,128)(2,1)}) %all-gather.9.cloned.1.call-update) | async-done | bytes 8388624 | tf_op jit(solution)/shard_map/all_gather | solution.py:105
  202.4 56.3 %while.24 = (s32[]{:T(128)}, bf16[4,516,512]{2,1,0:T(8,128)(2,1)}, bf16[4,516,512]{2,1,0:T(8,128)(2,1)S(1)}, bf16[4,512,2048]{2,1,0:T(8,128)(2,1)}, bf16[4,2048,512]{2,1,0:T(8,128)(2,1)}, /*index=5*/s32[]{:T(128)}) while((s32[]{:T(128)}, bf16[4,516,512]{2,1,0:T(8,128)(2,1)}, bf16[4,516,512]{2,1,0:T(8,128)(2,1)S(1)}, ...), condition=%wide.region_10.11_spmd, body=%wide.region_9.10_spmd.sunk | while | flops 2233214976 | bytes 5261389 | solution.py:142
  202.4 14.1 %fusion.294 = bf16[4,516,512]{2,1,0:T(8,128)(2,1)} fusion(bf16[4,516,512]{2,1,0:T(8,128)(2,1)} %get-tuple-element.248, s32[]{:T(128)S(6)} %copy.119, bf16[4,2048,512]{2,1,0:T(8,128)(2,1)} %get-tuple-element.257, bf16[4,512,2048]{2,1,0:T(8,128)(2,1)} %get-tuple-element.256, bf16[4,516,512]{2,1,0:T(8,128)(2,1)S(1)} %get-tuple-element.255), kind=kOutput, calls=%fused_computation.27.clone.1 | convolution fusion | flops 2233214976 | bytes 5261312 | tf_op jit(solution)/shard_map/while/body/eval_jaxpr/dot_general | solution.py:56
  216.4 14.1 %fusion.294 = bf16[4,516,512]{2,1,0:T(8,128)(2,1)} fusion(bf16[4,516,512]{2,1,0:T(8,128)(2,1)} %get-tuple-element.248, s32[]{:T(128)S(6)} %copy.119, bf16[4,2048,512]{2,1,0:T(8,128)(2,1)} %get-tuple-element.257, bf16[4,512,2048]{2,1,0:T(8,128)(2,1)} %get-tuple-element.256, bf16[4,516,512]{2,1,0:T(8,128)(2,1)S(1)} %get-tuple-element.255), kind=kOutput, calls=%fused_computation.27.clone.1 | convolution fusion | flops 2233214976 | bytes 5261312 | tf_op jit(solution)/shard_map/while/body/eval_jaxpr/dot_general | solution.py:56
  230.5 14.1 %fusion.294 = bf16[4,516,512]{2,1,0:T(8,128)(2,1)} fusion(bf16[4,516,512]{2,1,0:T(8,128)(2,1)} %get-tuple-element.248, s32[]{:T(128)S(6)} %copy.119, bf16[4,2048,512]{2,1,0:T(8,128)(2,1)} %get-tuple-element.257, bf16[4,512,2048]{2,1,0:T(8,128)(2,1)} %get-tuple-element.256, bf16[4,516,512]{2,1,0:T(8,128)(2,1)S(1)} %get-tuple-element.255), kind=kOutput, calls=%fused_computation.27.clone.1 | convolution fusion | flops 2233214976 | bytes 5261312 | tf_op jit(solution)/shard_map/while/body/eval_jaxpr/dot_general | solution.py:56
  244.6 14.1 %fusion.294 = bf16[4,516,512]{2,1,0:T(8,128)(2,1)} fusion(bf16[4,516,512]{2,1,0:T(8,128)(2,1)} %get-tuple-element.248, s32[]{:T(128)S(6)} %copy.119, bf16[4,2048,512]{2,1,0:T(8,128)(2,1)} %get-tuple-element.257, bf16[4,512,2048]{2,1,0:T(8,128)(2,1)} %get-tuple-element.256, bf16[4,516,512]{2,1,0:T(8,128)(2,1)S(1)} %get-tuple-element.255), kind=kOutput, calls=%fused_computation.27.clone.1 | convolution fusion | flops 2233214976 | bytes 5261312 | tf_op jit(solution)/shard_map/while/body/eval_jaxpr/dot_general | solution.py:56
  267.7 17.6 %all-gather = bf16[16,32,8]{1,2,0:T(8,128)(2,1)S(1)} all-gather(bf16[1,32,8]{1,2,0:T(8,128)(2,1)S(1)} %bitcast.216), channel_id=1, replica_groups=mesh['expert'=2,'fsdp'=16] {'fsdp'}, dimensions={0}, use_global_device_ids=true | all-gather | bytes 8704 | tf_op jit(solution)/shard_map/all_gather | solution.py:97
  285.9 7.6 all-to-all-done.1
  300.1 6.6 fusion.185
  310.7 6.9 fusion.192
  325.6 25.5 %all-to-all-done.2 = bf16[8,258,512]{2,1,0:T(8,128)(2,1)} async-done(((bf16[8,258,512]{2,1,0:T(8,128)(2,1)}), bf16[8,258,512]{2,1,0:T(8,128)(2,1)}, u32[]{:S(2)}, u32[]{:S(2)}) %all-to-all-start.2) | async-done | bytes 2113568 | tf_op jit(solution)/shard_map/all_to_all | solution.py:167
  359.8 112.2 %while.25 = (s32[]{:T(128)}, bf16[4,512,2048]{2,1,0:T(8,128)(2,1)}, bf16[4,2048,512]{2,1,0:T(8,128)(2,1)}, bf16[4,516,512]{2,1,0:T(8,128)(2,1)}, bf16[4,516,512]...) while((s32[]{:T(128)}, bf16[4,512,2048]{2,1,0:T(8,128)(2,1)}, ...), condition=%wide.region_12.13_spmd, body=%wide.region_11.12_spmd.sunk | while | flops 5490173952 | bytes 162346256 | solution.py:168
  370.6 10.7 %bitcast_dynamic-update-slice_fusion.5 = bf16[4,2048,512]{2,1,0:T(8,128)(2,1)S(1)} fusion(bf16[4,2048,512]{2,1,0:T(8,128)(2,1)S(1)} %bitcast.209, s32[]{:T(128)S(6)} %copy.127, f32[516,2048]{1,0:T(8,128)S(1)} %fusion.305, bf16[4,516,512]{2,1,0:T(8,128)(2,1)S(1)} %copy-done.24), kind=kOutput, calls=%fused_computation.86.clone.1 | convolution fusion | flops 1150820352 | bytes 8987648 | tf_op jit(solution)/shard_map/while/body/eval_jaxpr/dot_general | solution.py:17
  398.7 10.7 %bitcast_dynamic-update-slice_fusion.5 = bf16[4,2048,512]{2,1,0:T(8,128)(2,1)S(1)} fusion(bf16[4,2048,512]{2,1,0:T(8,128)(2,1)S(1)} %bitcast.209, s32[]{:T(128)S(6)} %copy.127, f32[516,2048]{1,0:T(8,128)S(1)} %fusion.305, bf16[4,516,512]{2,1,0:T(8,128)(2,1)S(1)} %copy-done.24), kind=kOutput, calls=%fused_computation.86.clone.1 | convolution fusion | flops 1150820352 | bytes 8987648 | tf_op jit(solution)/shard_map/while/body/eval_jaxpr/dot_general | solution.py:17
  426.8 10.7 %bitcast_dynamic-update-slice_fusion.5 = bf16[4,2048,512]{2,1,0:T(8,128)(2,1)S(1)} fusion(bf16[4,2048,512]{2,1,0:T(8,128)(2,1)S(1)} %bitcast.209, s32[]{:T(128)S(6)} %copy.127, f32[516,2048]{1,0:T(8,128)S(1)} %fusion.305, bf16[4,516,512]{2,1,0:T(8,128)(2,1)S(1)} %copy-done.24), kind=kOutput, calls=%fused_computation.86.clone.1 | convolution fusion | flops 1150820352 | bytes 8987648 | tf_op jit(solution)/shard_map/while/body/eval_jaxpr/dot_general | solution.py:17
  454.8 10.7 %bitcast_dynamic-update-slice_fusion.5 = bf16[4,2048,512]{2,1,0:T(8,128)(2,1)S(1)} fusion(bf16[4,2048,512]{2,1,0:T(8,128)(2,1)S(1)} %bitcast.209, s32[]{:T(128)S(6)} %copy.127, f32[516,2048]{1,0:T(8,128)S(1)} %fusion.305, bf16[4,516,512]{2,1,0:T(8,128)(2,1)S(1)} %copy-done.24), kind=kOutput, calls=%fused_computation.86.clone.1 | convolution fusion | flops 1150820352 | bytes 8987648 | tf_op jit(solution)/shard_map/while/body/eval_jaxpr/dot_general | solution.py:17
  480.0 23.8 %all-to-all-done.3 = bf16[4,516,512]{2,0,1:T(4,128)(2,1)S(1)} async-done(((bf16[4,516,512]{2,0,1:T(4,128)(2,1)}), bf16[4,516,512]{2,0,1:T(4,128)(2,1)S(1)}, u32[]{:S(2)}, u32[]{:S(2)}) %all-to-all-start.3) | async-done | bytes 2113568 | tf_op jit(solution)/shard_map/all_to_all | solution.py:171
  509.2 6.7 fusion.183
  541.3 8.9 convert_element_type.177
  560.5 52.5 %reduce-scatter.12.cloned.1.call-done = bf16[32,1536]{1,0:T(8,128)(2,1)} async-done(((bf16[512,1536]{1,0:T(8,128)(2,1)}), bf16[32,1536]{1,0:T(8,128)(2,1)}) %reduce-scatter.12.cloned.1.call-update) | async-done | bytes 98320 | tf_op jit(solution)/shard_map/reduce_scatter | solution.py:249
  615.1 56.3 %reduce-scatter.16.cloned.1.call-done = bf16[32,8]{1,0:T(8,128)(2,1)} async-done(((bf16[512,8]{1,0:T(8,128)(2,1)}), bf16[32,8]{1,0:T(8,128)(2,1)}) %reduce-scatter.16.cloned.1.call-update) | async-done | bytes 528
  677.8 26.5 %all-reduce.8 = (bf16[512]{0:T(512)(128)(2,1)S(1)}, bf16[512]{0:T(512)(128)(2,1)S(1)}, bf16[512]{0:T(512)(128)(2,1)S(1)}, bf16[512]{0:T(512)(128)(2,1)S(1)}) all-reduce(bf16[512]{0:T(512)(128)(2,1)S(1)} %get-tuple-element.90, bf16[512]{0:T(512)(128)(2,1)S(1)} %get-tuple-element.95, ...), channel_id=5, replica_groups=mesh['expert'=2,'fsdp'=16] {'fsdp'}, use_global_device_ids=true, to_apply=%region_29.30.clone | all-reduce | flops 2048 | bytes 8192
  707.6 23.0 %reduce-scatter.14.cloned.1.call-done = bf16[32,512]{1,0:T(8,128)(2,1)} async-done(((bf16[512,512]{1,0:T(8,128)(2,1)}), bf16[32,512]{1,0:T(8,128)(2,1)}) %reduce-scatter.14.cloned.1.call-update) | async-done | bytes 32784 | tf_op jit(solution)/shard_map/reduce_scatter | solution.py:252
  730.6 9.1 all-reduce.10
  743.0 11.9 %all-reduce.13.cloned.1.call-done = bf16[32,1536]{1,0:T(8,128)(2,1)} async-done(((bf16[32,1536]{1,0:T(8,128)(2,1)}), bf16[32,1536]{1,0:T(8,128)(2,1)}) %all-reduce.13.cloned.1.call-update) | async-done | bytes 98320 | tf_op jit(solution)/shard_map/psum | solution.py:240
  756.5 105.9 %reduce-scatter.10.cloned.1.call-done = bf16[4,128,512]{2,1,0:T(8,128)(2,1)} async-done(((bf16[4,2048,512]{2,1,0:T(8,128)(2,1)}), bf16[4,128,512]{2,1,0:T(8,128)(2,1)}) %reduce-scatter.10.cloned.1.call-update) | async-done | bytes 524304 | tf_op jit(solution)/shard_map/reduce_scatter | solution.py:176
  864.5 106.3 %reduce-scatter.8.cloned.1.call-done = bf16[4,32,2048]{2,1,0:T(8,128)(2,1)} async-done(((bf16[4,512,2048]{2,1,0:T(8,128)(2,1)}), bf16[4,32,2048]{2,1,0:T(8,128)(2,1)}) %reduce-scatter.8.cloned.1.call-update) | async-done | bytes 524304 | tf_op jit(solution)/shard_map/reduce_scatter | solution.py:173
  (319 shorter events, 220.7 us)
Async XLA Ops:
  7.2 63.7 %all-gather.5.cloned.1.call-start = ((), (), s32[]{:S(2)}) async-start(), calls=%async_computation.9 | async-start | bytes 1671168 | tf_op jit(solution)/shard_map/all_gather | solution.py:95
  7.9 138.5 %all-gather.7.cloned.1.call-start = ((), (), s32[]{:S(2)}) async-start(), calls=%async_computation.10 | async-start | bytes 8912896 | tf_op jit(solution)/shard_map/all_gather | solution.py:104
  8.7 192.2 %all-gather.9.cloned.1.call-start = ((), (), s32[]{:S(2)}) async-start(), calls=%async_computation.11 | async-start | bytes 8912896 | tf_op jit(solution)/shard_map/all_gather | solution.py:105
  41.4 34.9 %copy-start.59 = (f32[512]{0:T(512)}, f32[512]{0:T(512)S(1)}, u32[]{:S(2)}) copy-start(f32[512]{0:T(512)S(1)} %convert_element_type.158) | copy-start | bytes 6148
  41.4 34.9 %copy-start.53 = (f32[512]{0:T(512)}, f32[512]{0:T(512)S(1)}, u32[]{:S(2)}) copy-start(f32[512]{0:T(512)S(1)} %convert_element_type.157) | copy-start | bytes 6148
  41.4 57.8 %copy-start.48 = (f32[512]{0:T(512)}, f32[512]{0:T(512)S(1)}, u32[]{:S(2)}) copy-start(f32[512]{0:T(512)S(1)} %convert_element_type.165) | copy-start | bytes 6148
  42.3 58.7 %copy-start.55 = (s32[1960]{0:T(1024)}, s32[1960]{0:T(1024)S(1)}, u32[]{:S(2)}) copy-start(s32[1960]{0:T(1024)S(1)} %eq.31) | copy-start | bytes 23524
  43.7 32.6 %copy-start.34 = (f32[980]{0:T(1024)}, f32[980]{0:T(1024)S(1)}, u32[]{:S(2)}) copy-start(f32[980]{0:T(1024)S(1)} %broadcast_multiply_fusion.5) | copy-start | bytes 11764
  45.4 30.9 %copy-start.50 = (f32[980]{0:T(1024)}, f32[980]{0:T(1024)S(1)}, u32[]{:S(2)}) copy-start(f32[980]{0:T(1024)S(1)} %add_rsqrt_fusion.1) | copy-start | bytes 11764
  70.8 27.1 %copy-start.22 = (bf16[512,512]{1,0:T(8,128)(2,1)}, bf16[512,512]{1,0:T(8,128)(2,1)S(1)}, u32[]{:S(2)}) copy-start(bf16[512,512]{1,0:T(8,128)(2,1)S(1)} %all_gather.37) | copy-start | bytes 1572868
  111.7 30.3 %all-to-all-start = ((bf16[8,258,512]{2,1,0:T(8,128)(2,1)}), bf16[8,258,512]{2,1,0:T(8,128)(2,1)S(1)}, u32[]{:S(2)}, u32[]{:S(2)}) async-start(bf16[8,258,512]{2,1,0:T(8,128)(2,1)} %reshape.118), calls=%async_computation | async-start | bytes 4325376 | tf_op jit(solution)/shard_map/all_to_all | solution.py:141
  258.7 26.7 %copy-start.31 = (s32[980,2]{0,1:T(2,128)S(1)}, s32[980,2]{0,1:T(2,128)}, u32[]{:S(2)}) copy-start(s32[980,2]{0,1:T(2,128)} %param.19) | copy-start | bytes 23524
  258.7 26.7 %copy-start.18 = (bf16[980,512]{1,0:T(8,128)(2,1)S(1)}, bf16[980,512]{1,0:T(8,128)(2,1)}, u32[]{:S(2)}) copy-start(bf16[980,512]{1,0:T(8,128)(2,1)} %copy-done.17) | copy-start | bytes 3010564
  262.9 30.6 %all-to-all-start.1 = ((bf16[4,516,512]{2,0,1:T(4,128)(2,1)}), bf16[4,516,512]{2,0,1:T(4,128)(2,1)}, u32[]{:S(2)}, u32[]{:S(2)}) async-start(bf16[4,516,512]{2,0,1:T(4,128)(2,1)} %copy.54), calls=%async_computation.1 | async-start | bytes 4227072 | tf_op jit(solution)/shard_map/all_to_all | solution.py:143
  285.4 14.7 %copy-start.46 = (bf16[512,8]{0,1:T(8,128)(2,1)}, bf16[512,8]{0,1:T(8,128)(2,1)S(1)}, u32[]{:S(2)}) copy-start(bf16[512,8]{0,1:T(8,128)(2,1)S(1)} %reshape.136) | copy-start | bytes 24580
  285.4 24.0 %copy-start.27 = (f32[980,2,8]{0,2,1:T(8,128)}, f32[980,2,8]{0,2,1:T(8,128)S(1)}, u32[]{:S(2)}) copy-start(f32[980,2,8]{0,2,1:T(8,128)S(1)} %fusion.233) | copy-start | bytes 188164
  320.7 30.4 %all-to-all-start.2 = ((bf16[8,258,512]{2,1,0:T(8,128)(2,1)}), bf16[8,258,512]{2,1,0:T(8,128)(2,1)}, u32[]{:S(2)}, u32[]{:S(2)}) async-start(bf16[8,258,512]{2,1,0:T(8,128)(2,1)} %reshape.120), calls=%async_computation.2 | async-start | bytes 4325376 | tf_op jit(solution)/shard_map/all_to_all | solution.py:167
  359.8 10.8 %slice-start.2 = ((s8[8388608]{0:T(1024)(128)(4,1)}), s8[4194304]{0:T(1024)(128)(4,1)S(1)}, s32[]{:S(2)}) async-start(s8[8388608]{0:T(1024)(128)(4,1)} %bitcast.208), calls=%async_computation.20 | async-start | bytes 8388608 | tf_op jit(solution)/shard_map/while
  366.7 14.7 %slice-start.4 = ((s8[8388608]{0:T(1024)(128)(4,1)}), s8[4194304]{0:T(1024)(128)(4,1)S(1)}, s32[]{:S(2)}) async-start(s8[8388608]{0:T(1024)(128)(4,1)} %bitcast.210), calls=%async_computation.22 | async-start | bytes 8388608 | tf_op jit(solution)/shard_map/while
  387.9 10.8 %slice-start.2 = ((s8[8388608]{0:T(1024)(128)(4,1)}), s8[4194304]{0:T(1024)(128)(4,1)S(1)}, s32[]{:S(2)}) async-start(s8[8388608]{0:T(1024)(128)(4,1)} %bitcast.208), calls=%async_computation.20 | async-start | bytes 8388608 | tf_op jit(solution)/shard_map/while
  394.7 14.7 %slice-start.4 = ((s8[8388608]{0:T(1024)(128)(4,1)}), s8[4194304]{0:T(1024)(128)(4,1)S(1)}, s32[]{:S(2)}) async-start(s8[8388608]{0:T(1024)(128)(4,1)} %bitcast.210), calls=%async_computation.22 | async-start | bytes 8388608 | tf_op jit(solution)/shard_map/while
  415.9 10.8 %slice-start.2 = ((s8[8388608]{0:T(1024)(128)(4,1)}), s8[4194304]{0:T(1024)(128)(4,1)S(1)}, s32[]{:S(2)}) async-start(s8[8388608]{0:T(1024)(128)(4,1)} %bitcast.208), calls=%async_computation.20 | async-start | bytes 8388608 | tf_op jit(solution)/shard_map/while
  422.8 14.7 %slice-start.4 = ((s8[8388608]{0:T(1024)(128)(4,1)}), s8[4194304]{0:T(1024)(128)(4,1)S(1)}, s32[]{:S(2)}) async-start(s8[8388608]{0:T(1024)(128)(4,1)} %bitcast.210), calls=%async_computation.22 | async-start | bytes 8388608 | tf_op jit(solution)/shard_map/while
  444.0 10.8 %slice-start.2 = ((s8[8388608]{0:T(1024)(128)(4,1)}), s8[4194304]{0:T(1024)(128)(4,1)S(1)}, s32[]{:S(2)}) async-start(s8[8388608]{0:T(1024)(128)(4,1)} %bitcast.208), calls=%async_computation.20 | async-start | bytes 8388608 | tf_op jit(solution)/shard_map/while
  450.9 14.7 %slice-start.4 = ((s8[8388608]{0:T(1024)(128)(4,1)}), s8[4194304]{0:T(1024)(128)(4,1)S(1)}, s32[]{:S(2)}) async-start(s8[8388608]{0:T(1024)(128)(4,1)} %bitcast.210), calls=%async_computation.22 | async-start | bytes 8388608 | tf_op jit(solution)/shard_map/while
  476.1 27.7 %all-to-all-start.3 = ((bf16[4,516,512]{2,0,1:T(4,128)(2,1)}), bf16[4,516,512]{2,0,1:T(4,128)(2,1)S(1)}, u32[]{:S(2)}, u32[]{:S(2)}) async-start(bf16[4,516,512]{2,0,1:T(4,128)(2,1)} %copy.58), calls=%async_computation.3 | async-start | bytes 4227072 | tf_op jit(solution)/shard_map/all_to_all | solution.py:171
  479.9 133.1 %reduce-scatter.12.cloned.1.call-start = ((), (), s32[]{:S(2)}) async-start(), calls=%async_computation.14 | async-start | bytes 1671168 | tf_op jit(solution)/shard_map/reduce_scatter | solution.py:249
  555.3 116.1 %reduce-scatter.16.cloned.1.call-start = ((), (), s32[]{:S(2)}) async-start(), calls=%async_computation.17 | async-start | bytes 139264
  557.6 173.0 %reduce-scatter.14.cloned.1.call-start = ((), (), s32[]{:S(2)}) async-start(), calls=%async_computation.16 | async-start | bytes 557056 | tf_op jit(solution)/shard_map/reduce_scatter | solution.py:252
  560.4 194.5 %all-reduce.13.cloned.1.call-start = ((), (), s32[]{:S(2)}) async-start(), calls=%async_computation.15 | async-start | bytes 196608 | tf_op jit(solution)/shard_map/psum | solution.py:240
  613.0 249.4 %reduce-scatter.10.cloned.1.call-start = ((), (), s32[]{:S(2)}) async-start(), calls=%async_computation.13 | async-start | bytes 8912896 | tf_op jit(solution)/shard_map/reduce_scatter | solution.py:176
  613.8 357.1 %reduce-scatter.8.cloned.1.call-start = ((), (), s32[]{:S(2)}) async-start(), calls=%async_computation.12 | async-start | bytes 8912896 | tf_op jit(solution)/shard_map/reduce_scatter | solution.py:173
  (69 other events, 349.5 us)
Sparse Core Ops, SparseCore 0:
  10.3 38.6 all-gather.4
  51.1 74.2 all-gather.6
  127.7 73.1 all-gather.8
  555.4 57.5 reduce-scatter.11
  617.3 54.0 reduce-scatter.15
  675.8 54.7 reduce-scatter.13
  732.9 21.9 all-reduce.12
  758.9 103.4 reduce-scatter.9
  866.5 104.3 reduce-scatter.7
where the time goes:
time: 992 us; the launch traced here: 980 us
  waiting for transfers between devices  497 us (50%)
  matrix products  213 us (21%)
  local copies, waits for them, and re-layouts  105 us (11%)
  blocking collectives  105 us (11%)
  other arithmetic  25.7 us (3%)
  starting transfers between devices  17.6 us (2%)
  between operations  16.4 us (2%)
    reduce_scatter x1, waiting for transfers between devices, on_device(): lax.psum_scatter(up_part.astype(jnp.bfloat16), 'fsdp', scatter_dimension=...  106 us
    reduce_scatter x1, waiting for transfers between devices, on_device(): lax.psum_scatter(down_part.astype(jnp.bfloat16), 'fsdp', scatter_dimensio...  106 us
    dot_general x13, matrix products, inner_rows(): lax.dot_general(left, right, (((0,), (0,)), ((), ())), preferred_element_...  73.3 us
    unnamed x10, waiting for transfers between devices  59.8 us
    dot_general x4, matrix products, expert_forward(): jnp.dot(active, down_matrix, preferred_element_type=jnp.float32)  56.3 us
    all_gather x1, waiting for transfers between devices, on_device(): lax.all_gather(expert_down, 'fsdp', axis=1, tiled=True)  54.5 us
    unnamed x2, blocking collectives  53.1 us
    reduce_scatter x1, waiting for transfers between devices, on_device(): lax.psum_scatter(totals[0].astype(jnp.bfloat16), 'fsdp', scatter_dimensio...  52.5 us
  transfers between devices with their start and end apart: 13, of which 11 were waited for; matrix products, arithmetic and copies ran while one was open for 7% of the time, Pallas kernels for 0%

commit v1 on v0

v1 whole, which is shorter than its diff:
```python
import functools

import jax
import jax.numpy as jnp
from jax import lax
from jax.experimental import pallas as pl
from jax.experimental.pallas import tpu as pltpu
from jax.sharding import PartitionSpec as P

HEADS = 8
HEAD_DIM = 64
PATCHES = 49
EPS = 1e-06
ROOT_HALF = 0.7071067811865476
DENSITY_SCALE = 0.3989422804014327

BLOCK = 256
GROUP_IMAGES = BLOCK // PATCHES
GROUP_ROWS = GROUP_IMAGES * PATCHES
LANES = 128
NORM_LANE = 64
FF_CHUNK = 512
VMEM_LIMIT = 60 * 1024 * 1024

F32 = jnp.float32
BF16 = jnp.bfloat16


def dot(left, right):
    return lax.dot_general(left, right, (((1,), (0,)), ((), ())), preferred_element_type=F32)


def dot_rows(left, right):
    return lax.dot_general(left, right, (((0,), (0,)), ((), ())), preferred_element_type=F32)


def dot_against(left, right):
    return lax.dot_general(left, right, (((1,), (1,)), ((), ())), preferred_element_type=F32)


def iota(shape, dim):
    return lax.broadcasted_iota(jnp.int32, shape, dim)


def normalize(values):
    center = jnp.mean(values, axis=-1, keepdims=True)
    offset = values - center
    spread = jnp.mean(offset * offset, axis=-1, keepdims=True)
    inverse = lax.rsqrt(spread + EPS)
    return offset * inverse, inverse


def denormalize(upstream, normed, inverse, gain):
    scaled = upstream * gain
    return inverse * (
        scaled
        - jnp.mean(scaled, axis=-1, keepdims=True)
        - normed * jnp.mean(scaled * normed, axis=-1, keepdims=True)
    )


def to_row(column):
    n = column.shape[0]
    parts = []
    for at in range(0, n, LANES):
        eye = iota((LANES, LANES), 0) == iota((LANES, LANES), 1)
        parts.append(jnp.sum(jnp.where(eye, column[at : at + LANES], 0.0), axis=0, keepdims=True))
    return parts[0] if len(parts) == 1 else jnp.concatenate(parts, axis=1)


def rows_of(g):
    return pl.ds(pl.multiple_of(g * BLOCK, BLOCK), BLOCK)


def gates_of(probs, meta):
    lane = iota(probs.shape, 1)
    first = jnp.sum(jnp.where(lane == meta[:, 2:3], probs, 0.0), axis=1, keepdims=True)
    second = jnp.sum(jnp.where(lane == meta[:, 3:4], probs, 0.0), axis=1, keepdims=True)
    return first, second


def forward_kernel(
    experts,
    x_ref, cot_ref, meta_ref, meta_row_ref, params_ref,
    act_one_ref, triple_ref, weights_ref, attended_ref, mid_ref, act_two_ref, probs_ref,
    sent_ref, grad_sent_ref, cot_sent_ref,
    bias_ref, gate_rows_ref,
):
    width = x_ref.shape[1]
    groups = x_ref.shape[0] // BLOCK
    small = params_ref[:, 4 * width :]
    small_rows = jnp.transpose(small.astype(F32))
    image_row = iota((BLOCK, BLOCK), 0) // PATCHES
    image_col = iota((BLOCK, BLOCK), 1) // PATCHES
    bias_ref[...] = jnp.where(image_row == image_col, 0.0, -1e30)

    @pl.loop(0, groups)
    def _(g):
        rows = rows_of(g)
        x = x_ref[rows, :].astype(F32)
        normed, _ = normalize(x)
        act = (normed * small_rows[NORM_LANE : NORM_LANE + 1] + small_rows[NORM_LANE + 1 : NORM_LANE + 2]).astype(BF16)
        act_one_ref[rows, :] = act
        triple_ref[rows, :] = dot(act, params_ref[:, : 3 * width]).astype(BF16)
        low = iota((BLOCK, LANES), 1) < HEAD_DIM
        for pair in range(HEADS // 2):
            at = pair * LANES
            q = triple_ref[rows, at : at + LANES] * HEAD_DIM ** (-0.5)
            k = triple_ref[rows, width + at : width + at + LANES]
            v = triple_ref[rows, 2 * width + at : 2 * width + at + LANES]
            total = None
            for half in range(2):
                mask = low if half == 0 else jnp.logical_not(low)
                scores = dot_against(jnp.where(mask, q, 0.0).astype(BF16), k) + bias_ref[...]
                top = jnp.max(scores, axis=-1, keepdims=True)
                raised = jnp.exp(scores - top)
                probs = raised / jnp.sum(raised, axis=-1, keepdims=True)
                probs = probs.astype(BF16)
                weights_ref[g, 2 * pair + half] = probs
                part = dot(probs, jnp.where(mask, v, 0.0).astype(BF16))
                total = part if total is None else total + part
            attended_ref[rows, at : at + LANES] = total.astype(BF16)
        mid = x + dot(attended_ref[rows, :], params_ref[:, 3 * width : 4 * width])
        mid_ref[rows, :] = mid
        normed, _ = normalize(mid)
        act = (normed * small_rows[NORM_LANE + 2 : NORM_LANE + 3] + small_rows[NORM_LANE + 3 : NORM_LANE + 4]).astype(BF16)
        act_two_ref[rows, :] = act
        logits = jnp.where(iota((BLOCK, LANES), 1) < experts, dot(act, small), -1e30)
        raised = jnp.exp(logits - jnp.max(logits, axis=-1, keepdims=True))
        probs = raised / jnp.sum(raised, axis=-1, keepdims=True)
        probs_ref[rows, :] = probs
        first, second = gates_of(probs, meta_ref[rows, :])
        gate_rows_ref[0:1, rows] = to_row(first)
        gate_rows_ref[1:2, rows] = to_row(second)

    capacity = sent_ref.shape[1]

    @pl.loop(0, experts)
    def _(e):
        slot = iota((capacity, x_ref.shape[0]), 0) + e * capacity
        in_first = slot == meta_row_ref[0:1, :]
        in_second = slot == meta_row_ref[1:2, :]
        picks = jnp.where(jnp.logical_or(in_first, in_second), 1.0, 0.0).astype(BF16)
        gate = jnp.sum(
            jnp.where(in_first, gate_rows_ref[0:1, :], jnp.where(in_second, gate_rows_ref[1:2, :], 0.0)),
            axis=1, keepdims=True,
        )
        sent_ref[e] = dot(picks, act_two_ref[...]).astype(BF16)
        cot_slots = dot(picks, cot_ref[...])
        cot_sent_ref[e] = cot_slots.astype(BF16)
        grad_sent_ref[e] = (gate * cot_slots).astype(BF16)


def expert_kernel(rows_ref, grad_ref, up_ref, down_ref, back_ref, grad_rows_ref, up_part_ref, down_part_ref, back_sum, grad_sum):
    hidden_width = up_ref.shape[2]
    chunks = hidden_width // FF_CHUNK
    back_sum[...] = jnp.zeros_like(back_sum)
    grad_sum[...] = jnp.zeros_like(grad_sum)

    @pl.loop(0, chunks)
    def _(f):
        at = pl.ds(pl.multiple_of(f * FF_CHUNK, FF_CHUNK), FF_CHUNK)
        rows, grads = rows_ref[0], grad_ref[0]
        up, down = up_ref[0, :, at], down_ref[0, at, :]
        hidden = dot(rows, up)
        spread = 0.5 * (1.0 + lax.erf(hidden * ROOT_HALF))
        active = (hidden * spread).astype(BF16)
        slope = spread + hidden * (DENSITY_SCALE * jnp.exp(-0.5 * hidden * hidden))
        back_sum[...] += dot(active, down)
        grad_hidden = (dot_against(grads, down) * slope).astype(BF16)
        grad_sum[...] += dot_against(grad_hidden, up)
        up_part_ref[0, :, at] = dot_rows(rows, grad_hidden).astype(BF16)
        down_part_ref[0, at, :] = dot_rows(active, grads).astype(BF16)

    back_ref[0] = back_sum[...].astype(BF16)
    grad_rows_ref[0] = grad_sum[...].astype(BF16)


def backward_kernel(
    experts,
    x_ref, cot_ref, meta_ref, params_ref, act_one_ref, triple_ref, weights_ref, attended_ref, mid_ref, act_two_ref,
    probs_ref, back_ref, grad_slots_ref, cot_slots_ref,
    out_ref, input_grad_ref, params_grad_ref,
    dot_row_ref, place_ref, gated_ref, branch_ref, grad_triple_ref, logit_grad_ref, sums_ref,
):
    width = x_ref.shape[1]
    groups = x_ref.shape[0] // BLOCK
    places = back_ref.shape[0]
    small = params_ref[:, 4 * width :]
    small_rows = jnp.transpose(small.astype(F32))
    gain_one = small_rows[NORM_LANE : NORM_LANE + 1]
    gain_two = small_rows[NORM_LANE + 2 : NORM_LANE + 3]
    sums_ref[...] = jnp.zeros_like(sums_ref)

    @pl.loop(0, places // LANES)
    def _(c):
        at = pl.ds(pl.multiple_of(c * LANES, LANES), LANES)
        column = jnp.sum(back_ref[at, :].astype(F32) * cot_slots_ref[at, :].astype(F32), axis=1, keepdims=True)
        dot_row_ref[0:1, at] = to_row(column)

    @pl.loop(0, groups)
    def _(g):
        rows = rows_of(g)
        meta = meta_ref[rows, :]
        probs = probs_ref[rows, :]
        gate_first, gate_second = gates_of(probs, meta)
        lane = iota((BLOCK, LANES), 1)
        grad_first = jnp.zeros((BLOCK, LANES), F32)
        grad_second = jnp.zeros((BLOCK, LANES), F32)
        for c in range(places // LANES):
            at = c * LANES
            in_first = lane == meta[:, 0:1] - at
            in_second = lane == meta[:, 1:2] - at
            place_ref[:, at : at + LANES] = jnp.where(jnp.logical_or(in_first, in_second), 1.0, 0.0).astype(BF16)
            gated_ref[:, at : at + LANES] = jnp.where(in_first, gate_first, jnp.where(in_second, gate_second, 0.0)).astype(BF16)
            dots = dot_row_ref[0:1, at : at + LANES]
            grad_first += jnp.where(in_first, dots, 0.0)
            grad_second += jnp.where(in_second, dots, 0.0)
        grad_first = jnp.sum(grad_first, axis=1, keepdims=True)
        grad_second = jnp.sum(grad_second, axis=1, keepdims=True)
        mid = mid_ref[rows, :]
        out_ref[rows, :] = (mid + dot(gated_ref[...], back_ref[...])).astype(BF16)
        grad_probs = jnp.where(lane == meta[:, 2:3], grad_first, 0.0) + jnp.where(lane == meta[:, 3:4], grad_second, 0.0)
        grad_logits = (probs * (grad_probs - jnp.sum(grad_probs * probs, axis=-1, keepdims=True))).astype(BF16)
        logit_grad_ref[rows, :] = grad_logits
        grad_act = dot(place_ref[...], grad_slots_ref[...]) + dot_against(grad_logits, small)
        normed, inverse = normalize(mid)
        sums_ref[NORM_LANE + 2 : NORM_LANE + 3, :] += jnp.sum(grad_act * normed, axis=0, keepdims=True)
        sums_ref[NORM_LANE + 3 : NORM_LANE + 4, :] += jnp.sum(grad_act, axis=0, keepdims=True)
        grad_mid = cot_ref[rows, :].astype(F32) + denormalize(grad_act, normed, inverse, gain_two)
        input_grad_ref[rows, :] = grad_mid
        branch = grad_mid.astype(BF16)
        branch_ref[rows, :] = branch
        grad_attended = dot_against(branch, params_ref[:, 3 * width : 4 * width]).astype(BF16)
        low = lane < HEAD_DIM
        for pair in range(HEADS // 2):
            at = pair * LANES
            q = triple_ref[rows, at : at + LANES] * HEAD_DIM ** (-0.5)
            k = triple_ref[rows, width + at : width + at + LANES]
            v = triple_ref[rows, 2 * width + at : 2 * width + at + LANES]
            upstream = grad_attended[:, at : at + LANES]
            grad_q = grad_k = grad_v = jnp.zeros((BLOCK, LANES), F32)
            for half in range(2):
                mask = low if half == 0 else jnp.logical_not(low)
                upstream_half = jnp.where(mask, upstream, 0.0).astype(BF16)
                weights = weights_ref[g, 2 * pair + half]
                kept = weights.astype(F32)
                grad_weights = dot_against(upstream_half, v)
                inner = jnp.sum(grad_weights * kept, axis=-1, keepdims=True)
                grad_scores = (kept * (grad_weights - inner)).astype(BF16)
                grad_q += dot(grad_scores, jnp.where(mask, k, 0.0).astype(BF16))
                grad_k += dot_rows(grad_scores, jnp.where(mask, q, 0.0).astype(BF16))
                grad_v += dot_rows(weights, upstream_half)
            grad_triple_ref[rows, at : at + LANES] = (grad_q * HEAD_DIM ** (-0.5)).astype(BF16)
            grad_triple_ref[rows, width + at : width + at + LANES] = grad_k.astype(BF16)
            grad_triple_ref[rows, 2 * width + at : 2 * width + at + LANES] = grad_v.astype(BF16)
        grad_act = dot_against(grad_triple_ref[rows, :], params_ref[:, : 3 * width])
        normed, inverse = normalize(x_ref[rows, :].astype(F32))
        sums_ref[NORM_LANE : NORM_LANE + 1, :] += jnp.sum(grad_act * normed, axis=0, keepdims=True)
        sums_ref[NORM_LANE + 1 : NORM_LANE + 2, :] += jnp.sum(grad_act, axis=0, keepdims=True)
        input_grad_ref[rows, :] += denormalize(grad_act, normed, inverse, gain_one)

    params_grad_ref[:, : 3 * width] = dot_rows(act_one_ref[...], grad_triple_ref[...]).astype(BF16)
    params_grad_ref[:, 3 * width : 4 * width] = dot_rows(attended_ref[...], branch_ref[...]).astype(BF16)
    router_part = dot_rows(act_two_ref[...], logit_grad_ref[...])
    norm_part = jnp.transpose(sums_ref[...])
    params_grad_ref[:, 4 * width :] = (router_part + norm_part).astype(BF16)


def on_device(
    inputs, cotangent, routes, slots, qkv_weight, out_weight, router_weight,
    norm1_gain, norm1_shift, norm2_gain, norm2_shift, expert_up, expert_down,
):
    rows_dev, width = inputs.shape
    groups = rows_dev // GROUP_ROWS
    rows_pad = groups * BLOCK
    fsdp = lax.axis_size("fsdp")
    peers = lax.axis_size("expert")
    held = expert_up.shape[0]
    experts = held * peers
    capacity = (42 * rows_dev + 20 * experts - 1) // (20 * experts)
    capacity = -(-capacity // 16) * 16
    places = -(-experts * capacity // LANES) * LANES

    def pad_rows(array, value=0):
        array = array.reshape(groups, GROUP_ROWS, array.shape[1])
        array = jnp.pad(array, ((0, 0), (0, BLOCK - GROUP_ROWS), (0, 0)), constant_values=value)
        return array.reshape(rows_pad, array.shape[2])

    def cut_rows(array):
        return array.reshape(groups, BLOCK, width)[:, :GROUP_ROWS].reshape(rows_dev, width)

    norms = jnp.stack([norm1_gain, norm1_shift, norm2_gain, norm2_shift], axis=1)
    shard = jnp.concatenate(
        [
            qkv_weight,
            out_weight,
            jnp.pad(router_weight, ((0, 0), (0, NORM_LANE - experts))),
            jnp.pad(norms, ((0, 0), (0, LANES - NORM_LANE - 4))),
        ],
        axis=1,
    )
    params = lax.all_gather(shard, "fsdp", axis=0, tiled=True)
    up_full = lax.all_gather(expert_up, "fsdp", axis=1, tiled=True)
    down_full = lax.all_gather(expert_down, "fsdp", axis=1, tiled=True)

    x = pad_rows(inputs)
    cot = pad_rows(cotangent)
    targets = jnp.where(slots >= 0, routes * capacity + slots, -1)
    meta = pad_rows(jnp.concatenate([targets, routes], axis=1), -1)
    meta_row = jnp.transpose(meta)

    vmem = pl.BlockSpec(memory_space=pltpu.VMEM)
    shape = jax.ShapeDtypeStruct
    params_spec = pltpu.CompilerParams(vmem_limit_bytes=VMEM_LIMIT)
    saved = pl.pallas_call(
        functools.partial(forward_kernel, experts),
        out_shape=(
            shape((rows_pad, width), BF16),
            shape((rows_pad, 3 * width), BF16),
            shape((groups, HEADS, BLOCK, BLOCK), BF16),
            shape((rows_pad, width), BF16),
            shape((rows_pad, width), F32),
            shape((rows_pad, width), BF16),
            shape((rows_pad, LANES), F32),
            shape((experts, capacity, width), BF16),
            shape((experts, capacity, width), BF16),
            shape((experts, capacity, width), BF16),
        ),
        in_specs=[vmem] * 5,
        out_specs=[vmem] * 10,
        scratch_shapes=[pltpu.VMEM((BLOCK, BLOCK), F32), pltpu.VMEM((8, rows_pad), F32)],
        compiler_params=params_spec,
        name="attention_forward",
    )(x, cot, meta, meta_row, params)
    act_one, triple, weights, attended, mid, act_two, probs, sent, grad_sent, cot_slots = saved

    arrived = lax.all_to_all(sent, "expert", split_axis=0, concat_axis=1, tiled=True)
    grad_arrived = lax.all_to_all(grad_sent, "expert", split_axis=0, concat_axis=1, tiled=True)
    expert_rows = peers * capacity
    hidden_width = up_full.shape[2]

    def block(*dims):
        return pl.BlockSpec((1, *dims), lambda e: (e, 0, 0))

    back, grad_rows, up_part, down_part = pl.pallas_call(
        expert_kernel,
        grid=(held,),
        out_shape=(
            shape((held, expert_rows, width), BF16),
            shape((held, expert_rows, width), BF16),
            shape((held, width, hidden_width), BF16),
            shape((held, hidden_width, width), BF16),
        ),
        in_specs=[block(expert_rows, width)] * 2 + [block(width, hidden_width), block(hidden_width, width)],
        out_specs=[block(expert_rows, width)] * 2 + [block(width, hidden_width), block(hidden_width, width)],
        scratch_shapes=[pltpu.VMEM((expert_rows, width), F32)] * 2,
        compiler_params=params_spec,
        name="experts",
    )(arrived, grad_arrived, up_full, down_full)

    returned = lax.all_to_all(back, "expert", split_axis=1, concat_axis=0, tiled=True)
    grad_returned = lax.all_to_all(grad_rows, "expert", split_axis=1, concat_axis=0, tiled=True)
    up_grad = lax.psum_scatter(up_part, "fsdp", scatter_dimension=1, tiled=True).astype(F32)
    down_grad = lax.psum_scatter(down_part, "fsdp", scatter_dimension=1, tiled=True).astype(F32)

    def flat(array):
        array = array.reshape(experts * capacity, width)
        return jnp.pad(array, ((0, places - experts * capacity), (0, 0)))

    out, input_grad, params_grad = pl.pallas_call(
        functools.partial(backward_kernel, experts),
        out_shape=(
            shape((rows_pad, width), BF16),
            shape((rows_pad, width), F32),
            shape((width, 4 * width + LANES), BF16),
        ),
        in_specs=[vmem] * 14,
        out_specs=[vmem] * 3,
        scratch_shapes=[
            pltpu.VMEM((8, places), F32),
            pltpu.VMEM((BLOCK, places), BF16),
            pltpu.VMEM((BLOCK, places), BF16),
            pltpu.VMEM((rows_pad, width), BF16),
            pltpu.VMEM((rows_pad, 3 * width), BF16),
            pltpu.VMEM((rows_pad, LANES), BF16),
            pltpu.VMEM((LANES, width), F32),
        ],
        compiler_params=params_spec,
        name="attention_backward",
    )(
        x, cot, meta, params, act_one, triple, weights, attended, mid, act_two, probs,
        flat(returned), flat(grad_returned), flat(cot_slots),
    )
    share = lax.psum_scatter(params_grad, "fsdp", scatter_dimension=0, tiled=True)
    share = lax.psum(share, "expert").astype(F32)
    norm_share = share[:, 4 * width + NORM_LANE : 4 * width + NORM_LANE + 4]
    return (
        cut_rows(out),
        cut_rows(input_grad),
        share[:, : 3 * width],
        share[:, 3 * width : 4 * width],
        share[:, 4 * width : 4 * width + experts],
        norm_share[:, 0],
        norm_share[:, 1],
        norm_share[:, 2],
        norm_share[:, 3],
        up_grad,
        down_grad,
    )


def solution(mesh):
    tokens = P(("expert", "fsdp"), None)
    rows, vector, expert = P("fsdp", None), P("fsdp"), P("expert", "fsdp", None)
    return jax.shard_map(
        on_device,
        mesh=mesh,
        in_specs=(tokens,) * 4 + (rows,) * 3 + (vector,) * 4 + (expert,) * 2,
        out_specs=(tokens,) * 2 + (rows,) * 3 + (vector,) * 4 + (expert,) * 2,
        check_vma=False,
    )
```

time: 992 us -> 671 us (0.68)
  matrix products: 213 us -> 0 us
  Pallas kernels: 0 us -> 111 us
  blocking collectives: 105 us -> 32.8 us
  local copies, waits for them, and re-layouts: 105 us -> 36.1 us
  waiting for transfers between devices: 497 us -> 453 us
  other arithmetic: 25.7 us -> 7.41 us
    dot_general x43 -> x0, matrix products: 213 us -> none  [the longest x13 73.3 us: inner_rows(): lax.dot_general(left, right, (((0,), (0,)), ((), ())), preferred_element_...]
    pallas_call x0 -> x3, Pallas kernels: none -> 111 us  [the longest x1 42.9 us: on_device(): pl.pallas_call(expert_kernel, grid=(held,), out_shape=(shape((held, exper...]
    unnamed x10 -> x7, waiting for transfers between devices: 59.8 us -> 2.63 us
    unnamed x2 -> x0, blocking collectives: 53.1 us -> none
    all_gather x2 -> x0, blocking collectives: 42.9 us -> none  [the longest x1 25.4 us: on_device(): lax.all_gather(out_weight, 'fsdp', axis=0, tiled=True)]
    all_gather x3, waiting for transfers between devices: 54.5 us -> 93.2 us  [the longest x1 59 us: on_device(): down_full = lax.all_gather(expert_down, 'fsdp', axis=1, tiled=True)]
    all_to_all x0 -> x1, blocking collectives: none -> 32.8 us  [on_device(): lax.all_to_all(sent, 'expert', split_axis=0, concat_axis=1, tiled=True)]
    while x58 -> x0, local copies, waits for them, and re-layouts: 26.7 us -> none
  transfers between devices with their start and end apart: 13 -> 10, of which waited for: 11 -> 9; matrix products, arithmetic and copies ran while one was open for 7% -> 4% of each run, Pallas kernels for 0% -> 4%
where the time goes in v1:
time: 671 us; the launch traced here: 667 us
  waiting for transfers between devices  453 us (68%)
  Pallas kernels  111 us (17%)
  local copies, waits for them, and re-layouts  36.1 us (5%)
  blocking collectives  32.8 us (5%)
  between operations  14.3 us (2%)
  starting transfers between devices  12.9 us (2%)
  other arithmetic  7.41 us (1%)
    reduce_scatter x1, waiting for transfers between devices, on_device(): lax.psum_scatter(up_part, 'fsdp', scatter_dimension=1, tiled=True)  107 us
    reduce_scatter x1, waiting for transfers between devices, on_device(): lax.psum_scatter(down_part, 'fsdp', scatter_dimension=1, tiled=True)  102 us
    reduce_scatter x1, waiting for transfers between devices, on_device(): lax.psum_scatter(params_grad, 'fsdp', scatter_dimension=0, tiled=True)  60.8 us
    all_gather x1, waiting for transfers between devices, on_device(): down_full = lax.all_gather(expert_down, 'fsdp', axis=1, tiled=True)  59 us
    pallas_call x1, Pallas kernels, on_device(): pl.pallas_call(expert_kernel, grid=(held,), out_shape=(shape((held, exper...  42.9 us
    pallas_call x1, Pallas kernels, on_device(): pl.pallas_call(functools.partial(backward_kernel, experts), out_shape=(sh...  40.1 us
    all_gather x1, waiting for transfers between devices, on_device(): params = lax.all_gather(shard, 'fsdp', axis=0, tiled=True)  34.2 us
    all_to_all x1, blocking collectives, on_device(): lax.all_to_all(sent, 'expert', split_axis=0, concat_axis=1, tiled=True)  32.8 us
  transfers between devices with their start and end apart: 10, of which 9 were waited for; matrix products, arithmetic and copies ran while one was open for 4% of the time, Pallas kernels for 4%

profile of v1, /device:TPU:28, one launch (start us, length us, event | category | flops | bytes accessed | tf_op | source)
XLA Modules:
  0.0 667.0 jit_solution(4560464184462068701)
XLA Ops:
  8.9 1.6 concatenate.7
  15.0 1.1 pad.19
  16.3 1.1 pad.20
  17.4 34.2 %all-gather.4.cloned.1.call-done.params_ref = bf16[512,2176]{1,0:T(8,128)(2,1)} async-done(((bf16[32,2176]{1,0:T(8,128)(2,1)}), bf16[512,2176]{1,0:T(8,128)(2,1)}) %all-gather.4.cloned.1.call-update) | async-done | bytes 2228240 | tf_op jit(solution)/shard_map/all_gather | solution.py:303
  51.6 27.5 %attention_forward.1 = (bf16[1024,512]{1,0:T(8,128)(2,1)}, bf16[1024,1536]{1,0:T(8,128)(2,1)}, bf16[4,8,256,256]{3,2,1,0:T(8,128)(2,1)}, bf16[1024,512]{1,0:T(8,...) custom-call(bf16[1024,512]{1,0:T(8,128)(2,1)} %bitcast.30, ...), custom_call_target="tpu_custom_call" | custom-call | tf_op jit(solution)/shard_map/attention_forward/pallas_call | solution.py:316
  79.1 32.8 %all_to_all.66 = bf16[8,272,512]{2,1,0:T(8,128)(2,1)} all-to-all(bf16[8,272,512]{2,1,0:T(8,128)(2,1)} %get-tuple-element.35), channel_id=1, replica_groups=mesh['expert'=2,'fsdp'=16] {'expert'}, dimensions={0} | all-to-all | bytes 4456448 | tf_op jit(solution)/shard_map/all_to_all | solution.py:338
  112.0 3.8 all-to-all-start.1
  115.7 3.2 copy.52
  119.0 22.9 %all-to-all-done.1 = bf16[8,272,512]{2,1,0:T(8,128)(2,1)S(1)} async-done(((bf16[8,272,512]{2,1,0:T(8,128)(2,1)}), bf16[8,272,512]{2,1,0:T(8,128)(2,1)S(1)}, u32[]{:S(2)}, u32[]{:S(2)}) %all-to-all-start.1) | async-done | bytes 2228256 | tf_op jit(solution)/shard_map/all_to_all | solution.py:339
  141.9 1.6 copy.53
  143.5 59.0 %all-gather.8.cloned.1.call-done.down_ref = bf16[4,2048,512]{2,1,0:T(8,128)(2,1)} async-done(((bf16[4,128,512]{2,1,0:T(8,128)(2,1)}), bf16[4,2048,512]{2,1,0:T(8,128)(2,1)}) %all-gather.8.cloned.1.call-update) | async-done | bytes 8388624 | tf_op jit(solution)/shard_map/all_gather | solution.py:305
  202.4 42.9 %experts.1 = (bf16[4,544,512]{2,1,0:T(8,128)(2,1)}, bf16[4,544,512]{2,1,0:T(8,128)(2,1)}, bf16[4,512,2048]{2,1,0:T(8,128)(2,1)}, bf16[4,2048,512]{2,1,0:T(8,128)(2,1)}) custom-call(bf16[4,544,512]{2,1,0:T(8,128)(2,1)} %bitcast.39, bf16[4,544,512]{2,1,0:T(8,128)(2,1)} %bitcast.40, bf16[4,512,2048]{2,1,0:T(8,128)(2,1)} %all-gather.6.cloned.1.call-done.up_ref, ...), custom_call_target="tpu_custom_call" | custom-call | tf_op jit(solution)/shard_map/experts/pallas_call | solution.py:346
  245.4 4.7 copy.54
  250.1 3.8 all-to-all-start.2
  253.9 4.8 copy.56
  258.7 22.2 %all-to-all-done.2 = bf16[4,544,512]{2,0,1:T(4,128)(2,1)S(1)} async-done(((bf16[4,544,512]{2,0,1:T(4,128)(2,1)}), bf16[4,544,512]{2,0,1:T(4,128)(2,1)S(1)}, u32[]{:S(2)}, u32[]{:S(2)}) %all-to-all-start.2) | async-done | bytes 2228256 | tf_op jit(solution)/shard_map/all_to_all | solution.py:362
  280.8 4.9 all-to-all-start.3
  286.0 1.8 copy.55
  287.8 24.2 %all-to-all-done.3 = bf16[4,544,512]{2,0,1:T(4,128)(2,1)} async-done(((bf16[4,544,512]{2,0,1:T(4,128)(2,1)}), bf16[4,544,512]{2,0,1:T(4,128)(2,1)}, u32[]{:S(2)}, u32[]{:S(2)}) %all-to-all-start.3) | async-done | bytes 2228256 | tf_op jit(solution)/shard_map/all_to_all | solution.py:363
  312.0 3.4 copy.57
  315.4 40.1 %attention_backward.1 = (bf16[1024,512]{1,0:T(8,128)(2,1)}, f32[1024,512]{1,0:T(8,128)}, bf16[512,2176]{1,0:T(8,128)(2,1)}) custom-call(bf16[1024,512]{1,0:T(8,128)(2,1)} %bitcast.31, bf16[1024,512]{1,0:T(8,128)(2,1)} %bitcast.33, s32[1024,4]{1,0:T(8,128)} %bitcast.43, bf16[512,2176]{1,0:T(8,128)(2,1)} %all-gather.4.cloned.1.call-done.params_ref, ...), custom_call_target="tpu_custom_call" | custom-call | tf_op jit(solution)/shard_map/attention_backward/pallas_call | solution.py:371
  355.6 60.8 %reduce-scatter.4.cloned.1.call-done = bf16[32,2176]{1,0:T(8,128)(2,1)} async-done(((bf16[512,2176]{1,0:T(8,128)(2,1)}), bf16[32,2176]{1,0:T(8,128)(2,1)}) %reduce-scatter.4.cloned.1.call-update) | async-done | bytes 139280 | tf_op jit(solution)/shard_map/reduce_scatter | solution.py:395
  418.3 1.2 reshape.73
  419.5 1.7 slice.42
  421.3 1.5 reshape.75
  422.8 18.3 %all-reduce.7.cloned.1.call-done = bf16[32,2176]{1,0:T(8,128)(2,1)} async-done(((bf16[32,2176]{1,0:T(8,128)(2,1)}), bf16[32,2176]{1,0:T(8,128)(2,1)}) %all-reduce.7.cloned.1.call-update) | async-done | bytes 139280 | tf_op jit(solution)/shard_map/psum | solution.py:396
  442.4 1.4 slice.44
  443.8 1.6 slice.43
  447.1 102.0 %reduce-scatter.8.cloned.1.call-done = bf16[4,128,512]{2,1,0:T(8,128)(2,1)} async-done(((bf16[4,2048,512]{2,1,0:T(8,128)(2,1)}), bf16[4,128,512]{2,1,0:T(8,128)(2,1)}) %reduce-scatter.8.cloned.1.call-update) | async-done | bytes 524304 | tf_op jit(solution)/shard_map/reduce_scatter | solution.py:365
  549.1 2.1 convert_element_type.18
  551.2 106.8 %reduce-scatter.6.cloned.1.call-done = bf16[4,32,2048]{2,1,0:T(8,128)(2,1)} async-done(((bf16[4,512,2048]{2,1,0:T(8,128)(2,1)}), bf16[4,32,2048]{2,1,0:T(8,128)(2,1)}) %reduce-scatter.6.cloned.1.call-update) | async-done | bytes 524304 | tf_op jit(solution)/shard_map/reduce_scatter | solution.py:364
  658.1 2.1 convert_element_type.17
  (41 shorter events, 11.5 us)
Async XLA Ops:
  7.2 7.5 %copy-start.1 = (bf16[980,512]{1,0:T(8,128)(2,1)S(1)}, bf16[980,512]{1,0:T(8,128)(2,1)}, u32[]{:S(2)}) copy-start(bf16[980,512]{1,0:T(8,128)(2,1)} %param.13) | copy-start | bytes 3010564
  7.2 44.4 %all-gather.4.cloned.1.call-start = ((), (), s32[]{:S(2)}) async-start(), calls=%async_computation.7 | async-start | bytes 2367488 | tf_op jit(solution)/shard_map/all_gather | solution.py:303
  10.6 132.9 %all-gather.6.cloned.1.call-start = ((), (), s32[]{:S(2)}) async-start(), calls=%async_computation.8 | async-start | bytes 8912896 | tf_op jit(solution)/shard_map/all_gather | solution.py:304
  11.3 191.1 %all-gather.8.cloned.1.call-start = ((), (), s32[]{:S(2)}) async-start(), calls=%async_computation.9 | async-start | bytes 8912896 | tf_op jit(solution)/shard_map/all_gather | solution.py:305
  13.9 2.2 copy-start
  13.9 2.2 copy-start.2
  112.0 29.9 %all-to-all-start.1 = ((bf16[8,272,512]{2,1,0:T(8,128)(2,1)}), bf16[8,272,512]{2,1,0:T(8,128)(2,1)S(1)}, u32[]{:S(2)}, u32[]{:S(2)}) async-start(bf16[8,272,512]{2,1,0:T(8,128)(2,1)} %get-tuple-element.36), calls=%async_computation.1 | async-start | bytes 4456448 | tf_op jit(solution)/shard_map/all_to_all | solution.py:339
  250.1 30.7 %all-to-all-start.2 = ((bf16[4,544,512]{2,0,1:T(4,128)(2,1)}), bf16[4,544,512]{2,0,1:T(4,128)(2,1)S(1)}, u32[]{:S(2)}, u32[]{:S(2)}) async-start(bf16[4,544,512]{2,0,1:T(4,128)(2,1)} %copy.54), calls=%async_computation.2 | async-start | bytes 4456448 | tf_op jit(solution)/shard_map/all_to_all | solution.py:362
  280.8 31.1 %all-to-all-start.3 = ((bf16[4,544,512]{2,0,1:T(4,128)(2,1)}), bf16[4,544,512]{2,0,1:T(4,128)(2,1)}, u32[]{:S(2)}, u32[]{:S(2)}) async-start(bf16[4,544,512]{2,0,1:T(4,128)(2,1)} %copy.56), calls=%async_computation.3 | async-start | bytes 4456448 | tf_op jit(solution)/shard_map/all_to_all | solution.py:363
  285.7 130.6 %reduce-scatter.4.cloned.1.call-start = ((), (), s32[]{:S(2)}) async-start(), calls=%async_computation.10 | async-start | bytes 2367488 | tf_op jit(solution)/shard_map/reduce_scatter | solution.py:395
  355.5 85.5 %all-reduce.7.cloned.1.call-start = ((), (), s32[]{:S(2)}) async-start(), calls=%async_computation.11 | async-start | bytes 278528 | tf_op jit(solution)/shard_map/psum | solution.py:396
  416.4 132.7 %reduce-scatter.8.cloned.1.call-start = ((), (), s32[]{:S(2)}) async-start(), calls=%async_computation.13 | async-start | bytes 8912896 | tf_op jit(solution)/shard_map/reduce_scatter | solution.py:365
  416.9 241.1 %reduce-scatter.6.cloned.1.call-start = ((), (), s32[]{:S(2)}) async-start(), calls=%async_computation.12 | async-start | bytes 8912896 | tf_op jit(solution)/shard_map/reduce_scatter | solution.py:364
  417.0 1.2 copy-start.3
Sparse Core Ops, SparseCore 0:
  10.9 40.6 all-gather.3
  53.8 73.2 all-gather.5
  129.2 73.1 all-gather.7
  355.7 60.6 reduce-scatter.3
  418.5 22.4 all-reduce.6
  445.5 103.5 reduce-scatter.7
  553.7 104.3 reduce-scatter.5

commit v2 on v1

--- a/solution.py
+++ b/solution.py
@@ -22,6 +22,7 @@
 FF_CHUNK = 512
 VMEM_LIMIT = 60 * 1024 * 1024
 
+MESH = pl.DeviceIdType.MESH
 F32 = jnp.float32
 BF16 = jnp.bfloat16
 
@@ -79,20 +80,214 @@
     return first, second
 
 
+class Place:
+    def __init__(self, fsdp):
+        self.count = fsdp
+        self.A, self.B = 4, fsdp // 8
+        self.x = lax.axis_index("expert")
+        self.me = lax.axis_index("fsdp")
+        self.c = lax.rem(self.me, 2)
+        line = lax.div(self.me, 2)
+        self.b = lax.rem(line, self.B)
+        self.a = lax.div(line, self.B)
+
+    def index(self, a, b, c):
+        return (a * self.B + b) * 2 + c
+
+    def other_b(self, j):
+        return lax.rem(self.b + 1 + j, self.B)
+
+    def at(self, a, b, c):
+        return (self.x, self.index(a, b, c))
+
+
+def greet(place, peers, line_only):
+    barrier = pltpu.get_barrier_semaphore()
+
+    def signal(device):
+        pl.semaphore_signal(barrier, inc=1, device_id=device, device_id_type=MESH)
+
+    if line_only:
+        pl.when(place.a > 0)(lambda: signal(place.at(place.a - 1, place.b, place.c)))
+        pl.when(place.a < place.A - 1)(lambda: signal(place.at(place.a + 1, place.b, place.c)))
+        line = jnp.where(place.a > 0, 1, 0) + jnp.where(place.a < place.A - 1, 1, 0)
+    else:
+        for k in range(1, place.A):
+            signal(place.at(lax.rem(place.a + k, place.A), place.b, place.c))
+        line = place.A - 1
+    for j in range(place.B - 1):
+        signal(place.at(place.a, place.other_b(j), place.c))
+    signal(place.at(place.a, place.b, 1 - place.c))
+    for k in range(1, peers):
+        signal((lax.rem(place.x + k, peers), place.me))
+    pl.semaphore_wait(barrier, line + place.B - 1 + 1 + peers - 1)
+
+
+class Gather:
+    RIGHT, LEFT, CORE, ACROSS = 0, 1, 2, 3
+
+    def __init__(self, place, own, full, block, send_sem, recv_sem, local_sem):
+        self.place, self.own, self.full, self.block = place, own, full, block
+        self.send_sem, self.recv_sem, self.local_sem = send_sem, recv_sem, local_sem
+
+    def copy(self, shard, route, source, a, b, c):
+        return pltpu.make_async_remote_copy(
+            src_ref=source, dst_ref=self.block(self.full, shard),
+            send_sem=self.send_sem.at[shard, route], recv_sem=self.recv_sem.at[shard],
+            device_id=self.place.at(a, b, c), device_id_type=MESH,
+        )
+
+    def onward(self, shard, source, right, left, across, act):
+        p = self.place
+        if right is not None:
+            pl.when(right)(lambda: act(self.copy(shard, self.RIGHT, source, p.a + 1, p.b, p.c)))
+        if left is not None:
+            pl.when(left)(lambda: act(self.copy(shard, self.LEFT, source, p.a - 1, p.b, p.c)))
+        if across:
+            for j in range(p.B - 1):
+                act(self.copy(shard, self.ACROSS + j, source, p.a, p.other_b(j), p.c))
+        act(self.copy(shard, self.CORE, source, p.a, p.b, 1 - p.c))
+
+    def local(self):
+        return pltpu.make_async_copy(self.own, self.block(self.full, self.place.me), self.local_sem)
+
+    def start(self):
+        p = self.place
+        self.local().start()
+        self.onward(p.me, self.own, p.a < p.A - 1, p.a > 0, True, lambda copy: copy.start())
+
+    def arrived(self, shard):
+        p = self.place
+        self.copy(shard, self.CORE, self.block(self.full, shard), p.a, p.b, 1 - p.c).wait_recv()
+
+    def line_step(self, k):
+        p = self.place
+
+        def from_left():
+            shard = p.index(p.a - k, p.b, p.c)
+            self.arrived(shard)
+            self.onward(shard, self.block(self.full, shard), p.a < p.A - 1, None, True, lambda copy: copy.start())
+
+        def from_right():
+            shard = p.index(p.a + k, p.b, p.c)
+            self.arrived(shard)
+            self.onward(shard, self.block(self.full, shard), None, p.a > 0, True, lambda copy: copy.start())
+
+        pl.when(p.a - k >= 0)(from_left)
+        pl.when(p.a + k < p.A)(from_right)
+
+    def across_step(self, k):
+        p = self.place
+
+        def row(a):
+            for j in range(p.B - 1):
+                shard = p.index(a, p.other_b(j), p.c)
+                self.arrived(shard)
+                self.onward(shard, self.block(self.full, shard), None, None, False, lambda copy: copy.start())
+
+        if k == 0:
+            row(p.a)
+        else:
+            pl.when(p.a - k >= 0)(lambda: row(p.a - k))
+            pl.when(p.a + k < p.A)(lambda: row(p.a + k))
+
+    def finish_recv(self):
+        p = self.place
+        self.local().wait()
+        for a in range(p.A):
+            for b in range(p.B):
+                self.arrived(p.index(a, b, 1 - p.c))
+
+    def finish_send(self):
+        p = self.place
+        wait = lambda copy: copy.wait_send()
+        self.onward(p.me, self.own, p.a < p.A - 1, p.a > 0, True, wait)
+        for k in range(1, p.A):
+
+            def from_left(k=k):
+                shard = p.index(p.a - k, p.b, p.c)
+                self.onward(shard, self.block(self.full, shard), p.a < p.A - 1, None, True, wait)
+
+            def from_right(k=k):
+                shard = p.index(p.a + k, p.b, p.c)
+                self.onward(shard, self.block(self.full, shard), None, p.a > 0, True, wait)
+
+            pl.when(p.a - k >= 0)(from_left)
+            pl.when(p.a + k < p.A)(from_right)
+        for a in range(p.A):
+            for j in range(p.B - 1):
+                shard = p.index(a, p.other_b(j), p.c)
+                self.onward(shard, self.block(self.full, shard), None, None, False, wait)
+
+
 def forward_kernel(
-    experts,
-    x_ref, cot_ref, meta_ref, meta_row_ref, params_ref,
-    act_one_ref, triple_ref, weights_ref, attended_ref, mid_ref, act_two_ref, probs_ref,
-    sent_ref, grad_sent_ref, cot_sent_ref,
-    bias_ref, gate_rows_ref,
+    experts, fsdp, peers,
+    x_ref, cot_ref, meta_ref, meta_row_ref, shard_ref, up_ref, down_ref,
+    act_one_out, triple_out, weights_out, attended_out, mid_out, act_two_out, probs_out,
+    arrived_out, grad_arrived_out, cot_sent_out, params_out, up_full, down_full,
+    params_ref, act_one_ref, triple_ref, weights_ref, attended_ref, mid_ref, act_two_ref, probs_ref,
+    sent_ref, grad_sent_ref, cot_sent_ref, bias_ref, gate_rows_ref,
+    send_sem, recv_sem, local_sem, save_sem, swap_send, swap_recv, swap_local, tail_sem,
 ):
     width = x_ref.shape[1]
     groups = x_ref.shape[0] // BLOCK
-    small = params_ref[:, 4 * width :]
-    small_rows = jnp.transpose(small.astype(F32))
+    held = experts // peers
+    place = Place(fsdp)
+    greet(place, peers, True)
+
+    def rows_block(ref, shard):
+        size = shard_ref.shape[0]
+        return ref.at[pl.ds(pl.multiple_of(shard * size, size), size), :]
+
+    def middle_block(size):
+        return lambda ref, shard: ref.at[:, pl.ds(pl.multiple_of(shard * size, size), size), :]
+
+    gathers = [
+        Gather(place, own, full, block, send_sem.at[i], recv_sem.at[i], local_sem.at[i])
+        for i, (own, full, block) in enumerate(
+            (
+                (shard_ref, params_ref, rows_block),
+                (up_ref, up_full, middle_block(up_ref.shape[1])),
+                (down_ref, down_full, middle_block(down_ref.shape[1])),
+            )
+        )
+    ]
+    params, up, down = gathers
+    params.start()
     image_row = iota((BLOCK, BLOCK), 0) // PATCHES
     image_col = iota((BLOCK, BLOCK), 1) // PATCHES
     bias_ref[...] = jnp.where(image_row == image_col, 0.0, -1e30)
+    for k in range(1, place.A):
+        params.line_step(k)
+        params.across_step(k - 1)
+    up.start()
+    down.start()
+    params.across_step(place.A - 1)
+    params.finish_recv()
+    params_copy = pltpu.make_async_copy(params_ref, params_out, tail_sem.at[0])
+    params_copy.start()
+
+    events = []
+    for k in range(1, place.A):
+        for gather in (up, down):
+            events.append(functools.partial(gather.line_step, k))
+            events.append(functools.partial(gather.across_step, k - 1))
+    for gather in (up, down):
+        events.append(functools.partial(gather.across_step, place.A - 1))
+
+    small = params_ref[:, 4 * width :]
+    small_rows = jnp.transpose(small.astype(F32))
+
+    def saves(g):
+        rows = rows_of(g)
+        pairs = (
+            (act_one_ref, act_one_out), (triple_ref, triple_out), (weights_ref, weights_out), (attended_ref, attended_out),
+            (mid_ref, mid_out), (act_two_ref, act_two_out), (probs_ref, probs_out),
+        )
+        return [
+            pltpu.make_async_copy(here.at[rows, :], there.at[rows, :], save_sem.at[i, g])
+            for i, (here, there) in enumerate(pairs)
+        ]
 
     @pl.loop(0, groups)
     def _(g):
@@ -116,7 +311,8 @@
                 raised = jnp.exp(scores - top)
                 probs = raised / jnp.sum(raised, axis=-1, keepdims=True)
                 probs = probs.astype(BF16)
-                weights_ref[g, 2 * pair + half] = probs
+                head = (2 * pair + half) * BLOCK
+                weights_ref[rows, head : head + BLOCK] = probs
                 part = dot(probs, jnp.where(mask, v, 0.0).astype(BF16))
                 total = part if total is None else total + part
             attended_ref[rows, at : at + LANES] = total.astype(BF16)
@@ -132,11 +328,30 @@
         first, second = gates_of(probs, meta_ref[rows, :])
         gate_rows_ref[0:1, rows] = to_row(first)
         gate_rows_ref[1:2, rows] = to_row(second)
+        for copy in saves(g):
+            copy.start()
+        for i in range(2):
+            pl.when(g == 2 * i + 1)(events[2 * i])
+            pl.when(g == 2 * i + 1)(events[2 * i + 1])
 
     capacity = sent_ref.shape[1]
 
+    def swaps(e):
+        owner, slot = lax.div(e, held), lax.rem(e, held)
+        out = []
+        for i, (here, there) in enumerate(((sent_ref, arrived_out), (grad_sent_ref, grad_arrived_out))):
+            far = pltpu.make_async_remote_copy(
+                src_ref=here.at[e], dst_ref=there.at[slot, place.x],
+                send_sem=swap_send.at[i, e], recv_sem=swap_recv.at[i, slot, place.x],
+                device_id=(owner, place.me), device_id_type=MESH,
+            )
+            near = pltpu.make_async_copy(here.at[e], there.at[slot, place.x], swap_local.at[i, slot])
+            out.append((far, near))
+        return owner != place.x, out
+
     @pl.loop(0, experts)
-    def _(e):
+    def _(i):
+        e = lax.rem((place.x + 1) * held + i, experts)
         slot = iota((capacity, x_ref.shape[0]), 0) + e * capacity
         in_first = slot == meta_row_ref[0:1, :]
         in_second = slot == meta_row_ref[1:2, :]
@@ -149,6 +364,44 @@
         cot_slots = dot(picks, cot_ref[...])
         cot_sent_ref[e] = cot_slots.astype(BF16)
         grad_sent_ref[e] = (gate * cot_slots).astype(BF16)
+        away, copies = swaps(e)
+        for far, near in copies:
+            pl.when(away)(far.start)
+            pl.when(jnp.logical_not(away))(near.start)
+
+    cot_copy = pltpu.make_async_copy(cot_sent_ref, cot_sent_out, tail_sem.at[1])
+    cot_copy.start()
+    for event in events[4:]:
+        event()
+    for gather in (up, down):
+        gather.finish_recv()
+
+    @pl.loop(0, groups)
+    def _(g):
+        for copy in saves(g):
+            copy.wait()
+
+    params_copy.wait()
+    cot_copy.wait()
+
+    @pl.loop(0, experts)
+    def _(e):
+        away, copies = swaps(e)
+        for far, near in copies:
+            pl.when(away)(far.wait_send)
+            pl.when(jnp.logical_not(away))(near.wait)
+
+    for i, there in enumerate((arrived_out, grad_arrived_out)):
+        for slot in range(held):
+            for k in range(1, peers):
+                other = lax.rem(place.x + k, peers)
+                pltpu.make_async_remote_copy(
+                    src_ref=there.at[slot, other], dst_ref=there.at[slot, other],
+                    send_sem=swap_send.at[i, 0], recv_sem=swap_recv.at[i, slot, other],
+                    device_id=(other, place.me), device_id_type=MESH,
+                ).wait_recv()
+    for gather in gathers:
+        gather.finish_send()
 
 
 def expert_kernel(rows_ref, grad_ref, up_ref, down_ref, back_ref, grad_rows_ref, up_part_ref, down_part_ref, back_sum, grad_sum):
@@ -243,7 +496,8 @@
             for half in range(2):
                 mask = low if half == 0 else jnp.logical_not(low)
                 upstream_half = jnp.where(mask, upstream, 0.0).astype(BF16)
-                weights = weights_ref[g, 2 * pair + half]
+                head = (2 * pair + half) * BLOCK
+                weights = weights_ref[rows, head : head + BLOCK]
                 kept = weights.astype(F32)
                 grad_weights = dot_against(upstream_half, v)
                 inner = jnp.sum(grad_weights * kept, axis=-1, keepdims=True)
@@ -300,10 +554,6 @@
         ],
         axis=1,
     )
-    params = lax.all_gather(shard, "fsdp", axis=0, tiled=True)
-    up_full = lax.all_gather(expert_up, "fsdp", axis=1, tiled=True)
-    down_full = lax.all_gather(expert_down, "fsdp", axis=1, tiled=True)
-
     x = pad_rows(inputs)
     cot = pad_rows(cotangent)
     targets = jnp.where(slots >= 0, routes * capacity + slots, -1)
@@ -311,33 +561,46 @@
     meta_row = jnp.transpose(meta)
 
     vmem = pl.BlockSpec(memory_space=pltpu.VMEM)
+    hbm = pl.BlockSpec(memory_space=pl.ANY)
     shape = jax.ShapeDtypeStruct
     params_spec = pltpu.CompilerParams(vmem_limit_bytes=VMEM_LIMIT)
+    kept = (
+        shape((rows_pad, width), BF16),
+        shape((rows_pad, 3 * width), BF16),
+        shape((rows_pad, HEADS * BLOCK), BF16),
+        shape((rows_pad, width), BF16),
+        shape((rows_pad, width), F32),
+        shape((rows_pad, width), BF16),
+        shape((rows_pad, LANES), F32),
+    )
+    slots_shape = shape((experts, capacity, width), BF16)
+    arrived_shape = shape((held, peers, capacity, width), BF16)
+    packed = (fsdp * shard.shape[0], shard.shape[1])
+    scratch = lambda s: pltpu.VMEM(s.shape, s.dtype)
+    dma = pltpu.SemaphoreType.DMA
     saved = pl.pallas_call(
-        functools.partial(forward_kernel, experts),
+        functools.partial(forward_kernel, experts, fsdp, peers),
         out_shape=(
-            shape((rows_pad, width), BF16),
-            shape((rows_pad, 3 * width), BF16),
-            shape((groups, HEADS, BLOCK, BLOCK), BF16),
-            shape((rows_pad, width), BF16),
-            shape((rows_pad, width), F32),
-            shape((rows_pad, width), BF16),
-            shape((rows_pad, LANES), F32),
-            shape((experts, capacity, width), BF16),
-            shape((experts, capacity, width), BF16),
-            shape((experts, capacity, width), BF16),
+            *kept, arrived_shape, arrived_shape, slots_shape, shape(packed, BF16),
+            shape((held, fsdp * expert_up.shape[1], expert_up.shape[2]), BF16),
+            shape((held, fsdp * expert_down.shape[1], expert_down.shape[2]), BF16),
         ),
-        in_specs=[vmem] * 5,
-        out_specs=[vmem] * 10,
-        scratch_shapes=[pltpu.VMEM((BLOCK, BLOCK), F32), pltpu.VMEM((8, rows_pad), F32)],
-        compiler_params=params_spec,
+        in_specs=[vmem] * 5 + [hbm] * 2,
+        out_specs=[hbm] * 13,
+        scratch_shapes=[
+            pltpu.VMEM(packed, BF16), *map(scratch, kept), *[scratch(slots_shape)] * 3,
+            pltpu.VMEM((BLOCK, BLOCK), F32), pltpu.VMEM((8, rows_pad), F32),
+            dma((3, fsdp, 3 + fsdp // 8 - 1)), dma((3, fsdp)), dma((3,)), dma((len(kept), groups)),
+            dma((2, experts)), dma((2, held, peers)), dma((2, held)), dma((2,)),
+        ],
+        compiler_params=pltpu.CompilerParams(vmem_limit_bytes=VMEM_LIMIT, collective_id=0, has_side_effects=True),
         name="attention_forward",
-    )(x, cot, meta, meta_row, params)
-    act_one, triple, weights, attended, mid, act_two, probs, sent, grad_sent, cot_slots = saved
-
-    arrived = lax.all_to_all(sent, "expert", split_axis=0, concat_axis=1, tiled=True)
-    grad_arrived = lax.all_to_all(grad_sent, "expert", split_axis=0, concat_axis=1, tiled=True)
+    )(x, cot, meta, meta_row, shard, expert_up, expert_down)
+    act_one, triple, weights, attended, mid, act_two, probs, arrived, grad_arrived, cot_slots, params, up_full, down_full = saved
+
     expert_rows = peers * capacity
+    arrived = arrived.reshape(held, expert_rows, width)
+    grad_arrived = grad_arrived.reshape(held, expert_rows, width)
     hidden_width = up_full.shape[2]
 
     def block(*dims):

time: 671 us -> 598 us (0.89)
  waiting for transfers between devices: 453 us -> 336 us
  Pallas kernels: 111 us -> 196 us
  blocking collectives: 32.8 us -> 0 us
    all_gather x3 -> x0, waiting for transfers between devices: 93.2 us -> none  [the longest x1 59 us: on_device(): down_full = lax.all_gather(expert_down, 'fsdp', axis=1, tiled=True)]
    pallas_call x1, Pallas kernels: 27.5 us -> 113 us  [on_device(): pl.pallas_call(functools.partial(forward_kernel, experts, fsdp, peers), o...]
    all_to_all x1 -> x0, blocking collectives: 32.8 us -> none  [on_device(): lax.all_to_all(sent, 'expert', split_axis=0, concat_axis=1, tiled=True)]
    all_to_all x1 -> x0, waiting for transfers between devices: 22.9 us -> none  [on_device(): lax.all_to_all(grad_sent, 'expert', split_axis=0, concat_axis=1, tiled=True)]
  transfers between devices with their start and end apart: 10 -> 6, of which waited for: 9 -> 6; matrix products, arithmetic and copies ran while one was open for 4% -> 3% of each run, Pallas kernels for 4% -> 0%
where the time goes in v2:
time: 598 us; the launch traced here: 594 us
  waiting for transfers between devices  336 us (56%)
  Pallas kernels  196 us (33%)
  local copies, waits for them, and re-layouts  31.7 us (5%)
  between operations  13.9 us (2%)
  starting transfers between devices  9.01 us (2%)
  other arithmetic  7.42 us (1%)
    pallas_call x1, Pallas kernels, on_device(): pl.pallas_call(functools.partial(forward_kernel, experts, fsdp, peers), o...  113 us
    reduce_scatter x1, waiting for transfers between devices, on_device(): lax.psum_scatter(up_part, 'fsdp', scatter_dimension=1, tiled=True)  107 us
    reduce_scatter x1, waiting for transfers between devices, on_device(): lax.psum_scatter(down_part, 'fsdp', scatter_dimension=1, tiled=True)  102 us
    reduce_scatter x1, waiting for transfers between devices, on_device(): lax.psum_scatter(params_grad, 'fsdp', scatter_dimension=0, tiled=True)  60.8 us
    pallas_call x1, Pallas kernels, on_device(): pl.pallas_call(expert_kernel, grid=(held,), out_shape=(shape((held, exper...  43 us
    pallas_call x1, Pallas kernels, on_device(): pl.pallas_call(functools.partial(backward_kernel, experts), out_shape=(sh...  40.2 us
    all_to_all x1, waiting for transfers between devices, on_device(): lax.all_to_all(grad_rows, 'expert', split_axis=1, concat_axis=0, tiled=True)  24.7 us
    all_to_all x1, waiting for transfers between devices, on_device(): lax.all_to_all(back, 'expert', split_axis=1, concat_axis=0, tiled=True)  22.4 us
  transfers between devices with their start and end apart: 6, of which 6 were waited for; matrix products, arithmetic and copies ran while one was open for 3% of the time, Pallas kernels for 0%

profile of v2, /device:TPU:28, one launch (start us, length us, event | category | flops | bytes accessed | tf_op | source)
XLA Modules:
  0.0 594.2 jit_solution(12496750165974639480)
XLA Ops:
  7.2 0.8 pad_maximum_fusion
  8.1 0.7 compare_select_fusion
  8.8 0.7 pad_add_fusion
  9.6 0.8 copy.45
  11.9 0.8 copy.47.meta_row_ref
  13.0 1.1 pad.19
  14.3 1.1 pad.20
  15.4 0.7 concatenate.7.shard_ref
  16.2 112.6 %attention_forward.1 = (bf16[1024,512]{1,0:T(8,128)(2,1)}, bf16[1024,1536]{1,0:T(8,128)(2,1)}, bf16[1024,2048]{1,0:T(8,128)(2,1)}, bf16[1024,512]{1,0:T(8,128)(2...) custom-call(bf16[1024,512]{1,0:T(8,128)(2,1)} %bitcast.24, ...), custom_call_target="tpu_custom_call" | custom-call | tf_op jit(solution)/shard_map/attention_forward/pallas_call | solution.py:581
  128.7 43.0 %experts.1 = (bf16[4,544,512]{2,1,0:T(8,128)(2,1)}, bf16[4,544,512]{2,1,0:T(8,128)(2,1)}, bf16[4,512,2048]{2,1,0:T(8,128)(2,1)}, bf16[4,2048,512]{2,1,0:T(8,128)(2,1)}) custom-call(bf16[4,544,512]{2,1,0:T(8,128)(2,1)} %bitcast.35, bf16[4,544,512]{2,1,0:T(8,128)(2,1)} %bitcast.36, bf16[4,512,2048]{2,1,0:T(8,128)(2,1)} %get-tuple-element.41.up_ref, ...), custom_call_target="tpu_custom_call" | custom-call | tf_op jit(solution)/shard_map/experts/pallas_call | solution.py:609
  171.7 4.7 copy.48
  176.4 4.0 all-to-all-start
  180.4 4.8 copy.50
  185.1 22.4 %all-to-all-done = bf16[4,544,512]{2,0,1:T(4,128)(2,1)S(1)} async-done(((bf16[4,544,512]{2,0,1:T(4,128)(2,1)}), bf16[4,544,512]{2,0,1:T(4,128)(2,1)S(1)}, u32[]{:S(2)}, u32[]{:S(2)}) %all-to-all-start) | async-done | bytes 2228256 | tf_op jit(solution)/shard_map/all_to_all | solution.py:625
  207.5 4.9 all-to-all-start.1
  212.5 1.8 copy.49
  214.3 24.7 %all-to-all-done.1 = bf16[4,544,512]{2,0,1:T(4,128)(2,1)} async-done(((bf16[4,544,512]{2,0,1:T(4,128)(2,1)}), bf16[4,544,512]{2,0,1:T(4,128)(2,1)}, u32[]{:S(2)}, u32[]{:S(2)}) %all-to-all-start.1) | async-done | bytes 2228256 | tf_op jit(solution)/shard_map/all_to_all | solution.py:626
  239.0 3.4 copy.51
  242.4 40.2 %attention_backward.1 = (bf16[1024,512]{1,0:T(8,128)(2,1)}, f32[1024,512]{1,0:T(8,128)}, bf16[512,2176]{1,0:T(8,128)(2,1)}) custom-call(bf16[1024,512]{1,0:T(8,128)(2,1)} %bitcast.25, bf16[1024,512]{1,0:T(8,128)(2,1)} %bitcast.27, s32[1024,4]{1,0:T(8,128)} %bitcast.33, bf16[512,2176]{1,0:T(8,128)(2,1)} %get-tuple-element.31.params_ref, ...), custom_call_target="tpu_custom_call" | custom-call | tf_op jit(solution)/shard_map/attention_backward/pallas_call | solution.py:634
  282.6 60.8 %reduce-scatter.4.cloned.1.call-done = bf16[32,2176]{1,0:T(8,128)(2,1)} async-done(((bf16[512,2176]{1,0:T(8,128)(2,1)}), bf16[32,2176]{1,0:T(8,128)(2,1)}) %reduce-scatter.4.cloned.1.call-update) | async-done | bytes 139280 | tf_op jit(solution)/shard_map/reduce_scatter | solution.py:658
  345.6 1.2 reshape.81
  346.8 1.7 slice.42
  348.5 1.5 reshape.83
  350.0 18.3 %all-reduce.7.cloned.1.call-done = bf16[32,2176]{1,0:T(8,128)(2,1)} async-done(((bf16[32,2176]{1,0:T(8,128)(2,1)}), bf16[32,2176]{1,0:T(8,128)(2,1)}) %all-reduce.7.cloned.1.call-update) | async-done | bytes 139280 | tf_op jit(solution)/shard_map/psum | solution.py:659
  369.7 1.4 slice.44
  371.1 1.6 slice.43
  372.6 0.9 convert_element_type.16
  373.6 0.7 slice_reduce_fusion
  374.3 102.3 %reduce-scatter.8.cloned.1.call-done = bf16[4,128,512]{2,1,0:T(8,128)(2,1)} async-done(((bf16[4,2048,512]{2,1,0:T(8,128)(2,1)}), bf16[4,128,512]{2,1,0:T(8,128)(2,1)}) %reduce-scatter.8.cloned.1.call-update) | async-done | bytes 524304 | tf_op jit(solution)/shard_map/reduce_scatter | solution.py:628
  476.6 2.1 convert_element_type.18
  478.7 106.8 %reduce-scatter.6.cloned.1.call-done = bf16[4,32,2048]{2,1,0:T(8,128)(2,1)} async-done(((bf16[4,512,2048]{2,1,0:T(8,128)(2,1)}), bf16[4,32,2048]{2,1,0:T(8,128)(2,1)}) %reduce-scatter.6.cloned.1.call-update) | async-done | bytes 524304 | tf_op jit(solution)/shard_map/reduce_scatter | solution.py:627
  585.5 2.1 convert_element_type.17
  (35 shorter events, 5.8 us)
Async XLA Ops:
  7.2 5.5 copy-start.1
  11.9 2.2 copy-start
  11.9 2.2 copy-start.2
  14.0 1.4 copy-start.4
  14.0 1.4 copy-start.5
  14.0 1.4 copy-start.6
  14.1 1.4 copy-start.7
  176.4 31.1 %all-to-all-start = ((bf16[4,544,512]{2,0,1:T(4,128)(2,1)}), bf16[4,544,512]{2,0,1:T(4,128)(2,1)S(1)}, u32[]{:S(2)}, u32[]{:S(2)}) async-start(bf16[4,544,512]{2,0,1:T(4,128)(2,1)} %copy.48), calls=%async_computation | async-start | bytes 4456448 | tf_op jit(solution)/shard_map/all_to_all | solution.py:625
  207.5 31.5 %all-to-all-start.1 = ((bf16[4,544,512]{2,0,1:T(4,128)(2,1)}), bf16[4,544,512]{2,0,1:T(4,128)(2,1)}, u32[]{:S(2)}, u32[]{:S(2)}) async-start(bf16[4,544,512]{2,0,1:T(4,128)(2,1)} %copy.50), calls=%async_computation.1 | async-start | bytes 4456448 | tf_op jit(solution)/shard_map/all_to_all | solution.py:626
  212.4 131.0 %reduce-scatter.4.cloned.1.call-start = ((), (), s32[]{:S(2)}) async-start(), calls=%async_computation.5 | async-start | bytes 2367488 | tf_op jit(solution)/shard_map/reduce_scatter | solution.py:658
  282.6 85.7 %all-reduce.7.cloned.1.call-start = ((), (), s32[]{:S(2)}) async-start(), calls=%async_computation.6 | async-start | bytes 278528 | tf_op jit(solution)/shard_map/psum | solution.py:659
  343.4 133.2 %reduce-scatter.8.cloned.1.call-start = ((), (), s32[]{:S(2)}) async-start(), calls=%async_computation.8 | async-start | bytes 8912896 | tf_op jit(solution)/shard_map/reduce_scatter | solution.py:628
  344.2 241.4 %reduce-scatter.6.cloned.1.call-start = ((), (), s32[]{:S(2)}) async-start(), calls=%async_computation.7 | async-start | bytes 8912896 | tf_op jit(solution)/shard_map/reduce_scatter | solution.py:627
  344.2 1.2 copy-start.3
Sparse Core Ops, SparseCore 0:
  282.7 60.6 reduce-scatter.3
  345.8 22.4 all-reduce.6
  372.9 103.6 reduce-scatter.7
  481.1 104.4 reduce-scatter.5

commit v3 on v2

--- a/solution.py
+++ b/solution.py
@@ -20,7 +20,7 @@
 LANES = 128
 NORM_LANE = 64
 FF_CHUNK = 512
-VMEM_LIMIT = 60 * 1024 * 1024
+VMEM_LIMIT = 62 * 1024 * 1024
 
 MESH = pl.DeviceIdType.MESH
 F32 = jnp.float32
@@ -404,56 +404,288 @@
         gather.finish_send()
 
 
-def expert_kernel(rows_ref, grad_ref, up_ref, down_ref, back_ref, grad_rows_ref, up_part_ref, down_part_ref, back_sum, grad_sum):
+class Scatter:
+    def __init__(self, place, part, sums, across, line, send, recv):
+        self.place, self.part, self.sums, self.across, self.line = place, part, sums, across, line
+        self.send, self.recv = send, recv
+
+    def remote(self, source, target, item, route, a, b, c):
+        return pltpu.make_async_remote_copy(
+            src_ref=source, dst_ref=target, send_sem=self.send.at[item, route], recv_sem=self.recv.at[item, route],
+            device_id=self.place.at(a, b, c), device_id_type=MESH,
+        )
+
+    def core_copy(self, item):
+        p = self.place
+        return self.remote(self.part(item).at[:, :, 1 - p.c], self.sums.at[item], item, 0, p.a, p.b, 1 - p.c)
+
+    def across_copies(self, item):
+        p = self.place
+        out = []
+        for j in range(p.B - 1):
+            to, back = p.other_b(j), p.B - 2 - j
+            copy = self.remote(self.sums.at[item, :, to], self.across.at[item, back], item, 1 + back, p.a, to, p.c)
+            out.append(copy)
+        return out
+
+    def line_copies(self, item):
+        p = self.place
+        out = []
+        for k in range(1, p.A):
+            to, back = lax.rem(p.a + k, p.A), p.A - 1 - k
+            copy = self.remote(self.sums.at[item, to, p.b], self.line.at[item, back], item, p.B + back, to, p.b, p.c)
+            out.append(copy)
+        return out
+
+    def start(self, item):
+        self.core_copy(item).start()
+
+    def core_step(self, item):
+        p = self.place
+        self.core_copy(item).wait()
+        part = self.part(item)
+
+        @pl.loop(0, p.A * p.B)
+        def _(i):
+            a, b = lax.div(i, p.B), lax.rem(i, p.B)
+            total = self.sums[item, a, b].astype(F32) + part[a, b, p.c].astype(F32)
+            self.sums[item, a, b] = total.astype(BF16)
+
+        for copy in self.across_copies(item):
+            copy.start()
+
+    def across_step(self, item):
+        p = self.place
+        for copy in self.across_copies(item):
+            copy.wait_recv()
+
+        @pl.loop(0, p.A)
+        def _(a):
+            total = self.sums[item, a, p.b].astype(F32)
+            for j in range(p.B - 1):
+                total += self.across[item, j, a].astype(F32)
+            self.sums[item, a, p.b] = total.astype(BF16)
+
+        for copy in self.line_copies(item):
+            copy.start()
+
+    def line_step(self, item):
+        p = self.place
+        for copy in self.line_copies(item):
+            copy.wait_recv()
+        total = self.sums[item, p.a, p.b].astype(F32)
+        for k in range(p.A - 1):
+            total += self.line[item, k].astype(F32)
+        return total
+
+    def finish(self, item):
+        for copy in self.across_copies(item) + self.line_copies(item):
+            copy.wait_send()
+
+
+def backward_kernel(
+    experts, fsdp, peers,
+    x_in, cot_in, meta_ref, params_in, act_one_in, triple_in, weights_in, attended_in, mid_in, act_two_in, probs_in,
+    arrived_in, grad_arrived_in, cot_slots_in, up_full, down_full,
+    out_out, input_grad_out, share_out, up_grad_out, down_grad_out,
+    x_ref, params_ref, triple_ref, probs_ref,
+    rows_ref, grad_ref, up_ref, down_ref, back_ref, grad_slots_ref, float_ref,
+    part_up, part_down, sums_up, sums_down, sums_par, across_up, across_down, across_par, line_up, line_down, line_par,
+    stage_up, stage_down, swap_ref,
+    dot_row_ref, place_ref, gated_ref, logit_grad_ref, column_ref,
+    load_sem, expert_sem, late_sem, save_sem, return_send, return_recv, swap_send, swap_recv,
+    up_send, up_recv, down_send, down_recv, par_send, par_recv, stage_sem,
+):
+    width = x_ref.shape[1]
+    rows_pad = x_ref.shape[0]
+    groups = rows_pad // BLOCK
+    places = back_ref.shape[0]
+    capacity = places // experts
+    held = up_full.shape[0]
+    expert_rows = places // held
     hidden_width = up_ref.shape[2]
     chunks = hidden_width // FF_CHUNK
-    back_sum[...] = jnp.zeros_like(back_sum)
-    grad_sum[...] = jnp.zeros_like(grad_sum)
-
-    @pl.loop(0, chunks)
-    def _(f):
-        at = pl.ds(pl.multiple_of(f * FF_CHUNK, FF_CHUNK), FF_CHUNK)
-        rows, grads = rows_ref[0], grad_ref[0]
-        up, down = up_ref[0, :, at], down_ref[0, at, :]
-        hidden = dot(rows, up)
-        spread = 0.5 * (1.0 + lax.erf(hidden * ROOT_HALF))
-        active = (hidden * spread).astype(BF16)
-        slope = spread + hidden * (DENSITY_SCALE * jnp.exp(-0.5 * hidden * hidden))
-        back_sum[...] += dot(active, down)
-        grad_hidden = (dot_against(grads, down) * slope).astype(BF16)
-        grad_sum[...] += dot_against(grad_hidden, up)
-        up_part_ref[0, :, at] = dot_rows(rows, grad_hidden).astype(BF16)
-        down_part_ref[0, at, :] = dot_rows(active, grads).astype(BF16)
-
-    back_ref[0] = back_sum[...].astype(BF16)
-    grad_rows_ref[0] = grad_sum[...].astype(BF16)
-
-
-def backward_kernel(
-    experts,
-    x_ref, cot_ref, meta_ref, params_ref, act_one_ref, triple_ref, weights_ref, attended_ref, mid_ref, act_two_ref,
-    probs_ref, back_ref, grad_slots_ref, cot_slots_ref,
-    out_ref, input_grad_ref, params_grad_ref,
-    dot_row_ref, place_ref, gated_ref, branch_ref, grad_triple_ref, logit_grad_ref, sums_ref,
-):
-    width = x_ref.shape[1]
-    groups = x_ref.shape[0] // BLOCK
-    places = back_ref.shape[0]
+    place = Place(fsdp)
+    copy_in = pltpu.make_async_copy
+    loads = [
+        copy_in(there, here, load_sem.at[i])
+        for i, (there, here) in enumerate(
+            ((params_in, params_ref), (triple_in, triple_ref), (probs_in, probs_ref),
+             (x_in, x_ref))
+        )
+    ]
+
+    def held_rows(e):
+        return pl.ds(pl.multiple_of(e * expert_rows, 16), expert_rows)
+
+    def expert_loads(e):
+        slot = lax.rem(e, 2)
+        return [
+            copy_in(arrived_in.at[e], rows_ref.at[held_rows(e), :], expert_sem.at[0, slot]),
+            copy_in(grad_arrived_in.at[e], grad_ref.at[held_rows(e), :], expert_sem.at[1, slot]),
+            copy_in(up_full.at[e], up_ref.at[slot], expert_sem.at[2, slot]),
+            copy_in(down_full.at[e], down_ref.at[slot], expert_sem.at[3, slot]),
+        ]
+
+    for copy in expert_loads(0) + loads:
+        copy.start()
+    greet(place, peers, False)
+
+    A, B = place.A, place.B
+    up = Scatter(
+        place, lambda e: part_up.at[lax.rem(e, 2), :, :, :, :, pl.ds(0, hidden_width)],
+        sums_up, across_up, line_up, up_send, up_recv,
+    )
+    down = Scatter(place, lambda e: part_down.at[lax.rem(e, 2)], sums_down, across_down, line_down, down_send, down_recv)
+    par = Scatter(place, lambda e: part_up.at[0], sums_par, across_par, line_par, par_send, par_recv)
+
+    def slot_rows(e, x):
+        return pl.ds(pl.multiple_of((x * held + e) * capacity, 16), capacity)
+
+    def returns(e):
+        out = []
+        for i, (here, there) in enumerate(((rows_ref, back_ref), (grad_ref, grad_slots_ref))):
+            for k in range(1, peers):
+                to, back = lax.rem(place.x + k, peers), peers - 1 - k
+                out.append(
+                    pltpu.make_async_remote_copy(
+                        src_ref=here.at[pl.ds(pl.multiple_of(e * expert_rows + to * capacity, 16), capacity), :],
+                        dst_ref=there.at[slot_rows(e, place.x), :],
+                        send_sem=return_send.at[i, e, back], recv_sem=return_recv.at[i, e, back],
+                        device_id=(to, place.me), device_id_type=MESH,
+                    )
+                )
+        return out
+
+    @pl.loop(0, held)
+    def _(e):
+        slot = lax.rem(e, 2)
+
+        @pl.when(e + 1 < held)
+        def _():
+            for copy in expert_loads(e + 1):
+                copy.start()
+
+        for copy in expert_loads(e):
+            copy.wait()
+        float_ref[...] = jnp.zeros_like(float_ref)
+
+        @pl.loop(0, chunks)
+        def _(f):
+            at = pl.ds(pl.multiple_of(f * FF_CHUNK, FF_CHUNK), FF_CHUNK)
+            rows, grads = rows_ref[held_rows(e), :], grad_ref[held_rows(e), :]
+            up_part, down_part = up_ref[slot, :, at], down_ref[slot, at, :]
+            hidden = dot(rows, up_part)
+            spread = 0.5 * (1.0 + lax.erf(hidden * ROOT_HALF))
+            active = (hidden * spread).astype(BF16)
+            slope = spread + hidden * (DENSITY_SCALE * jnp.exp(-0.5 * hidden * hidden))
+            float_ref[:expert_rows, :] += dot(active, down_part)
+            grad_hidden = (dot_against(grads, down_part) * slope).astype(BF16)
+            float_ref[expert_rows : 2 * expert_rows, :] += dot_against(grad_hidden, up_part)
+            size = part_up.shape[4]
+            part_up[slot, :, :, :, :, at] = dot_rows(rows, grad_hidden).astype(BF16).reshape(A, B, 2, size, FF_CHUNK)
+            size = part_down.shape[4]
+            blocks = FF_CHUNK // size // 2
+            value = dot_rows(active, grads).astype(BF16).reshape(blocks, 2, size, width)
+            for i in range(blocks):
+                line = f * blocks + i
+                part_down[slot, lax.div(line, B), lax.rem(line, B)] = value[i]
+
+            @pl.when(jnp.logical_and(f == 0, e >= 1))
+            def _():
+                up.core_step(e - 1)
+                down.core_step(e - 1)
+
+        rows_ref[held_rows(e), :] = float_ref[:expert_rows, :].astype(BF16)
+        grad_ref[held_rows(e), :] = float_ref[expert_rows : 2 * expert_rows, :].astype(BF16)
+        for copy in returns(e):
+            copy.start()
+        own = pl.ds(pl.multiple_of(e * expert_rows + place.x * capacity, 16), capacity)
+        back_ref[slot_rows(e, place.x), :] = rows_ref[own, :]
+        grad_slots_ref[slot_rows(e, place.x), :] = grad_ref[own, :]
+        up.start(e)
+        down.start(e)
+
+    def late_loads():
+        out = []
+        for g in range(groups):
+            half = groups // 2
+            rows = pl.ds((g % half) * BLOCK, BLOCK)
+            out.append(copy_in(weights_in.at[pl.ds(g * BLOCK, BLOCK), :], up_ref.at[g // half, rows, :], late_sem.at[4 + g]))
+        for i, array in enumerate((act_one_in, attended_in, act_two_in, cot_in)):
+            rows = pl.ds((i % 2) * rows_pad, rows_pad)
+            out.append(copy_in(array, down_ref.at[i // 2, rows, :], late_sem.at[i]))
+        out.append(copy_in(mid_in, float_ref.at[pl.ds(0, rows_pad), :], late_sem.at[4 + groups]))
+        return out
+
+    for copy in late_loads():
+        copy.start()
+    act_one = down_ref.at[0, pl.ds(0, rows_pad), :]
+    attended = down_ref.at[0, pl.ds(rows_pad, rows_pad), :]
+    act_two = down_ref.at[1, pl.ds(0, rows_pad), :]
+    cot_ref = down_ref.at[1, pl.ds(rows_pad, rows_pad), :]
+    input_grad_ref = float_ref
+
+    def stage_copies(e):
+        slot = lax.rem(e, 2)
+        return (
+            copy_in(stage_up.at[slot], up_grad_out.at[e], stage_sem.at[0, slot]),
+            copy_in(stage_down.at[slot], down_grad_out.at[e], stage_sem.at[1, slot]),
+        )
+
+    def expert_line(e):
+        if e >= 2:
+            for copy in stage_copies(e - 2):
+                copy.wait()
+        stage_up[e % 2] = up.line_step(e)
+        stage_down[e % 2] = down.line_step(e)
+        for copy in stage_copies(e):
+            copy.start()
+
+    def expert_across(e):
+        up.across_step(e)
+        down.across_step(e)
+
+    up.core_step(held - 1)
+    down.core_step(held - 1)
+    expert_across(0)
+
+    for copy in loads + late_loads():
+        copy.wait()
+    slot_loads = [
+        copy_in(cot_slots_in.at[held_rows(e), :], rows_ref.at[held_rows(e), :], load_sem.at[4 + e]) for e in range(held)
+    ]
+    for e in range(held):
+        for copy in returns(e):
+            copy.wait()
+        slot_loads[e].start()
+    for copy in slot_loads:
+        copy.wait()
+
     small = params_ref[:, 4 * width :]
     small_rows = jnp.transpose(small.astype(F32))
     gain_one = small_rows[NORM_LANE : NORM_LANE + 1]
     gain_two = small_rows[NORM_LANE + 2 : NORM_LANE + 3]
-    sums_ref[...] = jnp.zeros_like(sums_ref)
+    column_ref[...] = jnp.zeros_like(column_ref)
 
     @pl.loop(0, places // LANES)
     def _(c):
         at = pl.ds(pl.multiple_of(c * LANES, LANES), LANES)
-        column = jnp.sum(back_ref[at, :].astype(F32) * cot_slots_ref[at, :].astype(F32), axis=1, keepdims=True)
+        column = jnp.sum(back_ref[at, :].astype(F32) * rows_ref[at, :].astype(F32), axis=1, keepdims=True)
         dot_row_ref[0:1, at] = to_row(column)
+
+    def saves(g):
+        rows = rows_of(g)
+        return (
+            copy_in(cot_ref.at[rows, :], out_out.at[rows, :], save_sem.at[0, g]),
+            copy_in(input_grad_ref.at[rows, :], input_grad_out.at[rows, :], save_sem.at[1, g]),
+        )
 
     @pl.loop(0, groups)
     def _(g):
         rows = rows_of(g)
+        half_groups = groups // 2
+        weight_rows = rows_of(lax.rem(g, half_groups))
         meta = meta_ref[rows, :]
         probs = probs_ref[rows, :]
         gate_first, gate_second = gates_of(probs, meta)
@@ -471,20 +703,18 @@
             grad_second += jnp.where(in_second, dots, 0.0)
         grad_first = jnp.sum(grad_first, axis=1, keepdims=True)
         grad_second = jnp.sum(grad_second, axis=1, keepdims=True)
-        mid = mid_ref[rows, :]
-        out_ref[rows, :] = (mid + dot(gated_ref[...], back_ref[...])).astype(BF16)
+        mid = input_grad_ref[rows, :]
         grad_probs = jnp.where(lane == meta[:, 2:3], grad_first, 0.0) + jnp.where(lane == meta[:, 3:4], grad_second, 0.0)
         grad_logits = (probs * (grad_probs - jnp.sum(grad_probs * probs, axis=-1, keepdims=True))).astype(BF16)
         logit_grad_ref[rows, :] = grad_logits
         grad_act = dot(place_ref[...], grad_slots_ref[...]) + dot_against(grad_logits, small)
         normed, inverse = normalize(mid)
-        sums_ref[NORM_LANE + 2 : NORM_LANE + 3, :] += jnp.sum(grad_act * normed, axis=0, keepdims=True)
-        sums_ref[NORM_LANE + 3 : NORM_LANE + 4, :] += jnp.sum(grad_act, axis=0, keepdims=True)
+        column_ref[NORM_LANE + 2 : NORM_LANE + 3, :] += jnp.sum(grad_act * normed, axis=0, keepdims=True)
+        column_ref[NORM_LANE + 3 : NORM_LANE + 4, :] += jnp.sum(grad_act, axis=0, keepdims=True)
         grad_mid = cot_ref[rows, :].astype(F32) + denormalize(grad_act, normed, inverse, gain_two)
+        cot_ref[rows, :] = (mid + dot(gated_ref[...], back_ref[...])).astype(BF16)
         input_grad_ref[rows, :] = grad_mid
-        branch = grad_mid.astype(BF16)
-        branch_ref[rows, :] = branch
-        grad_attended = dot_against(branch, params_ref[:, 3 * width : 4 * width]).astype(BF16)
+        grad_attended = dot_against(grad_mid.astype(BF16), params_ref[:, 3 * width : 4 * width]).astype(BF16)
         low = lane < HEAD_DIM
         for pair in range(HEADS // 2):
             at = pair * LANES
@@ -497,7 +727,7 @@
                 mask = low if half == 0 else jnp.logical_not(low)
                 upstream_half = jnp.where(mask, upstream, 0.0).astype(BF16)
                 head = (2 * pair + half) * BLOCK
-                weights = weights_ref[rows, head : head + BLOCK]
+                weights = up_ref[lax.div(g, half_groups), weight_rows, head : head + BLOCK]
                 kept = weights.astype(F32)
                 grad_weights = dot_against(upstream_half, v)
                 inner = jnp.sum(grad_weights * kept, axis=-1, keepdims=True)
@@ -505,20 +735,71 @@
                 grad_q += dot(grad_scores, jnp.where(mask, k, 0.0).astype(BF16))
                 grad_k += dot_rows(grad_scores, jnp.where(mask, q, 0.0).astype(BF16))
                 grad_v += dot_rows(weights, upstream_half)
-            grad_triple_ref[rows, at : at + LANES] = (grad_q * HEAD_DIM ** (-0.5)).astype(BF16)
-            grad_triple_ref[rows, width + at : width + at + LANES] = grad_k.astype(BF16)
-            grad_triple_ref[rows, 2 * width + at : 2 * width + at + LANES] = grad_v.astype(BF16)
-        grad_act = dot_against(grad_triple_ref[rows, :], params_ref[:, : 3 * width])
+            triple_ref[rows, at : at + LANES] = (grad_q * HEAD_DIM ** (-0.5)).astype(BF16)
+            triple_ref[rows, width + at : width + at + LANES] = grad_k.astype(BF16)
+            triple_ref[rows, 2 * width + at : 2 * width + at + LANES] = grad_v.astype(BF16)
+        grad_act = dot_against(triple_ref[rows, :], params_ref[:, : 3 * width])
         normed, inverse = normalize(x_ref[rows, :].astype(F32))
-        sums_ref[NORM_LANE : NORM_LANE + 1, :] += jnp.sum(grad_act * normed, axis=0, keepdims=True)
-        sums_ref[NORM_LANE + 1 : NORM_LANE + 2, :] += jnp.sum(grad_act, axis=0, keepdims=True)
-        input_grad_ref[rows, :] += denormalize(grad_act, normed, inverse, gain_one)
-
-    params_grad_ref[:, : 3 * width] = dot_rows(act_one_ref[...], grad_triple_ref[...]).astype(BF16)
-    params_grad_ref[:, 3 * width : 4 * width] = dot_rows(attended_ref[...], branch_ref[...]).astype(BF16)
-    router_part = dot_rows(act_two_ref[...], logit_grad_ref[...])
-    norm_part = jnp.transpose(sums_ref[...])
-    params_grad_ref[:, 4 * width :] = (router_part + norm_part).astype(BF16)
+        column_ref[NORM_LANE : NORM_LANE + 1, :] += jnp.sum(grad_act * normed, axis=0, keepdims=True)
+        column_ref[NORM_LANE + 1 : NORM_LANE + 2, :] += jnp.sum(grad_act, axis=0, keepdims=True)
+        grad_mid = input_grad_ref[rows, :]
+        x_ref[rows, :] = grad_mid.astype(BF16)
+        input_grad_ref[rows, :] = grad_mid + denormalize(grad_act, normed, inverse, gain_one)
+        for copy in saves(g):
+            copy.start()
+        pl.when(g == 0)(lambda: expert_across(1))
+        pl.when(g == 2)(lambda: expert_line(0))
+        pl.when(g == 2)(lambda: expert_across(2))
+
+    size = part_up.shape[4]
+    split = (A, B, 2, size)
+    part_up[0, :, :, :, :, : 3 * width] = dot_rows(act_one[...], triple_ref[...]).astype(BF16).reshape(*split, 3 * width)
+    part_up[0, :, :, :, :, 3 * width : 4 * width] = dot_rows(attended[...], x_ref[...]).astype(BF16).reshape(*split, width)
+    small_part = dot_rows(act_two[...], logit_grad_ref[...]) + jnp.transpose(column_ref[...])
+    part_up[0, :, :, :, :, 4 * width :] = small_part.astype(BF16).reshape(*split, LANES)
+    par.start(0)
+    expert_line(1)
+    par.core_step(0)
+    expert_across(3)
+    expert_line(2)
+    par.across_step(0)
+    expert_line(3)
+    swap_ref[place.x] = par.line_step(0).astype(BF16)
+
+    def swaps():
+        out = []
+        for k in range(1, peers):
+            to, back = lax.rem(place.x + k, peers), peers - 1 - k
+            out.append(
+                pltpu.make_async_remote_copy(
+                    src_ref=swap_ref.at[place.x], dst_ref=swap_ref.at[place.x],
+                    send_sem=swap_send.at[back], recv_sem=swap_recv.at[back],
+                    device_id=(to, place.me), device_id_type=MESH,
+                )
+            )
+        return out
+
+    for copy in swaps():
+        copy.start()
+
+    @pl.loop(0, groups)
+    def _(g):
+        for copy in saves(g):
+            copy.wait()
+
+    for e in range(held - 2, held):
+        for copy in stage_copies(e):
+            copy.wait()
+    for e in range(held):
+        up.finish(e)
+        down.finish(e)
+    par.finish(0)
+    for copy in swaps():
+        copy.wait()
+    total = swap_ref[0].astype(F32)
+    for i in range(1, peers):
+        total += swap_ref[i].astype(F32)
+    share_out[...] = total
 
 
 def on_device(
@@ -534,7 +815,7 @@
     experts = held * peers
     capacity = (42 * rows_dev + 20 * experts - 1) // (20 * experts)
     capacity = -(-capacity // 16) * 16
-    places = -(-experts * capacity // LANES) * LANES
+    places = experts * capacity
 
     def pad_rows(array, value=0):
         array = array.reshape(groups, GROUP_ROWS, array.shape[1])
@@ -602,61 +883,52 @@
     arrived = arrived.reshape(held, expert_rows, width)
     grad_arrived = grad_arrived.reshape(held, expert_rows, width)
     hidden_width = up_full.shape[2]
-
-    def block(*dims):
-        return pl.BlockSpec((1, *dims), lambda e: (e, 0, 0))
-
-    back, grad_rows, up_part, down_part = pl.pallas_call(
-        expert_kernel,
-        grid=(held,),
-        out_shape=(
-            shape((held, expert_rows, width), BF16),
-            shape((held, expert_rows, width), BF16),
-            shape((held, width, hidden_width), BF16),
-            shape((held, hidden_width, width), BF16),
-        ),
-        in_specs=[block(expert_rows, width)] * 2 + [block(width, hidden_width), block(hidden_width, width)],
-        out_specs=[block(expert_rows, width)] * 2 + [block(width, hidden_width), block(hidden_width, width)],
-        scratch_shapes=[pltpu.VMEM((expert_rows, width), F32)] * 2,
-        compiler_params=params_spec,
-        name="experts",
-    )(arrived, grad_arrived, up_full, down_full)
-
-    returned = lax.all_to_all(back, "expert", split_axis=1, concat_axis=0, tiled=True)
-    grad_returned = lax.all_to_all(grad_rows, "expert", split_axis=1, concat_axis=0, tiled=True)
-    up_grad = lax.psum_scatter(up_part, "fsdp", scatter_dimension=1, tiled=True).astype(F32)
-    down_grad = lax.psum_scatter(down_part, "fsdp", scatter_dimension=1, tiled=True).astype(F32)
-
-    def flat(array):
-        array = array.reshape(experts * capacity, width)
-        return jnp.pad(array, ((0, places - experts * capacity), (0, 0)))
-
-    out, input_grad, params_grad = pl.pallas_call(
-        functools.partial(backward_kernel, experts),
+    up_rows, down_rows = expert_up.shape[1], expert_down.shape[1]
+    A, B = 4, fsdp // 8
+    packed_width = shard.shape[1]
+
+    def buffer(*dims, dtype=BF16):
+        return pltpu.VMEM(dims, dtype)
+
+    out, input_grad, share, up_grad, down_grad = pl.pallas_call(
+        functools.partial(backward_kernel, experts, fsdp, peers),
         out_shape=(
             shape((rows_pad, width), BF16),
             shape((rows_pad, width), F32),
-            shape((width, 4 * width + LANES), BF16),
+            shape((up_rows, packed_width), F32),
+            shape(expert_up.shape, F32),
+            shape(expert_down.shape, F32),
         ),
-        in_specs=[vmem] * 14,
-        out_specs=[vmem] * 3,
+        in_specs=[hbm] * 2 + [vmem] + [hbm] * 13,
+        out_specs=[hbm] * 2 + [vmem] + [hbm] * 2,
         scratch_shapes=[
-            pltpu.VMEM((8, places), F32),
-            pltpu.VMEM((BLOCK, places), BF16),
-            pltpu.VMEM((BLOCK, places), BF16),
-            pltpu.VMEM((rows_pad, width), BF16),
-            pltpu.VMEM((rows_pad, 3 * width), BF16),
-            pltpu.VMEM((rows_pad, LANES), BF16),
-            pltpu.VMEM((LANES, width), F32),
+            buffer(rows_pad, width), buffer(*packed), buffer(rows_pad, 3 * width),
+            buffer(rows_pad, LANES, dtype=F32),
+            buffer(places, width), buffer(places, width),
+            buffer(2, width, hidden_width), buffer(2, hidden_width, width),
+            buffer(places, width), buffer(places, width),
+            buffer(max(2 * expert_rows, rows_pad), width, dtype=F32),
+            buffer(2, A, B, 2, up_rows, packed_width), buffer(2, A, B, 2, down_rows, width),
+            buffer(held, A, B, up_rows, hidden_width), buffer(held, A, B, down_rows, width), buffer(1, A, B, up_rows, packed_width),
+            buffer(held, B - 1, A, up_rows, hidden_width), buffer(held, B - 1, A, down_rows, width),
+            buffer(1, B - 1, A, up_rows, packed_width),
+            buffer(held, A - 1, up_rows, hidden_width), buffer(held, A - 1, down_rows, width),
+            buffer(1, A - 1, up_rows, packed_width),
+            buffer(2, up_rows, hidden_width, dtype=F32), buffer(2, down_rows, width, dtype=F32),
+            buffer(peers, up_rows, packed_width),
+            buffer(8, places, dtype=F32), buffer(BLOCK, places), buffer(BLOCK, places),
+            buffer(rows_pad, LANES), buffer(LANES, width, dtype=F32),
+            dma((4 + held,)), dma((4, 2)), dma((5 + groups,)), dma((2, groups)),
+            dma((2, held, peers - 1)), dma((2, held, peers - 1)), dma((peers - 1,)), dma((peers - 1,)),
+            dma((held, A + B - 1)), dma((held, A + B - 1)), dma((held, A + B - 1)), dma((held, A + B - 1)),
+            dma((1, A + B - 1)), dma((1, A + B - 1)), dma((2, 2)),
         ],
-        compiler_params=params_spec,
-        name="attention_backward",
+        compiler_params=pltpu.CompilerParams(vmem_limit_bytes=VMEM_LIMIT, collective_id=1, has_side_effects=True),
+        name="experts_and_backward",
     )(
         x, cot, meta, params, act_one, triple, weights, attended, mid, act_two, probs,
-        flat(returned), flat(grad_returned), flat(cot_slots),
+        arrived, grad_arrived, cot_slots.reshape(experts * capacity, width), up_full, down_full,
     )
-    share = lax.psum_scatter(params_grad, "fsdp", scatter_dimension=0, tiled=True)
-    share = lax.psum(share, "expert").astype(F32)
     norm_share = share[:, 4 * width + NORM_LANE : 4 * width + NORM_LANE + 4]
     return (
         cut_rows(out),

time: 598 us -> 298 us (0.50)
  waiting for transfers between devices: 336 us -> 0 us
  Pallas kernels: 196 us -> 277 us
  local copies, waits for them, and re-layouts: 31.7 us -> 16.8 us
  between operations: 13.9 us -> 0.74 us
  starting transfers between devices: 9.01 us -> 0 us
    reduce_scatter x3 -> x0, waiting for transfers between devices: 270 us -> none  [the longest x1 107 us: on_device(): lax.psum_scatter(up_part, 'fsdp', scatter_dimension=1, tiled=True)]
    pallas_call x2 -> x1, Pallas kernels: 83.1 us -> 164 us  [on_device(): pl.pallas_call(functools.partial(backward_kernel, experts, fsdp, peers),...]
    all_to_all x2 -> x0, waiting for transfers between devices: 47.1 us -> none  [the longest x1 24.7 us: on_device(): lax.all_to_all(grad_rows, 'expert', split_axis=1, concat_axis=0, tiled=True)]
    psum x1 -> x0, waiting for transfers between devices: 18.3 us -> none  [on_device(): share = lax.psum(share, 'expert').astype(F32)]
    pallas_call x2 -> x0, local copies, waits for them, and re-layouts: 9.46 us -> none  [on_device(): pl.pallas_call(expert_kernel, grid=(held,), out_shape=(shape((held, exper...]
    all_to_all x2 -> x0, starting transfers between devices: 8.85 us -> none  [the longest x1 4.89 us: on_device(): lax.all_to_all(grad_rows, 'expert', split_axis=1, concat_axis=0, tiled=True)]
  transfers between devices with their start and end apart: 6 -> 0, of which waited for: 6 -> 0; matrix products, arithmetic and copies ran while one was open for 3% -> 0% of each run, Pallas kernels for 0% -> 0%
where the time goes in v3:
time: 298 us; the launch traced here: 297 us
  Pallas kernels  277 us (93%)
  local copies, waits for them, and re-layouts  16.8 us (6%)
    pallas_call x1, Pallas kernels, on_device(): pl.pallas_call(functools.partial(backward_kernel, experts, fsdp, peers),...  164 us
    pallas_call x1, Pallas kernels, on_device(): pl.pallas_call(functools.partial(forward_kernel, experts, fsdp, peers), o...  113 us

profile of v3, /device:TPU:28, one launch (start us, length us, event | category | flops | bytes accessed | tf_op | source)
XLA Modules:
  0.0 296.7 jit_solution(754232196953831234)
XLA Ops:
  0.6 0.0 copy-start.3
  0.7 0.8 pad_maximum_fusion
  1.5 0.1 copy.42
  1.6 0.7 compare_select_fusion
  2.3 0.7 pad_add_fusion
  3.0 0.1 reshape.65
  3.1 0.8 copy.41
  3.9 1.6 concatenate.7.shard_ref
  5.5 0.2 copy.40
  5.8 0.0 copy-start
  5.8 0.0 copy-start.4
  5.8 0.8 copy.43.meta_row_ref
  6.6 0.0 copy-done.3
  6.6 0.3 reshape.61
  6.9 1.1 pad.19
  7.9 0.0 copy-done
  7.9 0.0 copy-done.4
  7.9 0.3 reshape.63
  8.2 1.1 pad.20
  9.3 112.6 %attention_forward.1 = (bf16[1024,512]{1,0:T(8,128)(2,1)}, bf16[1024,1536]{1,0:T(8,128)(2,1)}, bf16[1024,2048]{1,0:T(8,128)(2,1)}, bf16[1024,512]{1,0:T(8,128)(2...) custom-call(bf16[1024,512]{1,0:T(8,128)(2,1)} %bitcast.16, ...), custom_call_target="tpu_custom_call" | custom-call | tf_op jit(solution)/shard_map/attention_forward/pallas_call | solution.py:862
  121.9 164.4 %experts_and_backward.1 = (bf16[1024,512]{1,0:T(8,128)(2,1)}, f32[1024,512]{1,0:T(8,128)}, f32[32,2176]{1,0:T(8,128)}, f32[4,32,2048]{2,1,0:T(8,128)}, f32[4,128,512]{2,1,0:T(8,128)}) custom-call(bf16[1024,512]{1,0:T(8,128)(2,1)} %bitcast.17, bf16[1024,512]{1,0:T(8,128)(2,1)} %bitcast.19, s32[1024,4]{1,0:T(8,128)} %bitcast.22, ...), custom_call_target="tpu_custom_call" | custom-call | tf_op jit(solution)/shard_map/experts_and_backward/pallas_call | solution.py:893
  286.3 1.3 slice.41
  287.6 1.2 reshape.71
  288.8 1.7 slice.42
  290.5 1.5 reshape.73
  292.1 0.7 slice_reduce_fusion
  292.8 0.7 copy.44
  293.5 0.6 slice.35
  294.1 0.7 slice.34
  294.8 0.0 copy-done.2
  294.8 1.0 copy.47
  295.8 1.0 copy.48
  (9 shorter events, 0.1 us)
Async XLA Ops:
  0.6 6.0 %copy-start.3 = (bf16[980,512]{1,0:T(8,128)(2,1)S(1)}, bf16[980,512]{1,0:T(8,128)(2,1)}, u32[]{:S(2)}) copy-start(bf16[980,512]{1,0:T(8,128)(2,1)} %param.13) | copy-start | bytes 3010564
  5.8 2.2 copy-start
  5.8 2.2 copy-start.4
  290.5 1.5 copy-start.5
  290.5 4.3 %copy-start.2 = (f32[4,32,2048]{2,1,0:T(8,128)S(1)}, f32[4,32,2048]{2,1,0:T(8,128)}, u32[]{:S(2)}) copy-start(f32[4,32,2048]{2,1,0:T(8,128)} %get-tuple-element.104) | copy-start | bytes 3145732
  292.1 3.7 %copy-start.1 = (f32[4,128,512]{2,1,0:T(8,128)S(1)}, f32[4,128,512]{2,1,0:T(8,128)}, u32[]{:S(2)}) copy-start(f32[4,128,512]{2,1,0:T(8,128)} %get-tuple-element.105) | copy-start | bytes 3145732

commit v4 on v2

v4 whole, which is shorter than its diff:
```python
import functools

import jax
import jax.numpy as jnp
from jax import lax
from jax.experimental import pallas as pl
from jax.experimental.pallas import tpu as pltpu
from jax.sharding import PartitionSpec as P

HEADS = 8
HEAD_DIM = 64
PATCHES = 49
EPS = 1e-06
ROOT_HALF = 0.7071067811865476
DENSITY_SCALE = 0.3989422804014327

BLOCK = 256
GROUP_IMAGES = BLOCK // PATCHES
GROUP_ROWS = GROUP_IMAGES * PATCHES
LANES = 128
NORM_LANE = 64
FF_CHUNK = 256
MAX_ROWS = 1088
VMEM_LIMIT = 62 * 1024 * 1024

MESH = pl.DeviceIdType.MESH
F32 = jnp.float32
BF16 = jnp.bfloat16


def dot(left, right):
    return lax.dot_general(left, right, (((1,), (0,)), ((), ())), preferred_element_type=F32)


def dot_rows(left, right):
    return lax.dot_general(left, right, (((0,), (0,)), ((), ())), preferred_element_type=F32)


def dot_against(left, right):
    return lax.dot_general(left, right, (((1,), (1,)), ((), ())), preferred_element_type=F32)


def iota(shape, dim):
    return lax.broadcasted_iota(jnp.int32, shape, dim)


def normalize(values):
    center = jnp.mean(values, axis=-1, keepdims=True)
    offset = values - center
    spread = jnp.mean(offset * offset, axis=-1, keepdims=True)
    inverse = lax.rsqrt(spread + EPS)
    return offset * inverse, inverse


def denormalize(upstream, normed, inverse, gain):
    scaled = upstream * gain
    return inverse * (
        scaled
        - jnp.mean(scaled, axis=-1, keepdims=True)
        - normed * jnp.mean(scaled * normed, axis=-1, keepdims=True)
    )


def to_row(column):
    n = column.shape[0]
    parts = []
    for at in range(0, n, LANES):
        eye = iota((LANES, LANES), 0) == iota((LANES, LANES), 1)
        parts.append(jnp.sum(jnp.where(eye, column[at : at + LANES], 0.0), axis=0, keepdims=True))
    return parts[0] if len(parts) == 1 else jnp.concatenate(parts, axis=1)


def rows_of(g):
    return pl.ds(pl.multiple_of(g * BLOCK, BLOCK), BLOCK)


def gates_of(probs, meta):
    lane = iota(probs.shape, 1)
    first = jnp.sum(jnp.where(lane == meta[:, 2:3], probs, 0.0), axis=1, keepdims=True)
    second = jnp.sum(jnp.where(lane == meta[:, 3:4], probs, 0.0), axis=1, keepdims=True)
    return first, second


class Place:
    def __init__(self, fsdp, xs):
        self.A, self.B = 4, fsdp // 8
        self.x = lax.axis_index("expert")
        self.me = lax.axis_index("fsdp")
        self.c = lax.rem(self.me, 2)
        line = lax.div(self.me, 2)
        self.b = lax.rem(line, self.B)
        self.a = lax.div(line, self.B)
        self.peers = xs * self.B
        self.peer = self.x * self.B + self.b

    def index(self, a, b, c):
        return (a * self.B + b) * 2 + c

    def other_b(self, j):
        return lax.rem(self.b + 1 + j, self.B)

    def at(self, a, b, c):
        return (self.x, self.index(a, b, c))

    def at_peer(self, peer):
        return (lax.div(peer, self.B), self.index(self.a, lax.rem(peer, self.B), self.c))

    def other_peer(self, k):
        return lax.rem(self.peer + k, self.peers)


def greet(place):
    barrier = pltpu.get_barrier_semaphore()

    def signal(device):
        pl.semaphore_signal(barrier, inc=1, device_id=device, device_id_type=MESH)

    for k in range(1, place.A):
        signal(place.at(lax.rem(place.a + k, place.A), place.b, place.c))
    for k in range(1, place.peers):
        signal(place.at_peer(place.other_peer(k)))
    signal(place.at(place.a, place.b, 1 - place.c))
    pl.semaphore_wait(barrier, place.A - 1 + place.peers - 1 + 1)


class Gather:
    RIGHT, LEFT, CORE, ACROSS = 0, 1, 2, 3

    def __init__(self, place, own, full, block, send_sem, recv_sem, local_sem):
        self.place, self.own, self.full, self.block = place, own, full, block
        self.send_sem, self.recv_sem, self.local_sem = send_sem, recv_sem, local_sem

    def copy(self, shard, route, source, a, b, c):
        return pltpu.make_async_remote_copy(
            src_ref=source, dst_ref=self.block(self.full, shard),
            send_sem=self.send_sem.at[shard, route], recv_sem=self.recv_sem.at[shard],
            device_id=self.place.at(a, b, c), device_id_type=MESH,
        )

    def onward(self, shard, source, right, left, across, act):
        p = self.place
        if right is not None:
            pl.when(right)(lambda: act(self.copy(shard, self.RIGHT, source, p.a + 1, p.b, p.c)))
        if left is not None:
            pl.when(left)(lambda: act(self.copy(shard, self.LEFT, source, p.a - 1, p.b, p.c)))
        if across:
            for j in range(p.B - 1):
                act(self.copy(shard, self.ACROSS + j, source, p.a, p.other_b(j), p.c))
        act(self.copy(shard, self.CORE, source, p.a, p.b, 1 - p.c))

    def local(self):
        return pltpu.make_async_copy(self.own, self.block(self.full, self.place.me), self.local_sem)

    def start(self):
        p = self.place
        self.local().start()
        self.onward(p.me, self.own, p.a < p.A - 1, p.a > 0, True, lambda copy: copy.start())

    def arrived(self, shard):
        p = self.place
        self.copy(shard, self.CORE, self.block(self.full, shard), p.a, p.b, 1 - p.c).wait_recv()

    def line_step(self, k):
        p = self.place

        def from_left():
            shard = p.index(p.a - k, p.b, p.c)
            self.arrived(shard)
            self.onward(shard, self.block(self.full, shard), p.a < p.A - 1, None, True, lambda copy: copy.start())

        def from_right():
            shard = p.index(p.a + k, p.b, p.c)
            self.arrived(shard)
            self.onward(shard, self.block(self.full, shard), None, p.a > 0, True, lambda copy: copy.start())

        pl.when(p.a - k >= 0)(from_left)
        pl.when(p.a + k < p.A)(from_right)

    def across_step(self, k):
        p = self.place

        def row(a):
            for j in range(p.B - 1):
                shard = p.index(a, p.other_b(j), p.c)
                self.arrived(shard)
                self.onward(shard, self.block(self.full, shard), None, None, False, lambda copy: copy.start())

        if k == 0:
            row(p.a)
        else:
            pl.when(p.a - k >= 0)(lambda: row(p.a - k))
            pl.when(p.a + k < p.A)(lambda: row(p.a + k))

    def finish_recv(self):
        p = self.place
        self.local().wait()
        for a in range(p.A):
            for b in range(p.B):
                self.arrived(p.index(a, b, 1 - p.c))

    def finish_send(self):
        p = self.place
        wait = lambda copy: copy.wait_send()
        self.onward(p.me, self.own, p.a < p.A - 1, p.a > 0, True, wait)
        for k in range(1, p.A):

            def from_left(k=k):
                shard = p.index(p.a - k, p.b, p.c)
                self.onward(shard, self.block(self.full, shard), p.a < p.A - 1, None, True, wait)

            def from_right(k=k):
                shard = p.index(p.a + k, p.b, p.c)
                self.onward(shard, self.block(self.full, shard), None, p.a > 0, True, wait)

            pl.when(p.a - k >= 0)(from_left)
            pl.when(p.a + k < p.A)(from_right)
        for a in range(p.A):
            for j in range(p.B - 1):
                shard = p.index(a, p.other_b(j), p.c)
                self.onward(shard, self.block(self.full, shard), None, None, False, wait)


class ExpertGather:
    RIGHT, LEFT, CORE, ACROSS = 0, 1, 2, 3

    def __init__(self, place, own, full, count, send_sem, recv_sem, local_sem):
        self.place, self.own, self.full, self.count = place, own, full, count
        self.send_sem, self.recv_sem, self.local_sem = send_sem, recv_sem, local_sem
        self.size = own.shape[1]
        self.depth = self.size * place.A * place.B * 2

    def block(self, el, shard):
        return self.full.at[pl.ds(pl.multiple_of(el * self.depth + shard * self.size, self.size), self.size), :]

    def mine(self, el):
        return self.own.at[self.place.b * self.count + el]

    def copy(self, el, shard, route, source, a, b, c):
        return pltpu.make_async_remote_copy(
            src_ref=source, dst_ref=self.block(el, shard),
            send_sem=self.send_sem.at[el, shard, route], recv_sem=self.recv_sem.at[el, shard],
            device_id=self.place.at(a, b, c), device_id_type=MESH,
        )

    def across(self, el):
        p = self.place
        out = []
        for j in range(p.B - 1):
            to = p.other_b(j)
            out.append(self.copy(el, p.me, self.ACROSS + j, self.own.at[to * self.count + el], p.a, to, p.c))
        return out

    def local(self, el):
        return pltpu.make_async_copy(self.mine(el), self.block(el, self.place.me), self.local_sem.at[el])

    def onward(self, el, shard, source, right, left, act):
        p = self.place
        if right:
            pl.when(p.a < p.A - 1)(lambda: act(self.copy(el, shard, self.RIGHT, source, p.a + 1, p.b, p.c)))
        if left:
            pl.when(p.a > 0)(lambda: act(self.copy(el, shard, self.LEFT, source, p.a - 1, p.b, p.c)))
        act(self.copy(el, shard, self.CORE, source, p.a, p.b, 1 - p.c))

    def arrived(self, el, shard):
        p = self.place
        self.copy(el, shard, self.CORE, self.block(el, shard), p.a, p.b, 1 - p.c).wait_recv()

    def start_across(self, el):
        for copy in self.across(el):
            copy.start()

    def start_own(self, el):
        self.local(el).start()
        self.onward(el, self.place.me, self.mine(el), True, True, lambda copy: copy.start())

    def across_step(self, el):
        p = self.place
        for j in range(p.B - 1):
            shard = p.index(p.a, p.other_b(j), p.c)
            self.arrived(el, shard)
            self.onward(el, shard, self.block(el, shard), True, True, lambda copy: copy.start())

    def line_step(self, el, k):
        p = self.place

        def row(a, right, left):
            for b in range(p.B):
                shard = p.index(a, b, p.c)
                self.arrived(el, shard)
                self.onward(el, shard, self.block(el, shard), right, left, lambda copy: copy.start())

        pl.when(p.a - k >= 0)(lambda: row(p.a - k, True, False))
        pl.when(p.a + k < p.A)(lambda: row(p.a + k, False, True))

    def core_wait(self, el):
        p = self.place
        self.local(el).wait()
        for a in range(p.A):
            for b in range(p.B):
                self.arrived(el, p.index(a, b, 1 - p.c))

    def finish(self, el):
        p = self.place
        wait = lambda copy: copy.wait_send()
        for copy in self.across(el):
            wait(copy)
        self.onward(el, p.me, self.mine(el), True, True, wait)
        for j in range(p.B - 1):
            shard = p.index(p.a, p.other_b(j), p.c)
            self.onward(el, shard, self.block(el, shard), True, True, wait)

        def row(a, right, left):
            for b in range(p.B):
                shard = p.index(a, b, p.c)
                self.onward(el, shard, self.block(el, shard), right, left, wait)

        for k in range(1, p.A):
            pl.when(p.a - k >= 0)(functools.partial(row, p.a - k, True, False))
            pl.when(p.a + k < p.A)(functools.partial(row, p.a + k, False, True))


class ExpertScatter:
    def __init__(self, place, part, sums, line, out, count, send, recv, local_sem):
        self.place, self.part, self.sums, self.line, self.out, self.count = place, part, sums, line, out, count
        self.send, self.recv, self.local_sem = send, recv, local_sem

    def remote(self, source, target, el, route, a, b, c):
        return pltpu.make_async_remote_copy(
            src_ref=source, dst_ref=target, send_sem=self.send.at[el, route], recv_sem=self.recv.at[el, route],
            device_id=self.place.at(a, b, c), device_id_type=MESH,
        )

    def core_copy(self, el):
        p = self.place
        return self.remote(self.part(el).at[:, :, 1 - p.c], self.sums.at[el], el, 0, p.a, p.b, 1 - p.c)

    def line_copies(self, el):
        p = self.place
        out = []
        for k in range(1, p.A):
            to, back = lax.rem(p.a + k, p.A), p.A - 1 - k
            out.append(self.remote(self.sums.at[el, to], self.line.at[el, back], el, 1 + back, to, p.b, p.c))
        return out

    def last_copies(self, el):
        p = self.place
        out = []
        for j in range(p.B - 1):
            to, back = p.other_b(j), p.B - 2 - j
            target = self.out.at[p.b * self.count + el]
            out.append(self.remote(self.sums.at[el, p.a, to], target, el, p.A + back, p.a, to, p.c))
        return out

    def local(self, el):
        p = self.place
        return pltpu.make_async_copy(self.sums.at[el, p.a, p.b], self.out.at[p.b * self.count + el], self.local_sem.at[el])

    def start(self, el):
        self.core_copy(el).start()

    def core_step(self, el):
        p = self.place
        self.core_copy(el).wait()
        part = self.part(el)

        @pl.loop(0, p.A * p.B)
        def _(i):
            a, b = lax.div(i, p.B), lax.rem(i, p.B)
            total = self.sums[el, a, b].astype(F32) + part[a, b, p.c].astype(F32)
            self.sums[el, a, b] = total.astype(BF16)

        for copy in self.line_copies(el):
            copy.start()

    def line_step(self, el):
        p = self.place
        for copy in self.line_copies(el):
            copy.wait_recv()

        @pl.loop(0, p.B)
        def _(b):
            total = self.sums[el, p.a, b].astype(F32)
            for k in range(p.A - 1):
                total += self.line[el, k, b].astype(F32)
            self.sums[el, p.a, b] = total.astype(BF16)

        for copy in self.last_copies(el) + [self.local(el)]:
            copy.start()

    def finish(self, el):
        for copy in self.line_copies(el):
            copy.wait_send()
        for copy in self.last_copies(el) + [self.local(el)]:
            copy.wait()


class Scatter:
    def __init__(self, place, part, sums, across, line, send, recv):
        self.place, self.part, self.sums, self.across, self.line = place, part, sums, across, line
        self.send, self.recv = send, recv

    def remote(self, source, target, item, route, a, b, c):
        return pltpu.make_async_remote_copy(
            src_ref=source, dst_ref=target, send_sem=self.send.at[item, route], recv_sem=self.recv.at[item, route],
            device_id=self.place.at(a, b, c), device_id_type=MESH,
        )

    def core_copy(self, item):
        p = self.place
        return self.remote(self.part(item).at[:, :, 1 - p.c], self.sums.at[item], item, 0, p.a, p.b, 1 - p.c)

    def across_copies(self, item):
        p = self.place
        out = []
        for j in range(p.B - 1):
            to, back = p.other_b(j), p.B - 2 - j
            copy = self.remote(self.sums.at[item, :, to], self.across.at[item, back], item, 1 + back, p.a, to, p.c)
            out.append(copy)
        return out

    def line_copies(self, item):
        p = self.place
        out = []
        for k in range(1, p.A):
            to, back = lax.rem(p.a + k, p.A), p.A - 1 - k
            copy = self.remote(self.sums.at[item, to, p.b], self.line.at[item, back], item, p.B + back, to, p.b, p.c)
            out.append(copy)
        return out

    def start(self, item):
        self.core_copy(item).start()

    def core_step(self, item):
        p = self.place
        self.core_copy(item).wait()
        part = self.part(item)

        @pl.loop(0, p.A * p.B)
        def _(i):
            a, b = lax.div(i, p.B), lax.rem(i, p.B)
            total = self.sums[item, a, b].astype(F32) + part[a, b, p.c].astype(F32)
            self.sums[item, a, b] = total.astype(BF16)

        for copy in self.across_copies(item):
            copy.start()

    def across_step(self, item):
        p = self.place
        for copy in self.across_copies(item):
            copy.wait_recv()

        @pl.loop(0, p.A)
        def _(a):
            total = self.sums[item, a, p.b].astype(F32)
            for j in range(p.B - 1):
                total += self.across[item, j, a].astype(F32)
            self.sums[item, a, p.b] = total.astype(BF16)

        for copy in self.line_copies(item):
            copy.start()

    def line_step(self, item):
        p = self.place
        for copy in self.line_copies(item):
            copy.wait_recv()
        total = self.sums[item, p.a, p.b].astype(F32)
        for k in range(p.A - 1):
            total += self.line[item, k].astype(F32)
        return total

    def finish(self, item):
        for copy in self.across_copies(item) + self.line_copies(item):
            copy.wait_send()


def block_kernel(
    experts, fsdp, xs, count,
    x_in, cot_in, meta_ref, meta_row_ref, shard_ref, up_in, down_in,
    out_out, input_grad_out, share_out, up_grad_out, down_grad_out,
    act_one_save, weights_save, attended_save, mid_save, act_two_save,
    x_ref, params_ref, triple_ref, probs_ref,
    sent_ref, cot_sent_ref, gate_sent_ref, rows_ref, grad_ref, gate_ref, back_ref, grad_slots_ref,
    up_ref, down_ref, part_up_ref, part_down_ref, float_ref,
    sums_up, sums_down, line_up, line_down, sums_par, across_par, line_par, swap_ref,
    bias_ref, gate_rows_ref, dot_row_ref, place_ref, gated_ref, logit_grad_ref, column_ref,
    load_sem, save_sem, late_sem, store_sem, par_gather_send, par_gather_recv, par_gather_local,
    gather_send, gather_recv, gather_local, swap_send, swap_recv, return_send, return_recv,
    scatter_send, scatter_recv, scatter_local, par_send, par_recv, share_send, share_recv,
):
    rows_pad, width = x_ref.shape
    groups = rows_pad // BLOCK
    places = sent_ref.shape[0]
    capacity = places // experts
    hidden_width = up_ref.shape[1]
    chunks = hidden_width // FF_CHUNK
    held = up_in.shape[0]
    place = Place(fsdp, xs)
    A, B, sources = place.A, place.B, place.peers
    expert_rows = sources * capacity
    row_block = float_ref.shape[0] // 2
    copy_in = pltpu.make_async_copy

    weights_ref = part_up_ref
    act_one, attended, act_two, cot_ref = (part_down_ref.at[pl.ds(i * rows_pad, rows_pad), :] for i in range(4))
    mid_ref = float_ref

    loads = [copy_in(x_in, x_ref, load_sem.at[0]), copy_in(cot_in, cot_ref, load_sem.at[1])]
    for copy in loads:
        copy.start()
    greet(place)

    def rows_block(ref, shard):
        size = shard_ref.shape[0]
        return ref.at[pl.ds(pl.multiple_of(shard * size, size), size), :]

    params = Gather(place, shard_ref, params_ref, rows_block, par_gather_send, par_gather_recv, par_gather_local)
    weights_in = [
        ExpertGather(place, own, full, count, gather_send.at[i], gather_recv.at[i], gather_local.at[i])
        for i, (own, full) in enumerate(((up_in, up_ref), (down_in, down_ref)))
    ]

    def each(step, el, *more):
        if el < count:
            for gather in weights_in:
                getattr(gather, step)(el, *more)

    params.start()
    for el in range(count):
        each("start_across", el)
    image_row = iota((BLOCK, BLOCK), 0) // PATCHES
    image_col = iota((BLOCK, BLOCK), 1) // PATCHES
    bias_ref[...] = jnp.where(image_row == image_col, 0.0, -1e30)

    def slot_rows(e):
        return pl.ds(pl.multiple_of(e * capacity, 16), capacity)

    def source_rows(el, source):
        return pl.ds(pl.multiple_of(el * expert_rows + source * capacity, 16), capacity)

    def find(e):
        slot = iota((capacity, rows_pad), 0) + e * capacity
        in_first = slot == meta_row_ref[0:1, :]
        in_second = slot == meta_row_ref[1:2, :]
        return in_first, in_second, jnp.where(jnp.logical_or(in_first, in_second), 1.0, 0.0).astype(BF16)

    def swap(kind, here, there, el, peer):
        return pltpu.make_async_remote_copy(
            src_ref=here.at[slot_rows(peer * count + el), :], dst_ref=there.at[source_rows(el, place.peer), :],
            send_sem=swap_send.at[kind, peer * count + el], recv_sem=swap_recv.at[kind, el, place.peer],
            device_id=place.at_peer(peer), device_id_type=MESH,
        )

    def swap_wait(kind, there, el):
        @pl.loop(1, sources)
        def _(k):
            source = place.other_peer(k)
            pltpu.make_async_remote_copy(
                src_ref=there.at[source_rows(el, source), :], dst_ref=there.at[source_rows(el, source), :],
                send_sem=swap_send.at[kind, 0], recv_sem=swap_recv.at[kind, el, source],
                device_id=place.at_peer(source), device_id_type=MESH,
            ).wait_recv()

    for copy in loads:
        copy.wait()
    for k in range(1, A):
        params.line_step(k)
        params.across_step(k - 1)

        @pl.loop((k - 1) * experts // (A - 1), k * experts // (A - 1))
        def _(e):
            _, _, picks = find(e)
            cot_sent_ref[slot_rows(e), :] = dot(picks, cot_ref[...]).astype(BF16)

    params.across_step(A - 1)
    each("start_own", 0)
    params.finish_recv()
    for el in range(count):

        @pl.loop(1, sources)
        def _(k):
            swap(2, cot_sent_ref, grad_ref, el, place.other_peer(k)).start()

        grad_ref[source_rows(el, place.peer), :] = cot_sent_ref[slot_rows(place.peer * count + el), :]

    small = params_ref[:, 4 * width :]
    small_rows = jnp.transpose(small.astype(F32))

    def saves(g):
        rows = rows_of(g)
        pairs = (
            (act_one, act_one_save), (weights_ref.at[:, pl.ds(0, HEADS * BLOCK)], weights_save), (attended, attended_save),
            (mid_ref, mid_save), (act_two, act_two_save),
        )
        return [
            copy_in(here.at[rows, :], there.at[rows, :], save_sem.at[i, g]) for i, (here, there) in enumerate(pairs)
        ]

    @pl.loop(0, groups)
    def _(g):
        rows = rows_of(g)
        x = x_ref[rows, :].astype(F32)
        normed, _ = normalize(x)
        act = (normed * small_rows[NORM_LANE : NORM_LANE + 1] + small_rows[NORM_LANE + 1 : NORM_LANE + 2]).astype(BF16)
        act_one[rows, :] = act
        triple_ref[rows, :] = dot(act, params_ref[:, : 3 * width]).astype(BF16)
        low = iota((BLOCK, LANES), 1) < HEAD_DIM
        for pair in range(HEADS // 2):
            at = pair * LANES
            q = triple_ref[rows, at : at + LANES] * HEAD_DIM ** (-0.5)
            k = triple_ref[rows, width + at : width + at + LANES]
            v = triple_ref[rows, 2 * width + at : 2 * width + at + LANES]
            total = None
            for half in range(2):
                mask = low if half == 0 else jnp.logical_not(low)
                scores = dot_against(jnp.where(mask, q, 0.0).astype(BF16), k) + bias_ref[...]
                top = jnp.max(scores, axis=-1, keepdims=True)
                raised = jnp.exp(scores - top)
                probs = raised / jnp.sum(raised, axis=-1, keepdims=True)
                probs = probs.astype(BF16)
                head = (2 * pair + half) * BLOCK
                weights_ref[rows, head : head + BLOCK] = probs
                part = dot(probs, jnp.where(mask, v, 0.0).astype(BF16))
                total = part if total is None else total + part
            attended[rows, at : at + LANES] = total.astype(BF16)

        @pl.when(g == 0)
        def _():
            each("across_step", 0)

        mid = x + dot(attended[rows, :], params_ref[:, 3 * width : 4 * width])
        mid_ref[rows, :] = mid
        normed, _ = normalize(mid)
        act = (normed * small_rows[NORM_LANE + 2 : NORM_LANE + 3] + small_rows[NORM_LANE + 3 : NORM_LANE + 4]).astype(BF16)
        act_two[rows, :] = act
        logits = jnp.where(iota((BLOCK, LANES), 1) < experts, dot(act, small), -1e30)
        raised = jnp.exp(logits - jnp.max(logits, axis=-1, keepdims=True))
        probs = raised / jnp.sum(raised, axis=-1, keepdims=True)
        probs_ref[rows, :] = probs
        first, second = gates_of(probs, meta_ref[rows, :])
        gate_rows_ref[0:1, rows] = to_row(first)
        gate_rows_ref[1:2, rows] = to_row(second)
        for copy in saves(g):
            copy.start()

        @pl.when(g == 1)
        def _():
            each("line_step", 0, 1)
            each("start_own", 1)
            each("across_step", 1)

        @pl.when(g == groups - 1)
        def _():
            each("line_step", 0, 2)

    @pl.loop(0, experts)
    def _(i):
        el, peer = lax.div(i, sources), place.other_peer(lax.rem(i, sources) + 1)
        e = peer * count + el
        in_first, in_second, picks = find(e)
        gate = jnp.sum(
            jnp.where(in_first, gate_rows_ref[0:1, :], jnp.where(in_second, gate_rows_ref[1:2, :], 0.0)),
            axis=1, keepdims=True,
        )
        sent_ref[slot_rows(e), :] = dot(picks, act_two[...]).astype(BF16)
        gate_sent_ref[slot_rows(e), :] = jnp.broadcast_to(gate, (capacity, LANES))

        @pl.when(peer != place.peer)
        def _():
            swap(0, sent_ref, rows_ref, el, peer).start()
            swap(1, gate_sent_ref, gate_ref, el, peer).start()

        @pl.when(peer == place.peer)
        def _():
            rows_ref[source_rows(el, peer), :] = sent_ref[slot_rows(e), :]
            gate_ref[source_rows(el, peer), :] = gate_sent_ref[slot_rows(e), :]

        @pl.when(i == experts // 2)
        def _():
            each("line_step", 1, 1)

    each("line_step", 0, 3)

    @pl.loop(0, groups)
    def _(g):
        for copy in saves(g):
            copy.wait()

    part_up = part_up_ref.at[pl.ds(0, count * width), :].reshape(count, A, B, 2, up_in.shape[1], part_up_ref.shape[1])
    part_down = part_down_ref.at[pl.ds(0, count * hidden_width), :].reshape(count, A, B, 2, down_in.shape[1], width)
    scatters = [
        ExpertScatter(place, part, sums, line, out, count, scatter_send.at[i], scatter_recv.at[i], scatter_local.at[i])
        for i, (part, sums, line, out) in enumerate(
            (
                (lambda el: part_up.at[el, :, :, :, :, pl.ds(0, hidden_width)], sums_up, line_up, up_grad_out),
                (lambda el: part_down.at[el], sums_down, line_down, down_grad_out),
            )
        )
    ]

    def all_scatters(step, el):
        for scatter in scatters:
            getattr(scatter, step)(el)

    par = Scatter(place, lambda e: part_up.at[0], sums_par, across_par, line_par, par_send, par_recv)

    def returned(kind, here, there, el, peer):
        return pltpu.make_async_remote_copy(
            src_ref=here.at[source_rows(el, peer), :], dst_ref=there.at[slot_rows(place.peer * count + el), :],
            send_sem=return_send.at[kind, el, peer], recv_sem=return_recv.at[kind, el, place.peer],
            device_id=place.at_peer(peer), device_id_type=MESH,
        )

    def return_wait(kind, there, el):
        @pl.loop(1, sources)
        def _(k):
            source = place.other_peer(k)
            target = there.at[slot_rows(source * count + el), :]
            pltpu.make_async_remote_copy(
                src_ref=target, dst_ref=target,
                send_sem=return_send.at[kind, 0, 0], recv_sem=return_recv.at[kind, el, source],
                device_id=place.at_peer(source), device_id_type=MESH,
            ).wait_recv()

    def expert(el):
        each("core_wait", el)
        for kind, there in enumerate((rows_ref, gate_ref, grad_ref)):
            swap_wait(kind, there, el)

        @pl.loop(0, sources)
        def _(source):
            at = source_rows(el, source)
            grad_ref[at, :] = (gate_ref[at, 0:1] * grad_ref[at, :].astype(F32)).astype(BF16)

        for begin in range(0, expert_rows, row_block):
            here = pl.ds(el * expert_rows + begin, row_block)
            float_ref[...] = jnp.zeros_like(float_ref)

            @pl.loop(0, chunks)
            def _(f):
                at = pl.ds(pl.multiple_of(f * FF_CHUNK, FF_CHUNK), FF_CHUNK)
                down_at = pl.ds(pl.multiple_of(el * hidden_width + f * FF_CHUNK, FF_CHUNK), FF_CHUNK)
                rows, grads = rows_ref[here, :], grad_ref[here, :]
                up_part, down_part = up_ref[el * width : (el + 1) * width, at], down_ref[down_at, :]
                hidden = dot(rows, up_part)
                spread = 0.5 * (1.0 + lax.erf(hidden * ROOT_HALF))
                active = (hidden * spread).astype(BF16)
                slope = spread + hidden * (DENSITY_SCALE * jnp.exp(-0.5 * hidden * hidden))
                float_ref[:row_block, :] += dot(active, down_part)
                grad_hidden = (dot_against(grads, down_part) * slope).astype(BF16)
                float_ref[row_block:, :] += dot_against(grad_hidden, up_part)
                size = up_in.shape[1]
                up_sum = dot_rows(rows, grad_hidden).reshape(A, B, 2, size, FF_CHUNK)
                if begin > 0:
                    up_sum += part_up[el, :, :, :, :, at].astype(F32)
                part_up[el, :, :, :, :, at] = up_sum.astype(BF16)
                down_sum = dot_rows(active, grads)
                at = pl.ds(pl.multiple_of(el * hidden_width + f * FF_CHUNK, FF_CHUNK), FF_CHUNK)
                if begin > 0:
                    down_sum += part_down_ref[at, :].astype(F32)
                part_down_ref[at, :] = down_sum.astype(BF16)
                if begin == 0 and el == 0:
                    pl.when(f == 1)(lambda: each("line_step", 1, 2))
                    pl.when(f == chunks // 2)(lambda: each("line_step", 1, 3))
                if begin == 0 and el > 0:
                    pl.when(f == 0)(lambda: all_scatters("core_step", el - 1))

            rows_ref[here, :] = float_ref[:row_block, :].astype(BF16)
            grad_ref[here, :] = float_ref[row_block:, :].astype(BF16)

        all_scatters("start", el)

        @pl.loop(1, sources)
        def _(k):
            peer = place.other_peer(k)
            returned(0, rows_ref, back_ref, el, peer).start()
            returned(1, grad_ref, grad_slots_ref, el, peer).start()

        own, target = source_rows(el, place.peer), slot_rows(place.peer * count + el)
        back_ref[target, :] = rows_ref[own, :]
        grad_slots_ref[target, :] = grad_ref[own, :]

    for el in range(count):
        expert(el)

    def late_loads():
        out = [copy_in(weights_save, up_ref.at[pl.ds(0, rows_pad), :], late_sem.at[0])]
        for i, array in enumerate((act_one_save, attended_save, act_two_save, cot_in)):
            out.append(copy_in(array, down_ref.at[pl.ds(i * rows_pad, rows_pad), :], late_sem.at[1 + i]))
        out.append(copy_in(mid_save, float_ref.at[pl.ds(0, rows_pad), :], late_sem.at[5]))
        return out

    for el in range(count):
        each("finish", el)
    for copy in late_loads():
        copy.start()
    act_one, attended, act_two, cot_ref = (down_ref.at[pl.ds(i * rows_pad, rows_pad), :] for i in range(4))
    weights_ref = up_ref
    input_grad_ref = float_ref
    all_scatters("core_step", count - 1)
    for copy in late_loads():
        copy.wait()
    for el in range(count):
        return_wait(0, back_ref, el)
    gain_one = small_rows[NORM_LANE : NORM_LANE + 1]
    gain_two = small_rows[NORM_LANE + 2 : NORM_LANE + 3]
    column_ref[...] = jnp.zeros_like(column_ref)

    @pl.loop(0, places // LANES)
    def _(c):
        at = pl.ds(pl.multiple_of(c * LANES, LANES), LANES)
        column = jnp.sum(back_ref[at, :].astype(F32) * cot_sent_ref[at, :].astype(F32), axis=1, keepdims=True)
        dot_row_ref[0:1, at] = to_row(column)

    for el in range(count):
        return_wait(1, grad_slots_ref, el)

    def stores(g):
        rows = rows_of(g)
        return (
            copy_in(cot_ref.at[rows, :], out_out.at[rows, :], store_sem.at[0, g]),
            copy_in(input_grad_ref.at[rows, :], input_grad_out.at[rows, :], store_sem.at[1, g]),
        )

    @pl.loop(0, groups)
    def _(g):
        rows = rows_of(g)
        meta = meta_ref[rows, :]
        probs = probs_ref[rows, :]
        gate_first, gate_second = gates_of(probs, meta)
        lane = iota((BLOCK, LANES), 1)
        grad_first = jnp.zeros((BLOCK, LANES), F32)
        grad_second = jnp.zeros((BLOCK, LANES), F32)
        for c in range(places // LANES):
            at = c * LANES
            in_first = lane == meta[:, 0:1] - at
            in_second = lane == meta[:, 1:2] - at
            place_ref[:, at : at + LANES] = jnp.where(jnp.logical_or(in_first, in_second), 1.0, 0.0).astype(BF16)
            gated_ref[:, at : at + LANES] = jnp.where(in_first, gate_first, jnp.where(in_second, gate_second, 0.0)).astype(BF16)
            dots = dot_row_ref[0:1, at : at + LANES]
            grad_first += jnp.where(in_first, dots, 0.0)
            grad_second += jnp.where(in_second, dots, 0.0)
        grad_first = jnp.sum(grad_first, axis=1, keepdims=True)
        grad_second = jnp.sum(grad_second, axis=1, keepdims=True)
        mid = input_grad_ref[rows, :]
        grad_probs = jnp.where(lane == meta[:, 2:3], grad_first, 0.0) + jnp.where(lane == meta[:, 3:4], grad_second, 0.0)
        grad_logits = (probs * (grad_probs - jnp.sum(grad_probs * probs, axis=-1, keepdims=True))).astype(BF16)
        logit_grad_ref[rows, :] = grad_logits
        grad_act = dot(place_ref[...], grad_slots_ref[...]) + dot_against(grad_logits, small)
        normed, inverse = normalize(mid)
        column_ref[NORM_LANE + 2 : NORM_LANE + 3, :] += jnp.sum(grad_act * normed, axis=0, keepdims=True)
        column_ref[NORM_LANE + 3 : NORM_LANE + 4, :] += jnp.sum(grad_act, axis=0, keepdims=True)
        grad_mid = cot_ref[rows, :].astype(F32) + denormalize(grad_act, normed, inverse, gain_two)
        cot_ref[rows, :] = (mid + dot(gated_ref[...], back_ref[...])).astype(BF16)
        input_grad_ref[rows, :] = grad_mid
        grad_attended = dot_against(grad_mid.astype(BF16), params_ref[:, 3 * width : 4 * width]).astype(BF16)
        low = lane < HEAD_DIM
        for pair in range(HEADS // 2):
            at = pair * LANES
            q = triple_ref[rows, at : at + LANES] * HEAD_DIM ** (-0.5)
            k = triple_ref[rows, width + at : width + at + LANES]
            v = triple_ref[rows, 2 * width + at : 2 * width + at + LANES]
            upstream = grad_attended[:, at : at + LANES]
            grad_q = grad_k = grad_v = jnp.zeros((BLOCK, LANES), F32)
            for half in range(2):
                mask = low if half == 0 else jnp.logical_not(low)
                upstream_half = jnp.where(mask, upstream, 0.0).astype(BF16)
                head = (2 * pair + half) * BLOCK
                weights = weights_ref[rows, head : head + BLOCK]
                kept = weights.astype(F32)
                grad_weights = dot_against(upstream_half, v)
                inner = jnp.sum(grad_weights * kept, axis=-1, keepdims=True)
                grad_scores = (kept * (grad_weights - inner)).astype(BF16)
                grad_q += dot(grad_scores, jnp.where(mask, k, 0.0).astype(BF16))
                grad_k += dot_rows(grad_scores, jnp.where(mask, q, 0.0).astype(BF16))
                grad_v += dot_rows(weights, upstream_half)
            triple_ref[rows, at : at + LANES] = (grad_q * HEAD_DIM ** (-0.5)).astype(BF16)
            triple_ref[rows, width + at : width + at + LANES] = grad_k.astype(BF16)
            triple_ref[rows, 2 * width + at : 2 * width + at + LANES] = grad_v.astype(BF16)
        grad_act = dot_against(triple_ref[rows, :], params_ref[:, : 3 * width])
        normed, inverse = normalize(x_ref[rows, :].astype(F32))
        column_ref[NORM_LANE : NORM_LANE + 1, :] += jnp.sum(grad_act * normed, axis=0, keepdims=True)
        column_ref[NORM_LANE + 1 : NORM_LANE + 2, :] += jnp.sum(grad_act, axis=0, keepdims=True)
        grad_mid = input_grad_ref[rows, :]
        x_ref[rows, :] = grad_mid.astype(BF16)
        input_grad_ref[rows, :] = grad_mid + denormalize(grad_act, normed, inverse, gain_one)
        for copy in stores(g):
            copy.start()
        pl.when(g == 1)(lambda: all_scatters("line_step", 0))

    size = up_in.shape[1]
    split = (A, B, 2, size)
    part_up[0, :, :, :, :, : 3 * width] = dot_rows(act_one[...], triple_ref[...]).astype(BF16).reshape(*split, 3 * width)
    part_up[0, :, :, :, :, 3 * width : 4 * width] = dot_rows(attended[...], x_ref[...]).astype(BF16).reshape(*split, width)
    small_part = dot_rows(act_two[...], logit_grad_ref[...]) + jnp.transpose(column_ref[...])
    part_up[0, :, :, :, :, 4 * width :] = small_part.astype(BF16).reshape(*split, LANES)
    par.start(0)
    par.core_step(0)
    par.across_step(0)
    for el in range(1, count):
        all_scatters("line_step", el)
    swap_ref[place.x] = par.line_step(0).astype(BF16)

    def shares():
        out = []
        for k in range(1, xs):
            to, back = lax.rem(place.x + k, xs), xs - 1 - k
            out.append(
                pltpu.make_async_remote_copy(
                    src_ref=swap_ref.at[place.x], dst_ref=swap_ref.at[place.x],
                    send_sem=share_send.at[back], recv_sem=share_recv.at[back],
                    device_id=(to, place.me), device_id_type=MESH,
                )
            )
        return out

    for copy in shares():
        copy.start()

    @pl.loop(0, groups)
    def _(g):
        for copy in stores(g):
            copy.wait()

    params.finish_send()
    for el in range(count):

        @pl.loop(1, sources)
        def _(k):
            peer = place.other_peer(k)
            swap(0, sent_ref, rows_ref, el, peer).wait_send()
            swap(1, gate_sent_ref, gate_ref, el, peer).wait_send()
            swap(2, cot_sent_ref, grad_ref, el, peer).wait_send()
            returned(0, rows_ref, back_ref, el, peer).wait_send()
            returned(1, grad_ref, grad_slots_ref, el, peer).wait_send()

        all_scatters("finish", el)
    par.finish(0)
    for copy in shares():
        copy.wait()
    total = swap_ref[0].astype(F32)
    for i in range(1, xs):
        total += swap_ref[i].astype(F32)
    share_out[...] = total


def on_device(
    inputs, cotangent, routes, slots, qkv_weight, out_weight, router_weight,
    norm1_gain, norm1_shift, norm2_gain, norm2_shift, expert_up, expert_down,
):
    rows_dev, width = inputs.shape
    groups = rows_dev // GROUP_ROWS
    rows_pad = groups * BLOCK
    fsdp = lax.axis_size("fsdp")
    peers = lax.axis_size("expert")
    held = expert_up.shape[0]
    experts = held * peers
    capacity = (42 * rows_dev + 20 * experts - 1) // (20 * experts)
    capacity = -(-capacity // 16) * 16
    places = experts * capacity

    def pad_rows(array, value=0):
        array = array.reshape(groups, GROUP_ROWS, array.shape[1])
        array = jnp.pad(array, ((0, 0), (0, BLOCK - GROUP_ROWS), (0, 0)), constant_values=value)
        return array.reshape(rows_pad, array.shape[2])

    def cut_rows(array):
        return array.reshape(groups, BLOCK, width)[:, :GROUP_ROWS].reshape(rows_dev, width)

    norms = jnp.stack([norm1_gain, norm1_shift, norm2_gain, norm2_shift], axis=1)
    shard = jnp.concatenate(
        [
            qkv_weight,
            out_weight,
            jnp.pad(router_weight, ((0, 0), (0, NORM_LANE - experts))),
            jnp.pad(norms, ((0, 0), (0, LANES - NORM_LANE - 4))),
        ],
        axis=1,
    )
    x = pad_rows(inputs)
    cot = pad_rows(cotangent)
    targets = jnp.where(slots >= 0, routes * capacity + slots, -1)
    meta = pad_rows(jnp.concatenate([targets, routes], axis=1), -1)
    meta_row = jnp.transpose(meta)

    vmem = pl.BlockSpec(memory_space=pltpu.VMEM)
    hbm = pl.BlockSpec(memory_space=pl.ANY)
    shape = jax.ShapeDtypeStruct
    dma = pltpu.SemaphoreType.DMA
    A, B = 4, fsdp // 8
    count = held // B
    sources = peers * B
    up_rows, down_rows = expert_up.shape[1], expert_down.shape[1]
    hidden_width = expert_up.shape[2]
    packed_width = shard.shape[1]
    expert_rows = sources * capacity
    row_block = max(n for n in range(16, MAX_ROWS + 1, 16) if expert_rows % n == 0)
    routes_of = 3 + B - 1

    def buffer(*dims, dtype=BF16):
        return pltpu.VMEM(dims, dtype)

    out, input_grad, share, up_grad, down_grad, *_ = pl.pallas_call(
        functools.partial(block_kernel, experts, fsdp, peers, count),
        out_shape=(
            shape((rows_pad, width), BF16),
            shape((rows_pad, width), F32),
            shape((up_rows, packed_width), F32),
            shape(expert_up.shape, BF16),
            shape(expert_down.shape, BF16),
            shape((rows_pad, width), BF16),
            shape((rows_pad, HEADS * BLOCK), BF16),
            shape((rows_pad, width), BF16),
            shape((rows_pad, width), F32),
            shape((rows_pad, width), BF16),
        ),
        in_specs=[hbm] * 2 + [vmem] * 3 + [hbm] * 2,
        out_specs=[hbm] * 2 + [vmem] + [hbm] * 7,
        scratch_shapes=[
            buffer(rows_pad, width), buffer(fsdp * up_rows, packed_width), buffer(rows_pad, 3 * width),
            buffer(rows_pad, LANES, dtype=F32),
            buffer(places, width), buffer(places, width), buffer(places, LANES, dtype=F32),
            buffer(places, width), buffer(places, width), buffer(places, LANES, dtype=F32),
            buffer(places, width), buffer(places, width),
            buffer(max(count * width, rows_pad), hidden_width), buffer(max(count * hidden_width, 4 * rows_pad), width),
            buffer(max(count * width, rows_pad), packed_width), buffer(max(count * hidden_width, 4 * rows_pad), width),
            buffer(max(2 * row_block, rows_pad), width, dtype=F32),
            buffer(count, A, B, up_rows, hidden_width), buffer(count, A, B, down_rows, width),
            buffer(count, A - 1, B, up_rows, hidden_width), buffer(count, A - 1, B, down_rows, width),
            buffer(1, A, B, up_rows, packed_width), buffer(1, B - 1, A, up_rows, packed_width),
            buffer(1, A - 1, up_rows, packed_width), buffer(peers, up_rows, packed_width),
            buffer(BLOCK, BLOCK, dtype=F32), buffer(8, rows_pad, dtype=F32), buffer(8, places, dtype=F32),
            buffer(BLOCK, places), buffer(BLOCK, places), buffer(rows_pad, LANES), buffer(LANES, width, dtype=F32),
            dma((2,)), dma((5, groups)), dma((6,)), dma((2, groups)),
            dma((fsdp, routes_of)), dma((fsdp,)), dma,
            dma((2, count, fsdp, routes_of)), dma((2, count, fsdp)), dma((2, count)),
            dma((3, experts)), dma((3, count, sources)), dma((2, count, sources)), dma((2, count, sources)),
            dma((2, count, A + B - 1)), dma((2, count, A + B - 1)), dma((2, count)),
            dma((1, A + B - 1)), dma((1, A + B - 1)), dma((peers - 1,)), dma((peers - 1,)),
        ],
        compiler_params=pltpu.CompilerParams(vmem_limit_bytes=VMEM_LIMIT, collective_id=0, has_side_effects=True),
        name="encoder_block",
    )(x, cot, meta, meta_row, shard, expert_up, expert_down)
    norm_share = share[:, 4 * width + NORM_LANE : 4 * width + NORM_LANE + 4]
    return (
        cut_rows(out),
        cut_rows(input_grad),
        share[:, : 3 * width],
        share[:, 3 * width : 4 * width],
        share[:, 4 * width : 4 * width + experts],
        norm_share[:, 0],
        norm_share[:, 1],
        norm_share[:, 2],
        norm_share[:, 3],
        up_grad.astype(F32),
        down_grad.astype(F32),
    )


def solution(mesh):
    tokens = P(("expert", "fsdp"), None)
    rows, vector, expert = P("fsdp", None), P("fsdp"), P("expert", "fsdp", None)
    return jax.shard_map(
        on_device,
        mesh=mesh,
        in_specs=(tokens,) * 4 + (rows,) * 3 + (vector,) * 4 + (expert,) * 2,
        out_specs=(tokens,) * 2 + (rows,) * 3 + (vector,) * 4 + (expert,) * 2,
        check_vma=False,
    )
```

time: 598 us -> 249 us (0.42)
  waiting for transfers between devices: 336 us -> 0 us
  Pallas kernels: 196 us -> 227 us
  local copies, waits for them, and re-layouts: 31.7 us -> 16.1 us
  between operations: 13.9 us -> 0.72 us
  starting transfers between devices: 9.01 us -> 0 us
    reduce_scatter x3 -> x0, waiting for transfers between devices: 270 us -> none  [the longest x1 107 us: on_device(): lax.psum_scatter(up_part, 'fsdp', scatter_dimension=1, tiled=True)]
    all_to_all x2 -> x0, waiting for transfers between devices: 47.1 us -> none  [the longest x1 24.7 us: on_device(): lax.all_to_all(grad_rows, 'expert', split_axis=1, concat_axis=0, tiled=True)]
    pallas_call x3 -> x1, Pallas kernels: 196 us -> 227 us  [on_device(): pl.pallas_call(functools.partial(block_kernel, experts, fsdp, peers, coun...]
    psum x1 -> x0, waiting for transfers between devices: 18.3 us -> none  [on_device(): share = lax.psum(share, 'expert').astype(F32)]
    pallas_call x2 -> x0, local copies, waits for them, and re-layouts: 9.46 us -> none  [on_device(): pl.pallas_call(expert_kernel, grid=(held,), out_shape=(shape((held, exper...]
    all_to_all x2 -> x0, starting transfers between devices: 8.85 us -> none  [the longest x1 4.89 us: on_device(): lax.all_to_all(grad_rows, 'expert', split_axis=1, concat_axis=0, tiled=True)]
  transfers between devices with their start and end apart: 6 -> 0, of which waited for: 6 -> 0; matrix products, arithmetic and copies ran while one was open for 3% -> 0% of each run, Pallas kernels for 0% -> 0%
where the time goes in v4:
time: 249 us; the launch traced here: 248 us
  Pallas kernels  227 us (91%)
  local copies, waits for them, and re-layouts  16.1 us (6%)
  other arithmetic  4.32 us (2%)
    pallas_call x1, Pallas kernels, on_device(): pl.pallas_call(functools.partial(block_kernel, experts, fsdp, peers, coun...  227 us

profile of v4, /device:TPU:28, one launch (start us, length us, event | category | flops | bytes accessed | tf_op | source)
XLA Modules:
  0.0 248.2 jit_solution(17955408567410535008)
XLA Ops:
  0.6 0.7 pad_maximum_fusion
  1.4 0.1 copy.39
  1.5 0.7 compare_select_fusion
  2.2 0.7 pad_add_fusion
  2.9 0.1 reshape.56
  3.0 0.0 copy-start.4
  3.0 0.8 copy.38
  3.8 1.6 concatenate.7.shard_ref
  5.5 1.0 copy.40.meta_ref
  6.5 0.0 copy-start
  6.5 1.6 reshape.52
  8.0 1.1 pad.19
  9.1 0.0 copy-done.4
  9.1 0.0 copy-done
  9.1 0.3 reshape.54
  9.4 1.1 pad.20
  10.5 227.0 %encoder_block.1 = (bf16[1024,512]{1,0:T(8,128)(2,1)}, f32[1024,512]{1,0:T(8,128)}, f32[32,2176]{1,0:T(8,128)}, bf16[4,32,2048]{2,1,0:T(8,128)(2,1)}, bf16[4,128...) custom-call(bf16[1024,512]{1,0:T(8,128)(2,1)} %bitcast.17, ...), custom_call_target="tpu_custom_call" | custom-call | tf_op jit(solution)/shard_map/encoder_block/pallas_call | solution.py:1002
  237.5 1.3 slice.41
  238.8 1.2 reshape.59
  240.0 1.7 slice.42
  241.8 0.0 copy-start.3
  241.8 0.0 copy-start.2
  241.8 1.5 reshape.61
  243.3 0.0 copy-done.3
  243.3 0.7 slice_reduce_fusion
  244.0 0.7 copy.41
  244.7 0.6 slice.35
  245.3 0.7 slice.34
  246.0 0.0 copy-done.2
  246.0 1.1 convert_element_type.13
  247.1 0.0 copy-done.1
  247.1 1.1 convert_element_type.14
  (6 shorter events, 0.0 us)
Async XLA Ops:
  3.0 6.1 %copy-start.4 = (s32[1,4,4,256]{3,1,2,0:T(4,128)}, s32[1,4,4,256]{3,1,2,0:T(4,128)S(1)}, u32[]{:S(2)}) copy-start(s32[1,4,4,256]{3,1,2,0:T(4,128)S(1)} %copy.42) | copy-start | bytes 49156
  6.5 2.6 %copy-start = (bf16[980,512]{1,0:T(8,128)(2,1)S(1)}, bf16[980,512]{1,0:T(8,128)(2,1)}, u32[]{:S(2)}) copy-start(bf16[980,512]{1,0:T(8,128)(2,1)} %param.14) | copy-start | bytes 3010564
  241.8 1.5 copy-start.3
  241.8 4.3 %copy-start.2 = (bf16[4,32,2048]{2,1,0:T(8,128)(2,1)S(1)}, bf16[4,32,2048]{2,1,0:T(8,128)(2,1)}, u32[]{:S(2)}) copy-start(bf16[4,32,2048]{2,1,0:T(8,128)(2,1)} %get-tuple-element.19) | copy-start | bytes 1572868
  243.3 3.8 %copy-start.1 = (bf16[4,128,512]{2,1,0:T(8,128)(2,1)S(1)}, bf16[4,128,512]{2,1,0:T(8,128)(2,1)}, u32[]{:S(2)}) copy-start(bf16[4,128,512]{2,1,0:T(8,128)(2,1)} %get-tuple-element.20) | copy-start | bytes 1572868

commit v5 on v4

--- a/solution.py
+++ b/solution.py
@@ -19,11 +19,32 @@
 GROUP_ROWS = GROUP_IMAGES * PATCHES
 LANES = 128
 NORM_LANE = 64
-FF_CHUNK = 256
-MAX_ROWS = 1088
+FF_CHUNK = 512
+MAX_ROWS = 640
 VMEM_LIMIT = 62 * 1024 * 1024
 
 MESH = pl.DeviceIdType.MESH
+PLAN = {
+    ("start", 0): [("across", 0)],
+    ("start", 1): [("own", 0)],
+    ("start", 3): [("passed", 0)],
+    ("begin", 0): [("relay", 0, 1, True), ("cots", 0)],
+    ("middle", 1): [("relay", 0, 1, False), ("relay", 0, 2, True)],
+    ("end", 1): [("across", 1)],
+    ("end", 2): [("own", 1)],
+    ("middle", 3): [("relay", 0, 2, False), ("relay", 0, 3, True)],
+    ("end", 3): [("passed", 1)],
+    ("dispatch", 7): [("relay", 0, 3, False), ("relay", 1, 1, True)],
+    ("before", 0, 0): [("rows", 1)],
+    ("expert", 0, 0): [("relay", 1, 1, False)],
+    ("expert", 0, 1): [("cots", 1), ("relay", 1, 2, True)],
+    ("expert", 0, 3): [("relay", 1, 2, False)],
+    ("expert", 0, 6): [("relay", 1, 3, True)],
+    ("expert", 0, 7): [("relay", 1, 3, False)],
+    ("expert", 1, 0): [("sums", 0), ("sum_relay", 0, 0)],
+    ("expert", 1, 4): [("outputs", 0)],
+    ("expert", 1, 5): [("sum_relay", 0, 1)],
+}
 F32 = jnp.float32
 BF16 = jnp.bfloat16
 
@@ -65,9 +86,15 @@
     n = column.shape[0]
     parts = []
     for at in range(0, n, LANES):
-        eye = iota((LANES, LANES), 0) == iota((LANES, LANES), 1)
-        parts.append(jnp.sum(jnp.where(eye, column[at : at + LANES], 0.0), axis=0, keepdims=True))
+        size = min(LANES, n - at)
+        eye = iota((size, LANES), 0) == iota((size, LANES), 1)
+        parts.append(jnp.sum(jnp.where(eye, column[at : at + size], 0.0), axis=0, keepdims=True))
     return parts[0] if len(parts) == 1 else jnp.concatenate(parts, axis=1)
+
+
+def to_column(row, n):
+    eye = iota((n, row.shape[1]), 0) == iota((n, row.shape[1]), 1)
+    return jnp.sum(jnp.where(eye, row, 0.0), axis=1, keepdims=True)
 
 
 def rows_of(g):
@@ -90,7 +117,7 @@
         line = lax.div(self.me, 2)
         self.b = lax.rem(line, self.B)
         self.a = lax.div(line, self.B)
-        self.peers = xs * self.B
+        self.xs, self.peers = xs, xs * self.B
         self.peer = self.x * self.B + self.b
 
     def index(self, a, b, c):
@@ -106,10 +133,15 @@
         return (lax.div(peer, self.B), self.index(self.a, lax.rem(peer, self.B), self.c))
 
     def other_peer(self, k):
-        return lax.rem(self.peer + k, self.peers)
-
-
-def greet(place):
+        x, b = lax.rem(self.x + lax.rem(k, self.xs), self.xs), lax.rem(self.b + lax.div(k, self.xs), self.B)
+        return x * self.B + b
+
+    def seen_from(self, k):
+        x, b = lax.rem(self.xs - lax.rem(k, self.xs), self.xs), lax.rem(self.B - lax.div(k, self.xs), self.B)
+        return b * self.xs + x
+
+
+def greet(place, meanwhile):
     barrier = pltpu.get_barrier_semaphore()
 
     def signal(device):
@@ -120,6 +152,7 @@
     for k in range(1, place.peers):
         signal(place.at_peer(place.other_peer(k)))
     signal(place.at(place.a, place.b, 1 - place.c))
+    meanwhile()
     pl.semaphore_wait(barrier, place.A - 1 + place.peers - 1 + 1)
 
 
@@ -280,11 +313,11 @@
             self.arrived(el, shard)
             self.onward(el, shard, self.block(el, shard), True, True, lambda copy: copy.start())
 
-    def line_step(self, el, k):
+    def line_step(self, el, k, own):
         p = self.place
 
         def row(a, right, left):
-            for b in range(p.B):
+            for b in [p.b] if own else [p.other_b(j) for j in range(p.B - 1)]:
                 shard = p.index(a, b, p.c)
                 self.arrived(el, shard)
                 self.onward(el, shard, self.block(el, shard), right, left, lambda copy: copy.start())
@@ -334,13 +367,44 @@
         p = self.place
         return self.remote(self.part(el).at[:, :, 1 - p.c], self.sums.at[el], el, 0, p.a, p.b, 1 - p.c)
 
-    def line_copies(self, el):
-        p = self.place
-        out = []
-        for k in range(1, p.A):
-            to, back = lax.rem(p.a + k, p.A), p.A - 1 - k
-            out.append(self.remote(self.sums.at[el, to], self.line.at[el, back], el, 1 + back, to, p.b, p.c))
-        return out
+    def right_copy(self, el, target):
+        p = self.place
+        return self.remote(self.sums.at[el, target], self.line.at[el, 0, target - 1], el, target, p.a + 1, p.b, p.c)
+
+    def left_copy(self, el, target):
+        p = self.place
+        return self.remote(self.sums.at[el, target], self.line.at[el, 1, target], el, p.A + target, p.a - 1, p.b, p.c)
+
+    def add(self, el, target, way, slot):
+        @pl.loop(0, self.place.B)
+        def _(b):
+            total = self.sums[el, target, b].astype(F32) + self.line[el, way, slot, b].astype(F32)
+            self.sums[el, target, b] = total.astype(BF16)
+
+    def relay_step(self, el, step):
+        p = self.place
+
+        @pl.when(p.a <= step)
+        def _():
+            target = p.a + p.A - 1 - step
+
+            @pl.when(p.a > 0)
+            def _():
+                self.right_copy(el, target).wait_recv()
+                self.add(el, target, 0, target - 1)
+
+            self.right_copy(el, target).start()
+
+        @pl.when(p.a >= p.A - 1 - step)
+        def _():
+            target = p.a - (p.A - 1 - step)
+
+            @pl.when(p.a < p.A - 1)
+            def _():
+                self.left_copy(el, target).wait_recv()
+                self.add(el, target, 1, target)
+
+            self.left_copy(el, target).start()
 
     def last_copies(self, el):
         p = self.place
@@ -348,7 +412,7 @@
         for j in range(p.B - 1):
             to, back = p.other_b(j), p.B - 2 - j
             target = self.out.at[p.b * self.count + el]
-            out.append(self.remote(self.sums.at[el, p.a, to], target, el, p.A + back, p.a, to, p.c))
+            out.append(self.remote(self.sums.at[el, p.a, to], target, el, 2 * p.A - 1 + back, p.a, to, p.c))
         return out
 
     def local(self, el):
@@ -369,27 +433,28 @@
             total = self.sums[el, a, b].astype(F32) + part[a, b, p.c].astype(F32)
             self.sums[el, a, b] = total.astype(BF16)
 
-        for copy in self.line_copies(el):
-            copy.start()
-
     def line_step(self, el):
         p = self.place
-        for copy in self.line_copies(el):
-            copy.wait_recv()
-
-        @pl.loop(0, p.B)
-        def _(b):
-            total = self.sums[el, p.a, b].astype(F32)
-            for k in range(p.A - 1):
-                total += self.line[el, k, b].astype(F32)
-            self.sums[el, p.a, b] = total.astype(BF16)
+
+        @pl.when(p.a > 0)
+        def _():
+            self.right_copy(el, p.a).wait_recv()
+            self.add(el, p.a, 0, p.a - 1)
+
+        @pl.when(p.a < p.A - 1)
+        def _():
+            self.left_copy(el, p.a).wait_recv()
+            self.add(el, p.a, 1, p.a)
 
         for copy in self.last_copies(el) + [self.local(el)]:
             copy.start()
 
     def finish(self, el):
-        for copy in self.line_copies(el):
-            copy.wait_send()
+        p = self.place
+        for target in range(1, p.A):
+            pl.when(p.a < target)(self.right_copy(el, target).wait_send)
+        for target in range(p.A - 1):
+            pl.when(p.a > target)(self.left_copy(el, target).wait_send)
         for copy in self.last_copies(el) + [self.local(el)]:
             copy.wait()
 
@@ -475,11 +540,12 @@
 
 def block_kernel(
     experts, fsdp, xs, count,
-    x_in, cot_in, meta_ref, meta_row_ref, shard_ref, up_in, down_in,
+    x_in, cot_in, routes_ref, slots_ref, qkv_ref, out_ref, router_ref, gain_one_ref, shift_one_ref, gain_two_ref, shift_two_ref,
+    up_in, down_in,
     out_out, input_grad_out, share_out, up_grad_out, down_grad_out,
     act_one_save, weights_save, attended_save, mid_save, act_two_save,
-    x_ref, params_ref, triple_ref, probs_ref,
-    sent_ref, cot_sent_ref, gate_sent_ref, rows_ref, grad_ref, gate_ref, back_ref, grad_slots_ref,
+    x_raw, cot_raw, shard_ref, meta_row_ref, meta_ref, x_ref, params_ref, triple_ref, probs_ref,
+    sent_ref, cot_sent_ref, gate_sent_ref, rows_ref, grad_ref, gate_ref, back_ref, grad_slots_ref, dots_sent_ref, dots_ref,
     up_ref, down_ref, part_up_ref, part_down_ref, float_ref,
     sums_up, sums_down, line_up, line_down, sums_par, across_par, line_par, swap_ref,
     bias_ref, gate_rows_ref, dot_row_ref, place_ref, gated_ref, logit_grad_ref, column_ref,
@@ -497,17 +563,37 @@
     place = Place(fsdp, xs)
     A, B, sources = place.A, place.B, place.peers
     expert_rows = sources * capacity
-    row_block = float_ref.shape[0] // 2
+    row_block = gated_ref.shape[0]
     copy_in = pltpu.make_async_copy
 
     weights_ref = part_up_ref
     act_one, attended, act_two, cot_ref = (part_down_ref.at[pl.ds(i * rows_pad, rows_pad), :] for i in range(4))
     mid_ref = float_ref
 
-    loads = [copy_in(x_in, x_ref, load_sem.at[0]), copy_in(cot_in, cot_ref, load_sem.at[1])]
+    loads = [copy_in(x_in, x_raw, load_sem.at[0]), copy_in(cot_in, cot_raw, load_sem.at[1])]
     for copy in loads:
         copy.start()
-    greet(place)
+
+    def spread(raw, there):
+        for g in range(groups):
+            there[g * BLOCK : g * BLOCK + GROUP_ROWS, :] = raw[g * GROUP_ROWS : (g + 1) * GROUP_ROWS, :]
+            there[g * BLOCK + GROUP_ROWS : (g + 1) * BLOCK, :] = jnp.zeros((BLOCK - GROUP_ROWS, width), BF16)
+
+    def prepare():
+        shard_ref[:, : 3 * width] = qkv_ref[...]
+        shard_ref[:, 3 * width : 4 * width] = out_ref[...]
+        size = shard_ref.shape[0]
+        eye = iota((size, size), 0) == iota((size, size), 1)
+        lane = iota((size, LANES), 1)
+        small = jnp.zeros((size, LANES), F32)
+        for i, norm_ref in enumerate((gain_one_ref, shift_one_ref, gain_two_ref, shift_two_ref)):
+            row = norm_ref[...].astype(F32).reshape(1, size)
+            column = jnp.sum(jnp.where(eye, row, 0.0), axis=1, keepdims=True)
+            small = jnp.where(lane == NORM_LANE + i, column, small)
+        shard_ref[:, 4 * width :] = small.astype(BF16)
+        shard_ref[:, 4 * width : 4 * width + experts] = jnp.transpose(router_ref[...].astype(F32)).astype(BF16)
+
+    greet(place, prepare)
 
     def rows_block(ref, shard):
         size = shard_ref.shape[0]
@@ -524,9 +610,31 @@
             for gather in weights_in:
                 getattr(gather, step)(el, *more)
 
+    def do(*point):
+        for name, el, *more in PLAN.get(point, ()):
+            if el < count:
+                with jax.named_scope("_".join(map(str, (name, el, *more)))):
+                    actions[name](el, *more)
+
+    actions = {
+        "across": lambda el: each("start_across", el),
+        "own": lambda el: each("start_own", el),
+        "passed": lambda el: each("across_step", el),
+        "relay": lambda *more: each("line_step", *more),
+        "cots": lambda el: cot_swaps(el),
+        "rows": lambda el: row_swaps(el),
+        "sums": lambda el: all_scatters("core_step", el),
+        "sum_relay": lambda el, step: all_scatters("relay_step", el, step),
+        "outputs": lambda el: give_back(2, el),
+    }
     params.start()
-    for el in range(count):
-        each("start_across", el)
+    do("start", 0)
+    targets = jnp.where(slots_ref[...] >= 0, routes_ref[...] * capacity + slots_ref[...], -1)
+    meta_row_ref[...] = jnp.full(meta_row_ref.shape, -1, jnp.int32)
+    for g in range(groups):
+        at = slice(g * BLOCK, g * BLOCK + GROUP_ROWS)
+        meta_row_ref[0:2, at] = targets[:, g * GROUP_ROWS : (g + 1) * GROUP_ROWS]
+        meta_row_ref[2:4, at] = routes_ref[:, g * GROUP_ROWS : (g + 1) * GROUP_ROWS]
     image_row = iota((BLOCK, BLOCK), 0) // PATCHES
     image_col = iota((BLOCK, BLOCK), 1) // PATCHES
     bias_ref[...] = jnp.where(image_row == image_col, 0.0, -1e30)
@@ -543,27 +651,48 @@
         in_second = slot == meta_row_ref[1:2, :]
         return in_first, in_second, jnp.where(jnp.logical_or(in_first, in_second), 1.0, 0.0).astype(BF16)
 
-    def swap(kind, here, there, el, peer):
+    def swap(kind, el, k):
+        peer, back = place.other_peer(k), place.seen_from(k)
+        e = peer * count + el
+        if kind == 1:
+            source, target = gate_sent_ref.at[e], gate_ref.at[el * sources + back]
+        else:
+            here, there = (sent_ref, rows_ref) if kind == 0 else (cot_sent_ref, grad_ref)
+            source, target = here.at[slot_rows(e), :], there.at[source_rows(el, back), :]
         return pltpu.make_async_remote_copy(
-            src_ref=here.at[slot_rows(peer * count + el), :], dst_ref=there.at[source_rows(el, place.peer), :],
-            send_sem=swap_send.at[kind, peer * count + el], recv_sem=swap_recv.at[kind, el, place.peer],
+            src_ref=source, dst_ref=target, send_sem=swap_send.at[kind, el, k], recv_sem=swap_recv.at[kind, el, back],
             device_id=place.at_peer(peer), device_id_type=MESH,
         )
 
-    def swap_wait(kind, there, el):
+    def swap_wait(kind, el, k):
+        if kind == 1:
+            target = gate_ref.at[el * sources + k]
+        else:
+            target = (rows_ref if kind == 0 else grad_ref).at[source_rows(el, k), :]
+        pltpu.make_async_remote_copy(
+            src_ref=target, dst_ref=target, send_sem=swap_send.at[kind, el, k], recv_sem=swap_recv.at[kind, el, k],
+            device_id=place.at_peer(place.other_peer(k)), device_id_type=MESH,
+        ).wait_recv()
+
+    def cot_swaps(el):
         @pl.loop(1, sources)
         def _(k):
-            source = place.other_peer(k)
-            pltpu.make_async_remote_copy(
-                src_ref=there.at[source_rows(el, source), :], dst_ref=there.at[source_rows(el, source), :],
-                send_sem=swap_send.at[kind, 0], recv_sem=swap_recv.at[kind, el, source],
-                device_id=place.at_peer(source), device_id_type=MESH,
-            ).wait_recv()
+            swap(2, el, k).start()
+
+        grad_ref[source_rows(el, 0), :] = cot_sent_ref[slot_rows(place.peer * count + el), :]
+
+    def row_swaps(el):
+        @pl.loop(1, sources)
+        def _(k):
+            swap(0, el, k).start()
+            swap(1, el, k).start()
 
     for copy in loads:
         copy.wait()
+    spread(cot_raw, cot_ref)
     for k in range(1, A):
         params.line_step(k)
+        do("start", k)
         params.across_step(k - 1)
 
         @pl.loop((k - 1) * experts // (A - 1), k * experts // (A - 1))
@@ -571,16 +700,13 @@
             _, _, picks = find(e)
             cot_sent_ref[slot_rows(e), :] = dot(picks, cot_ref[...]).astype(BF16)
 
+        if k == 1:
+            spread(x_raw, x_ref)
+            meta_ref[...] = jnp.transpose(meta_row_ref[...])
+
     params.across_step(A - 1)
-    each("start_own", 0)
     params.finish_recv()
-    for el in range(count):
-
-        @pl.loop(1, sources)
-        def _(k):
-            swap(2, cot_sent_ref, grad_ref, el, place.other_peer(k)).start()
-
-        grad_ref[source_rows(el, place.peer), :] = cot_sent_ref[slot_rows(place.peer * count + el), :]
+    do("begin", 0)
 
     small = params_ref[:, 4 * width :]
     small_rows = jnp.transpose(small.astype(F32))
@@ -623,9 +749,8 @@
                 total = part if total is None else total + part
             attended[rows, at : at + LANES] = total.astype(BF16)
 
-        @pl.when(g == 0)
-        def _():
-            each("across_step", 0)
+        for i in range(groups):
+            pl.when(g == i)(functools.partial(do, "middle", i))
 
         mid = x + dot(attended[rows, :], params_ref[:, 3 * width : 4 * width])
         mid_ref[rows, :] = mid
@@ -642,43 +767,33 @@
         for copy in saves(g):
             copy.start()
 
-        @pl.when(g == 1)
-        def _():
-            each("line_step", 0, 1)
-            each("start_own", 1)
-            each("across_step", 1)
-
-        @pl.when(g == groups - 1)
-        def _():
-            each("line_step", 0, 2)
+        for i in range(groups):
+            pl.when(g == i)(functools.partial(do, "end", i))
 
     @pl.loop(0, experts)
     def _(i):
-        el, peer = lax.div(i, sources), place.other_peer(lax.rem(i, sources) + 1)
-        e = peer * count + el
+        el, k = lax.div(i, sources), lax.rem(lax.rem(i, sources) + 1, sources)
+        e = place.other_peer(k) * count + el
         in_first, in_second, picks = find(e)
         gate = jnp.sum(
             jnp.where(in_first, gate_rows_ref[0:1, :], jnp.where(in_second, gate_rows_ref[1:2, :], 0.0)),
             axis=1, keepdims=True,
         )
         sent_ref[slot_rows(e), :] = dot(picks, act_two[...]).astype(BF16)
-        gate_sent_ref[slot_rows(e), :] = jnp.broadcast_to(gate, (capacity, LANES))
-
-        @pl.when(peer != place.peer)
+        gate_sent_ref[e, 0:1, :] = to_row(gate)
+
+        @pl.when(jnp.logical_and(el == 0, k > 0))
         def _():
-            swap(0, sent_ref, rows_ref, el, peer).start()
-            swap(1, gate_sent_ref, gate_ref, el, peer).start()
-
-        @pl.when(peer == place.peer)
+            swap(0, el, k).start()
+            swap(1, el, k).start()
+
+        @pl.when(k == 0)
         def _():
-            rows_ref[source_rows(el, peer), :] = sent_ref[slot_rows(e), :]
-            gate_ref[source_rows(el, peer), :] = gate_sent_ref[slot_rows(e), :]
-
-        @pl.when(i == experts // 2)
-        def _():
-            each("line_step", 1, 1)
-
-    each("line_step", 0, 3)
+            rows_ref[source_rows(el, 0), :] = sent_ref[slot_rows(e), :]
+            gate_ref[el * sources] = gate_sent_ref[e]
+
+        for at in range(8):
+            pl.when(i == at)(functools.partial(do, "dispatch", at))
 
     @pl.loop(0, groups)
     def _(g):
@@ -697,49 +812,67 @@
         )
     ]
 
-    def all_scatters(step, el):
+    def all_scatters(step, el, *more):
         for scatter in scatters:
-            getattr(scatter, step)(el)
+            getattr(scatter, step)(el, *more)
 
     par = Scatter(place, lambda e: part_up.at[0], sums_par, across_par, line_par, par_send, par_recv)
 
-    def returned(kind, here, there, el, peer):
+    def returned(kind, el, k):
+        e = place.peer * count + el
+        if kind == 1:
+            source, target = dots_sent_ref.at[el * sources + k], dots_ref.at[e]
+        else:
+            here, there = (grad_ref, grad_slots_ref) if kind == 0 else (rows_ref, back_ref)
+            source, target = here.at[source_rows(el, k), :], there.at[slot_rows(e), :]
         return pltpu.make_async_remote_copy(
-            src_ref=here.at[source_rows(el, peer), :], dst_ref=there.at[slot_rows(place.peer * count + el), :],
-            send_sem=return_send.at[kind, el, peer], recv_sem=return_recv.at[kind, el, place.peer],
-            device_id=place.at_peer(peer), device_id_type=MESH,
+            src_ref=source, dst_ref=target,
+            send_sem=return_send.at[kind, el, k], recv_sem=return_recv.at[kind, el, place.seen_from(k)],
+            device_id=place.at_peer(place.other_peer(k)), device_id_type=MESH,
         )
 
-    def return_wait(kind, there, el):
+    def give_back(kind, el, first=1, stop=sources):
+        @pl.loop(first, stop)
+        def _(k):
+            returned(kind, el, k).start()
+
+    def return_wait(kind, el):
         @pl.loop(1, sources)
         def _(k):
-            source = place.other_peer(k)
-            target = there.at[slot_rows(source * count + el), :]
+            e = place.other_peer(k) * count + el
+            target = dots_ref.at[e] if kind == 1 else (grad_slots_ref if kind == 0 else back_ref).at[slot_rows(e), :]
             pltpu.make_async_remote_copy(
-                src_ref=target, dst_ref=target,
-                send_sem=return_send.at[kind, 0, 0], recv_sem=return_recv.at[kind, el, source],
-                device_id=place.at_peer(source), device_id_type=MESH,
+                src_ref=target, dst_ref=target, send_sem=return_send.at[kind, el, k], recv_sem=return_recv.at[kind, el, k],
+                device_id=place.at_peer(place.other_peer(k)), device_id_type=MESH,
             ).wait_recv()
 
     def expert(el):
+        blocks = expert_rows // row_block
+        block_sources = row_block // capacity
+        order = list(range(blocks))
+        if el > 0 and el == count - 1:
+            order.reverse()
         each("core_wait", el)
-        for kind, there in enumerate((rows_ref, gate_ref, grad_ref)):
-            swap_wait(kind, there, el)
-
-        @pl.loop(0, sources)
-        def _(source):
-            at = source_rows(el, source)
-            grad_ref[at, :] = (gate_ref[at, 0:1] * grad_ref[at, :].astype(F32)).astype(BF16)
-
-        for begin in range(0, expert_rows, row_block):
-            here = pl.ds(el * expert_rows + begin, row_block)
-            float_ref[...] = jnp.zeros_like(float_ref)
+        for turn, block in enumerate(order):
+            first, stop = block * block_sources, (block + 1) * block_sources
+            for kind in range(3):
+                pl.loop(max(first, 1), stop)(functools.partial(swap_wait, kind, el))
+            do("before", el, turn)
+            here = pl.ds(el * expert_rows + block * row_block, row_block)
+            float_ref[: 2 * row_block, :] = jnp.zeros((2 * row_block, width), F32)
+
+            @pl.loop(first, stop)
+            def _(k):
+                gate = to_column(gate_ref[el * sources + k, 0:1, :], capacity)
+                cots = grad_ref[source_rows(el, k), :].astype(F32)
+                local = pl.ds(pl.multiple_of((k - first) * capacity, 16), capacity)
+                gated_ref[local, :] = (gate * cots).astype(BF16)
 
             @pl.loop(0, chunks)
             def _(f):
                 at = pl.ds(pl.multiple_of(f * FF_CHUNK, FF_CHUNK), FF_CHUNK)
                 down_at = pl.ds(pl.multiple_of(el * hidden_width + f * FF_CHUNK, FF_CHUNK), FF_CHUNK)
-                rows, grads = rows_ref[here, :], grad_ref[here, :]
+                rows, grads = rows_ref[here, :], gated_ref[...]
                 up_part, down_part = up_ref[el * width : (el + 1) * width, at], down_ref[down_at, :]
                 hidden = dot(rows, up_part)
                 spread = 0.5 * (1.0 + lax.erf(hidden * ROOT_HALF))
@@ -747,86 +880,96 @@
                 slope = spread + hidden * (DENSITY_SCALE * jnp.exp(-0.5 * hidden * hidden))
                 float_ref[:row_block, :] += dot(active, down_part)
                 grad_hidden = (dot_against(grads, down_part) * slope).astype(BF16)
-                float_ref[row_block:, :] += dot_against(grad_hidden, up_part)
+                float_ref[row_block : 2 * row_block, :] += dot_against(grad_hidden, up_part)
                 size = up_in.shape[1]
                 up_sum = dot_rows(rows, grad_hidden).reshape(A, B, 2, size, FF_CHUNK)
-                if begin > 0:
+                down_sum = dot_rows(active, grads)
+                if turn > 0:
                     up_sum += part_up[el, :, :, :, :, at].astype(F32)
+                    down_sum += part_down_ref[down_at, :].astype(F32)
                 part_up[el, :, :, :, :, at] = up_sum.astype(BF16)
-                down_sum = dot_rows(active, grads)
-                at = pl.ds(pl.multiple_of(el * hidden_width + f * FF_CHUNK, FF_CHUNK), FF_CHUNK)
-                if begin > 0:
-                    down_sum += part_down_ref[at, :].astype(F32)
-                part_down_ref[at, :] = down_sum.astype(BF16)
-                if begin == 0 and el == 0:
-                    pl.when(f == 1)(lambda: each("line_step", 1, 2))
-                    pl.when(f == chunks // 2)(lambda: each("line_step", 1, 3))
-                if begin == 0 and el > 0:
-                    pl.when(f == 0)(lambda: all_scatters("core_step", el - 1))
-
-            rows_ref[here, :] = float_ref[:row_block, :].astype(BF16)
-            grad_ref[here, :] = float_ref[row_block:, :].astype(BF16)
+                part_down_ref[down_at, :] = down_sum.astype(BF16)
+                for i in range(chunks):
+                    pl.when(f == i)(functools.partial(do, "expert", el, turn * chunks + i))
+
+            @pl.loop(first, stop)
+            def _(k):
+                at = source_rows(el, k)
+                local = pl.ds(pl.multiple_of((k - first) * capacity, 16), capacity)
+                back = float_ref[local, :].astype(BF16)
+                rows_ref[at, :] = back
+                dots = jnp.sum(back.astype(F32) * grad_ref[at, :].astype(F32), axis=1, keepdims=True)
+                dots_sent_ref[el * sources + k, 0:1, :] = to_row(dots)
+                local = pl.ds(pl.multiple_of(row_block + (k - first) * capacity, 16), capacity)
+                grad_ref[at, :] = float_ref[local, :].astype(BF16)
+
+            give_back(0, el, max(first, 1), stop)
+            give_back(1, el, max(first, 1), stop)
 
         all_scatters("start", el)
-
-        @pl.loop(1, sources)
-        def _(k):
-            peer = place.other_peer(k)
-            returned(0, rows_ref, back_ref, el, peer).start()
-            returned(1, grad_ref, grad_slots_ref, el, peer).start()
-
-        own, target = source_rows(el, place.peer), slot_rows(place.peer * count + el)
-        back_ref[target, :] = rows_ref[own, :]
-        grad_slots_ref[target, :] = grad_ref[own, :]
+        own, e = source_rows(el, 0), place.peer * count + el
+        back_ref[slot_rows(e), :] = rows_ref[own, :]
+        grad_slots_ref[slot_rows(e), :] = grad_ref[own, :]
+        dots_ref[e] = dots_sent_ref[el * sources]
 
     for el in range(count):
         expert(el)
 
     def late_loads():
         out = [copy_in(weights_save, up_ref.at[pl.ds(0, rows_pad), :], late_sem.at[0])]
-        for i, array in enumerate((act_one_save, attended_save, act_two_save, cot_in)):
+        for i, array in enumerate((act_one_save, attended_save, act_two_save)):
             out.append(copy_in(array, down_ref.at[pl.ds(i * rows_pad, rows_pad), :], late_sem.at[1 + i]))
-        out.append(copy_in(mid_save, float_ref.at[pl.ds(0, rows_pad), :], late_sem.at[5]))
+        for i in range(2):
+            out.append(copy_in(mid_save, float_ref.at[pl.ds(i * rows_pad, rows_pad), :], late_sem.at[4 + i]))
         return out
 
     for el in range(count):
         each("finish", el)
     for copy in late_loads():
         copy.start()
+    spread(cot_raw, down_ref.at[pl.ds(3 * rows_pad, rows_pad), :])
     act_one, attended, act_two, cot_ref = (down_ref.at[pl.ds(i * rows_pad, rows_pad), :] for i in range(4))
     weights_ref = up_ref
     input_grad_ref = float_ref
     all_scatters("core_step", count - 1)
+    if count > 1:
+        all_scatters("relay_step", count - 2, 2)
     for copy in late_loads():
         copy.wait()
-    for el in range(count):
-        return_wait(0, back_ref, el)
+    for kind in range(2):
+        for el in range(count):
+            return_wait(kind, el)
+    give_back(2, count - 1)
+    all_scatters("relay_step", count - 1, 0)
     gain_one = small_rows[NORM_LANE : NORM_LANE + 1]
     gain_two = small_rows[NORM_LANE + 2 : NORM_LANE + 3]
     column_ref[...] = jnp.zeros_like(column_ref)
-
-    @pl.loop(0, places // LANES)
-    def _(c):
-        at = pl.ds(pl.multiple_of(c * LANES, LANES), LANES)
-        column = jnp.sum(back_ref[at, :].astype(F32) * cot_sent_ref[at, :].astype(F32), axis=1, keepdims=True)
-        dot_row_ref[0:1, at] = to_row(column)
-
-    for el in range(count):
-        return_wait(1, grad_slots_ref, el)
-
-    def stores(g):
+    flat = jnp.zeros((8, places), F32)
+    for e in range(experts):
+        row = dots_ref[e]
+        row = jnp.concatenate([row, jnp.zeros((8, places - row.shape[1]), F32)], axis=1)
+        flat += pltpu.roll(row, e * capacity, 1) if e else row
+    dot_row_ref[...] = flat
+
+    def last_sums(g):
+        with jax.named_scope("last_sums_%d" % g):
+            if g == 0 and count > 1:
+                all_scatters("line_step", count - 2)
+            if g == 1:
+                all_scatters("relay_step", count - 1, 1)
+            if g == 3:
+                all_scatters("relay_step", count - 1, 2)
+
+    def store(i, g):
         rows = rows_of(g)
-        return (
-            copy_in(cot_ref.at[rows, :], out_out.at[rows, :], store_sem.at[0, g]),
-            copy_in(input_grad_ref.at[rows, :], input_grad_out.at[rows, :], store_sem.at[1, g]),
-        )
+        here, there = ((cot_ref, out_out), (input_grad_ref, input_grad_out))[i]
+        return copy_in(here.at[rows, :], there.at[rows, :], store_sem.at[i, g])
 
     @pl.loop(0, groups)
     def _(g):
         rows = rows_of(g)
         meta = meta_ref[rows, :]
         probs = probs_ref[rows, :]
-        gate_first, gate_second = gates_of(probs, meta)
         lane = iota((BLOCK, LANES), 1)
         grad_first = jnp.zeros((BLOCK, LANES), F32)
         grad_second = jnp.zeros((BLOCK, LANES), F32)
@@ -835,7 +978,6 @@
             in_first = lane == meta[:, 0:1] - at
             in_second = lane == meta[:, 1:2] - at
             place_ref[:, at : at + LANES] = jnp.where(jnp.logical_or(in_first, in_second), 1.0, 0.0).astype(BF16)
-            gated_ref[:, at : at + LANES] = jnp.where(in_first, gate_first, jnp.where(in_second, gate_second, 0.0)).astype(BF16)
             dots = dot_row_ref[0:1, at : at + LANES]
             grad_first += jnp.where(in_first, dots, 0.0)
             grad_second += jnp.where(in_second, dots, 0.0)
@@ -850,7 +992,6 @@
         column_ref[NORM_LANE + 2 : NORM_LANE + 3, :] += jnp.sum(grad_act * normed, axis=0, keepdims=True)
         column_ref[NORM_LANE + 3 : NORM_LANE + 4, :] += jnp.sum(grad_act, axis=0, keepdims=True)
         grad_mid = cot_ref[rows, :].astype(F32) + denormalize(grad_act, normed, inverse, gain_two)
-        cot_ref[rows, :] = (mid + dot(gated_ref[...], back_ref[...])).astype(BF16)
         input_grad_ref[rows, :] = grad_mid
         grad_attended = dot_against(grad_mid.astype(BF16), params_ref[:, 3 * width : 4 * width]).astype(BF16)
         low = lane < HEAD_DIM
@@ -883,9 +1024,9 @@
         grad_mid = input_grad_ref[rows, :]
         x_ref[rows, :] = grad_mid.astype(BF16)
         input_grad_ref[rows, :] = grad_mid + denormalize(grad_act, normed, inverse, gain_one)
-        for copy in stores(g):
-            copy.start()
-        pl.when(g == 1)(lambda: all_scatters("line_step", 0))
+        store(1, g).start()
+        for i in range(groups):
+            pl.when(g == i)(functools.partial(last_sums, i))
 
     size = up_in.shape[1]
     split = (A, B, 2, size)
@@ -894,10 +1035,28 @@
     small_part = dot_rows(act_two[...], logit_grad_ref[...]) + jnp.transpose(column_ref[...])
     part_up[0, :, :, :, :, 4 * width :] = small_part.astype(BF16).reshape(*split, LANES)
     par.start(0)
+    for el in range(count):
+        return_wait(2, el)
+
+    def combine(g):
+        rows = rows_of(g)
+        meta = meta_ref[rows, :]
+        gate_first, gate_second = gates_of(probs_ref[rows, :], meta)
+        lane = iota((BLOCK, LANES), 1)
+        for c in range(places // LANES):
+            at = c * LANES
+            in_first = lane == meta[:, 0:1] - at
+            in_second = lane == meta[:, 1:2] - at
+            place_ref[:, at : at + LANES] = jnp.where(in_first, gate_first, jnp.where(in_second, gate_second, 0.0)).astype(BF16)
+        mid = float_ref[pl.ds(pl.multiple_of(rows_pad + g * BLOCK, BLOCK), BLOCK), :]
+        cot_ref[rows, :] = (mid + dot(place_ref[...], back_ref[...])).astype(BF16)
+        store(0, g).start()
+
+    pl.loop(0, groups // 2)(combine)
     par.core_step(0)
+    pl.loop(groups // 2, groups)(combine)
     par.across_step(0)
-    for el in range(1, count):
-        all_scatters("line_step", el)
+    all_scatters("line_step", count - 1)
     swap_ref[place.x] = par.line_step(0).astype(BF16)
 
     def shares():
@@ -918,20 +1077,17 @@
 
     @pl.loop(0, groups)
     def _(g):
-        for copy in stores(g):
-            copy.wait()
+        for i in range(2):
+            store(i, g).wait()
 
     params.finish_send()
     for el in range(count):
 
         @pl.loop(1, sources)
         def _(k):
-            peer = place.other_peer(k)
-            swap(0, sent_ref, rows_ref, el, peer).wait_send()
-            swap(1, gate_sent_ref, gate_ref, el, peer).wait_send()
-            swap(2, cot_sent_ref, grad_ref, el, peer).wait_send()
-            returned(0, rows_ref, back_ref, el, peer).wait_send()
-            returned(1, grad_ref, grad_slots_ref, el, peer).wait_send()
+            for kind in range(3):
+                swap(kind, el, k).wait_send()
+                returned(kind, el, k).wait_send()
 
         all_scatters("finish", el)
     par.finish(0)
@@ -941,6 +1097,25 @@
     for i in range(1, xs):
         total += swap_ref[i].astype(F32)
     share_out[...] = total
+
+
+def finish_kernel(
+    experts, out_pad, input_grad_pad, share, up_half, down_half,
+    out, input_grad, qkv, out_weight, router, gain_one, shift_one, gain_two, shift_two, up, down,
+):
+    width = out.shape[1]
+    for g in range(out_pad.shape[0] // BLOCK):
+        here, there = slice(g * BLOCK, g * BLOCK + GROUP_ROWS), slice(g * GROUP_ROWS, (g + 1) * GROUP_ROWS)
+        out[there, :] = out_pad[here, :]
+        input_grad[there, :] = input_grad_pad[here, :]
+    qkv[...] = share[:, : 3 * width]
+    out_weight[...] = share[:, 3 * width : 4 * width]
+    small = jnp.transpose(share[:, 4 * width :])
+    router[...] = small[:experts, :]
+    for i, vector in enumerate((gain_one, shift_one, gain_two, shift_two)):
+        vector[...] = small[NORM_LANE + i : NORM_LANE + i + 1, :].reshape(vector.shape)
+    up[...] = up_half[...].astype(F32)
+    down[...] = down_half[...].astype(F32)
 
 
 def on_device(
@@ -958,30 +1133,6 @@
     capacity = -(-capacity // 16) * 16
     places = experts * capacity
 
-    def pad_rows(array, value=0):
-        array = array.reshape(groups, GROUP_ROWS, array.shape[1])
-        array = jnp.pad(array, ((0, 0), (0, BLOCK - GROUP_ROWS), (0, 0)), constant_values=value)
-        return array.reshape(rows_pad, array.shape[2])
-
-    def cut_rows(array):
-        return array.reshape(groups, BLOCK, width)[:, :GROUP_ROWS].reshape(rows_dev, width)
-
-    norms = jnp.stack([norm1_gain, norm1_shift, norm2_gain, norm2_shift], axis=1)
-    shard = jnp.concatenate(
-        [
-            qkv_weight,
-            out_weight,
-            jnp.pad(router_weight, ((0, 0), (0, NORM_LANE - experts))),
-            jnp.pad(norms, ((0, 0), (0, LANES - NORM_LANE - 4))),
-        ],
-        axis=1,
-    )
-    x = pad_rows(inputs)
-    cot = pad_rows(cotangent)
-    targets = jnp.where(slots >= 0, routes * capacity + slots, -1)
-    meta = pad_rows(jnp.concatenate([targets, routes], axis=1), -1)
-    meta_row = jnp.transpose(meta)
-
     vmem = pl.BlockSpec(memory_space=pltpu.VMEM)
     hbm = pl.BlockSpec(memory_space=pl.ANY)
     shape = jax.ShapeDtypeStruct
@@ -991,10 +1142,11 @@
     sources = peers * B
     up_rows, down_rows = expert_up.shape[1], expert_down.shape[1]
     hidden_width = expert_up.shape[2]
-    packed_width = shard.shape[1]
+    packed_width = 4 * width + LANES
     expert_rows = sources * capacity
-    row_block = max(n for n in range(16, MAX_ROWS + 1, 16) if expert_rows % n == 0)
+    row_block = max(n for n in range(capacity, MAX_ROWS + 1, capacity) if expert_rows % n == 0)
     routes_of = 3 + B - 1
+    lanes_of = -(-capacity // LANES) * LANES
 
     def buffer(*dims, dtype=BF16):
         return pltpu.VMEM(dims, dtype)
@@ -1013,47 +1165,58 @@
             shape((rows_pad, width), F32),
             shape((rows_pad, width), BF16),
         ),
-        in_specs=[hbm] * 2 + [vmem] * 3 + [hbm] * 2,
+        in_specs=[hbm] * 2 + [vmem] * 9 + [hbm] * 2,
         out_specs=[hbm] * 2 + [vmem] + [hbm] * 7,
         scratch_shapes=[
+            buffer(rows_dev, width), buffer(rows_dev, width), buffer(up_rows, packed_width),
+            buffer(8, rows_pad, dtype=jnp.int32), buffer(rows_pad, 8, dtype=jnp.int32),
             buffer(rows_pad, width), buffer(fsdp * up_rows, packed_width), buffer(rows_pad, 3 * width),
             buffer(rows_pad, LANES, dtype=F32),
-            buffer(places, width), buffer(places, width), buffer(places, LANES, dtype=F32),
-            buffer(places, width), buffer(places, width), buffer(places, LANES, dtype=F32),
+            buffer(places, width), buffer(places, width), buffer(experts, 8, lanes_of, dtype=F32),
+            buffer(places, width), buffer(places, width), buffer(experts, 8, lanes_of, dtype=F32),
             buffer(places, width), buffer(places, width),
+            buffer(experts, 8, lanes_of, dtype=F32), buffer(experts, 8, lanes_of, dtype=F32),
             buffer(max(count * width, rows_pad), hidden_width), buffer(max(count * hidden_width, 4 * rows_pad), width),
             buffer(max(count * width, rows_pad), packed_width), buffer(max(count * hidden_width, 4 * rows_pad), width),
-            buffer(max(2 * row_block, rows_pad), width, dtype=F32),
+            buffer(max(2 * row_block, 2 * rows_pad), width, dtype=F32),
             buffer(count, A, B, up_rows, hidden_width), buffer(count, A, B, down_rows, width),
-            buffer(count, A - 1, B, up_rows, hidden_width), buffer(count, A - 1, B, down_rows, width),
+            buffer(count, 2, A - 1, B, up_rows, hidden_width), buffer(count, 2, A - 1, B, down_rows, width),
             buffer(1, A, B, up_rows, packed_width), buffer(1, B - 1, A, up_rows, packed_width),
             buffer(1, A - 1, up_rows, packed_width), buffer(peers, up_rows, packed_width),
             buffer(BLOCK, BLOCK, dtype=F32), buffer(8, rows_pad, dtype=F32), buffer(8, places, dtype=F32),
-            buffer(BLOCK, places), buffer(BLOCK, places), buffer(rows_pad, LANES), buffer(LANES, width, dtype=F32),
+            buffer(BLOCK, places), buffer(row_block, width), buffer(rows_pad, LANES), buffer(LANES, width, dtype=F32),
             dma((2,)), dma((5, groups)), dma((6,)), dma((2, groups)),
             dma((fsdp, routes_of)), dma((fsdp,)), dma,
             dma((2, count, fsdp, routes_of)), dma((2, count, fsdp)), dma((2, count)),
-            dma((3, experts)), dma((3, count, sources)), dma((2, count, sources)), dma((2, count, sources)),
-            dma((2, count, A + B - 1)), dma((2, count, A + B - 1)), dma((2, count)),
+            dma((3, count, sources)), dma((3, count, sources)), dma((3, count, sources)), dma((3, count, sources)),
+            dma((2, count, 2 * A + B - 2)), dma((2, count, 2 * A + B - 2)), dma((2, count)),
             dma((1, A + B - 1)), dma((1, A + B - 1)), dma((peers - 1,)), dma((peers - 1,)),
         ],
         compiler_params=pltpu.CompilerParams(vmem_limit_bytes=VMEM_LIMIT, collective_id=0, has_side_effects=True),
         name="encoder_block",
-    )(x, cot, meta, meta_row, shard, expert_up, expert_down)
-    norm_share = share[:, 4 * width + NORM_LANE : 4 * width + NORM_LANE + 4]
-    return (
-        cut_rows(out),
-        cut_rows(input_grad),
-        share[:, : 3 * width],
-        share[:, 3 * width : 4 * width],
-        share[:, 4 * width : 4 * width + experts],
-        norm_share[:, 0],
-        norm_share[:, 1],
-        norm_share[:, 2],
-        norm_share[:, 3],
-        up_grad.astype(F32),
-        down_grad.astype(F32),
+    )(
+        inputs, cotangent, routes.T, slots.T, qkv_weight, out_weight, router_weight.T,
+        norm1_gain, norm1_shift, norm2_gain, norm2_shift, expert_up, expert_down,
     )
+    vector = shape((up_rows,), F32)
+    results = pl.pallas_call(
+        functools.partial(finish_kernel, experts),
+        out_shape=(
+            shape((rows_dev, width), BF16),
+            shape((rows_dev, width), F32),
+            shape((up_rows, 3 * width), F32),
+            shape((up_rows, width), F32),
+            shape((experts, up_rows), F32),
+            *[vector] * 4,
+            shape(expert_up.shape, F32),
+            shape(expert_down.shape, F32),
+        ),
+        in_specs=[vmem] * 5,
+        out_specs=[vmem] * 11,
+        compiler_params=pltpu.CompilerParams(vmem_limit_bytes=VMEM_LIMIT),
+        name="results",
+    )(out, input_grad, share, up_grad, down_grad)
+    return (*results[:4], results[4].T, *results[5:])
 
 
 def solution(mesh):

time: 249 us -> 199 us (0.80)
  Pallas kernels: 227 us -> 196 us
  local copies, waits for them, and re-layouts: 16.1 us -> 0 us
  other arithmetic: 4.32 us -> 0 us
    pallas_call x1, Pallas kernels: 227 us -> 191 us  [on_device(): pl.pallas_call(functools.partial(block_kernel, experts, fsdp, peers, coun...]
    reshape x6 -> x0, local copies, waits for them, and re-layouts: 5.68 us -> none  [the longest x2 2.74 us: cut_rows(): array.reshape(groups, BLOCK, width)[:, :GROUP_ROWS].reshape(rows_dev, width)]
    slice x6 -> x0, local copies, waits for them, and re-layouts: 5.08 us -> none  [the longest x2 3.02 us: cut_rows(): array.reshape(groups, BLOCK, width)[:, :GROUP_ROWS].reshape(rows_dev, width)]
    pallas_call x0 -> x1, Pallas kernels: none -> 4.78 us  [on_device(): pl.pallas_call(functools.partial(finish_kernel, experts), out_shape=(shap...]
where the time goes in v5:
time: 199 us; the launch traced here: 197 us
  Pallas kernels  196 us (98%)
    pallas_call x1, Pallas kernels, on_device(): pl.pallas_call(functools.partial(block_kernel, experts, fsdp, peers, coun...  191 us
    pallas_call x1, Pallas kernels, on_device(): pl.pallas_call(functools.partial(finish_kernel, experts), out_shape=(shap...  4.78 us

profile of v5, /device:TPU:28, one launch (start us, length us, event | category | flops | bytes accessed | tf_op | source)
XLA Modules:
  0.0 196.8 jit_solution(8429354391274072473)
XLA Ops:
  0.6 191.4 %encoder_block.1 = (bf16[1024,512]{1,0:T(8,128)(2,1)}, f32[1024,512]{1,0:T(8,128)}, f32[32,2176]{1,0:T(8,128)}, bf16[4,32,2048]{2,1,0:T(8,128)(2,1)}, bf16[4,128...) custom-call(bf16[980,512]{1,0:T(8,128)(2,1)} %x_in.1, ...), custom_call_target="tpu_custom_call" | custom-call | tf_op jit(solution)/shard_map/encoder_block/pallas_call | solution.py:1154
  192.1 4.8 %results.1 = (bf16[980,512]{1,0:T(8,128)(2,1)}, f32[980,512]{1,0:T(8,128)}, f32[32,1536]{1,0:T(8,128)}, f32[32,512]{1,0:T(8,128)}, f32[8,32]{1,0:T(8,128)}, /*in...) custom-call(bf16[1024,512]{1,0:T(8,128)(2,1)} %get-tuple-element.27., ...), custom_call_target="tpu_custom_call" | custom-call | tf_op jit(solution)/shard_map/results/pallas_call | solution.py:1202

commit v6 on v5

--- a/solution.py
+++ b/solution.py
@@ -21,29 +21,30 @@
 NORM_LANE = 64
 FF_CHUNK = 512
 MAX_ROWS = 640
-VMEM_LIMIT = 62 * 1024 * 1024
+VMEM_LIMIT = 63 * 1024 * 1024
 
 MESH = pl.DeviceIdType.MESH
 PLAN = {
     ("start", 0): [("across", 0)],
     ("start", 1): [("own", 0)],
     ("start", 3): [("passed", 0)],
-    ("begin", 0): [("relay", 0, 1, True), ("cots", 0)],
-    ("middle", 1): [("relay", 0, 1, False), ("relay", 0, 2, True)],
+    ("after", 3): [("relay", 0, 1, True)],
+    ("begin", 0): [("cots", 0)],
+    ("end", 0): [("relay", 0, 1, False)],
+    ("middle", 1): [("relay", 0, 2, True)],
     ("end", 1): [("across", 1)],
-    ("end", 2): [("own", 1)],
-    ("middle", 3): [("relay", 0, 2, False), ("relay", 0, 3, True)],
-    ("end", 3): [("passed", 1)],
-    ("dispatch", 7): [("relay", 0, 3, False), ("relay", 1, 1, True)],
-    ("before", 0, 0): [("rows", 1)],
-    ("expert", 0, 0): [("relay", 1, 1, False)],
-    ("expert", 0, 1): [("cots", 1), ("relay", 1, 2, True)],
-    ("expert", 0, 3): [("relay", 1, 2, False)],
-    ("expert", 0, 6): [("relay", 1, 3, True)],
-    ("expert", 0, 7): [("relay", 1, 3, False)],
+    ("end", 2): [("relay", 0, 2, False), ("cots_across", 1)],
+    ("dispatch", 7): [("own", 1), ("passed", 1), ("ends", 0)],
+    ("expert", 0, 0): [("relay", 1, 1, True)],
+    ("expert", 0, 1): [("rows", 1), ("relay", 1, 1, False)],
+    ("expert", 0, 3): [("cots_along", 1), ("relay", 1, 2, True)],
+    ("expert", 0, 4): [("relay", 1, 2, False)],
+    ("expert", 0, 7): [("ends", 1)],
     ("expert", 1, 0): [("sums", 0), ("sum_relay", 0, 0)],
-    ("expert", 1, 4): [("outputs", 0)],
-    ("expert", 1, 5): [("sum_relay", 0, 1)],
+    ("expert", 1, 4): [("sum_relay", 0, 1)],
+    ("after_expert", 1): [("outputs_across", 0)],
+    ("returned", 0): [("outputs_along", 0)],
+    ("returned", 1): [("outputs", 1)],
 }
 F32 = jnp.float32
 BF16 = jnp.bfloat16
@@ -166,8 +167,20 @@
     def copy(self, shard, route, source, a, b, c):
         return pltpu.make_async_remote_copy(
             src_ref=source, dst_ref=self.block(self.full, shard),
-            send_sem=self.send_sem.at[shard, route], recv_sem=self.recv_sem.at[shard],
+            send_sem=self.send_sem.at[route], recv_sem=self.recv_sem.at[self.arrival(shard, route)],
             device_id=self.place.at(a, b, c), device_id_type=MESH,
+        )
+
+    def arrival(self, shard, route):
+        return self.place.A * self.place.B if route == self.CORE else lax.div(shard, 2)
+
+    def some(self, route, blocks):
+        size = self.own.shape[0]
+        ref = self.full.at[pl.ds(0, blocks * size), :]
+        p = self.place
+        return pltpu.make_async_remote_copy(
+            src_ref=ref, dst_ref=ref, send_sem=self.send_sem.at[route], recv_sem=self.recv_sem.at[p.A * p.B],
+            device_id=p.at(p.a, p.b, 1 - p.c), device_id_type=MESH,
         )
 
     def onward(self, shard, source, right, left, across, act):
@@ -191,7 +204,7 @@
 
     def arrived(self, shard):
         p = self.place
-        self.copy(shard, self.CORE, self.block(self.full, shard), p.a, p.b, 1 - p.c).wait_recv()
+        self.copy(shard, self.RIGHT, self.block(self.full, shard), p.a, p.b, 1 - p.c).wait_recv()
 
     def line_step(self, k):
         p = self.place
@@ -227,30 +240,16 @@
     def finish_recv(self):
         p = self.place
         self.local().wait()
-        for a in range(p.A):
-            for b in range(p.B):
-                self.arrived(p.index(a, b, 1 - p.c))
+        self.some(self.CORE, p.A * p.B).wait_recv()
 
     def finish_send(self):
         p = self.place
-        wait = lambda copy: copy.wait_send()
-        self.onward(p.me, self.own, p.a < p.A - 1, p.a > 0, True, wait)
-        for k in range(1, p.A):
-
-            def from_left(k=k):
-                shard = p.index(p.a - k, p.b, p.c)
-                self.onward(shard, self.block(self.full, shard), p.a < p.A - 1, None, True, wait)
-
-            def from_right(k=k):
-                shard = p.index(p.a + k, p.b, p.c)
-                self.onward(shard, self.block(self.full, shard), None, p.a > 0, True, wait)
-
-            pl.when(p.a - k >= 0)(from_left)
-            pl.when(p.a + k < p.A)(from_right)
-        for a in range(p.A):
-            for j in range(p.B - 1):
-                shard = p.index(a, p.other_b(j), p.c)
-                self.onward(shard, self.block(self.full, shard), None, None, False, wait)
+        for a in range(p.A - 1):
+            pl.when(p.a == a)(self.some(self.RIGHT, a + 1).wait_send)
+            pl.when(p.a == a + 1)(self.some(self.LEFT, p.A - 1 - a).wait_send)
+        for j in range(p.B - 1):
+            self.some(self.ACROSS + j, p.A).wait_send()
+        self.some(self.CORE, p.A * p.B).wait_send()
 
 
 class ExpertGather:
@@ -271,8 +270,19 @@
     def copy(self, el, shard, route, source, a, b, c):
         return pltpu.make_async_remote_copy(
             src_ref=source, dst_ref=self.block(el, shard),
-            send_sem=self.send_sem.at[el, shard, route], recv_sem=self.recv_sem.at[el, shard],
+            send_sem=self.send_sem.at[el, route], recv_sem=self.recv_sem.at[el, self.arrival(shard, route)],
             device_id=self.place.at(a, b, c), device_id_type=MESH,
+        )
+
+    def arrival(self, shard, route):
+        return self.place.A * self.place.B if route == self.CORE else lax.div(shard, 2)
+
+    def some(self, el, route, blocks):
+        ref = self.full.at[pl.ds(el * self.depth, blocks * self.size), :]
+        p = self.place
+        return pltpu.make_async_remote_copy(
+            src_ref=ref, dst_ref=ref, send_sem=self.send_sem.at[el, route], recv_sem=self.recv_sem.at[el, p.A * p.B],
+            device_id=p.at(p.a, p.b, 1 - p.c), device_id_type=MESH,
         )
 
     def across(self, el):
@@ -296,7 +306,7 @@
 
     def arrived(self, el, shard):
         p = self.place
-        self.copy(el, shard, self.CORE, self.block(el, shard), p.a, p.b, 1 - p.c).wait_recv()
+        self.copy(el, shard, self.RIGHT, self.block(el, shard), p.a, p.b, 1 - p.c).wait_recv()
 
     def start_across(self, el):
         for copy in self.across(el):
@@ -328,28 +338,16 @@
     def core_wait(self, el):
         p = self.place
         self.local(el).wait()
-        for a in range(p.A):
-            for b in range(p.B):
-                self.arrived(el, p.index(a, b, 1 - p.c))
+        self.some(el, self.CORE, p.A * p.B).wait_recv()
 
     def finish(self, el):
         p = self.place
-        wait = lambda copy: copy.wait_send()
         for copy in self.across(el):
-            wait(copy)
-        self.onward(el, p.me, self.mine(el), True, True, wait)
-        for j in range(p.B - 1):
-            shard = p.index(p.a, p.other_b(j), p.c)
-            self.onward(el, shard, self.block(el, shard), True, True, wait)
-
-        def row(a, right, left):
-            for b in range(p.B):
-                shard = p.index(a, b, p.c)
-                self.onward(el, shard, self.block(el, shard), right, left, wait)
-
-        for k in range(1, p.A):
-            pl.when(p.a - k >= 0)(functools.partial(row, p.a - k, True, False))
-            pl.when(p.a + k < p.A)(functools.partial(row, p.a + k, False, True))
+            copy.wait_send()
+        for a in range(p.A - 1):
+            pl.when(p.a == a)(self.some(el, self.RIGHT, (a + 1) * p.B).wait_send)
+            pl.when(p.a == a + 1)(self.some(el, self.LEFT, (p.A - 1 - a) * p.B).wait_send)
+        self.some(el, self.CORE, p.A * p.B).wait_send()
 
 
 class ExpertScatter:
@@ -357,23 +355,29 @@
         self.place, self.part, self.sums, self.line, self.out, self.count = place, part, sums, line, out, count
         self.send, self.recv, self.local_sem = send, recv, local_sem
 
-    def remote(self, source, target, el, route, a, b, c):
+    CORE, RIGHT, LEFT, LAST = 0, 1, 2, 3
+
+    def remote(self, source, target, el, route, arrival, a, b, c):
         return pltpu.make_async_remote_copy(
-            src_ref=source, dst_ref=target, send_sem=self.send.at[el, route], recv_sem=self.recv.at[el, route],
+            src_ref=source, dst_ref=target, send_sem=self.send.at[el, route], recv_sem=self.recv.at[el, arrival],
             device_id=self.place.at(a, b, c), device_id_type=MESH,
         )
 
     def core_copy(self, el):
         p = self.place
-        return self.remote(self.part(el).at[:, :, 1 - p.c], self.sums.at[el], el, 0, p.a, p.b, 1 - p.c)
+        return self.remote(self.part(el).at[:, :, 1 - p.c], self.sums.at[el], el, self.CORE, 0, p.a, p.b, 1 - p.c)
 
     def right_copy(self, el, target):
         p = self.place
-        return self.remote(self.sums.at[el, target], self.line.at[el, 0, target - 1], el, target, p.a + 1, p.b, p.c)
+        return self.remote(
+            self.sums.at[el, target], self.line.at[el, 0, target - 1], el, self.RIGHT, target, p.a + 1, p.b, p.c
+        )
 
     def left_copy(self, el, target):
         p = self.place
-        return self.remote(self.sums.at[el, target], self.line.at[el, 1, target], el, p.A + target, p.a - 1, p.b, p.c)
+        return self.remote(
+            self.sums.at[el, target], self.line.at[el, 1, target], el, self.LEFT, p.A + target, p.a - 1, p.b, p.c
+        )
 
     def add(self, el, target, way, slot):
         @pl.loop(0, self.place.B)
@@ -412,7 +416,7 @@
         for j in range(p.B - 1):
             to, back = p.other_b(j), p.B - 2 - j
             target = self.out.at[p.b * self.count + el]
-            out.append(self.remote(self.sums.at[el, p.a, to], target, el, 2 * p.A - 1 + back, p.a, to, p.c))
+            out.append(self.remote(self.sums.at[el, p.a, to], target, el, self.LAST + j, 2 * p.A - 1 + back, p.a, to, p.c))
         return out
 
     def local(self, el):
@@ -451,44 +455,51 @@
 
     def finish(self, el):
         p = self.place
-        for target in range(1, p.A):
-            pl.when(p.a < target)(self.right_copy(el, target).wait_send)
-        for target in range(p.A - 1):
-            pl.when(p.a > target)(self.left_copy(el, target).wait_send)
+        for a in range(p.A - 1):
+            for route, at, count in ((self.RIGHT, a, p.A - 1 - a), (self.LEFT, a + 1, a + 1)):
+                some = self.sums.at[el, pl.ds(0, count)]
+                pl.when(p.a == at)(self.remote(some, some, el, route, 0, p.a, p.b, 1 - p.c).wait_send)
         for copy in self.last_copies(el) + [self.local(el)]:
             copy.wait()
 
 
 class Scatter:
-    def __init__(self, place, part, sums, across, line, send, recv):
+    def __init__(self, place, part, sums, across, line, columns, send, recv):
         self.place, self.part, self.sums, self.across, self.line = place, part, sums, across, line
-        self.send, self.recv = send, recv
+        self.columns, self.send, self.recv = columns, send, recv
+
+    CORE, ACROSS, LINE = 0, 1, 2
 
     def remote(self, source, target, item, route, a, b, c):
         return pltpu.make_async_remote_copy(
-            src_ref=source, dst_ref=target, send_sem=self.send.at[item, route], recv_sem=self.recv.at[item, route],
+            src_ref=source, dst_ref=target,
+            send_sem=self.send.at[item, min(route, 1)], recv_sem=self.recv.at[item, route],
             device_id=self.place.at(a, b, c), device_id_type=MESH,
         )
 
+    def all_of(self, ref, item, route):
+        p = self.place
+        return self.remote(ref, ref, item, route, p.a, p.b, 1 - p.c)
+
     def core_copy(self, item):
-        p = self.place
-        return self.remote(self.part(item).at[:, :, 1 - p.c], self.sums.at[item], item, 0, p.a, p.b, 1 - p.c)
+        p, at = self.place, self.columns[item]
+        return self.remote(self.part.at[:, :, 1 - p.c, :, at], self.sums.at[:, :, :, at], item, self.CORE, p.a, p.b, 1 - p.c)
 
     def across_copies(self, item):
-        p = self.place
+        p, at = self.place, self.columns[item]
         out = []
         for j in range(p.B - 1):
             to, back = p.other_b(j), p.B - 2 - j
-            copy = self.remote(self.sums.at[item, :, to], self.across.at[item, back], item, 1 + back, p.a, to, p.c)
+            copy = self.remote(self.sums.at[:, to, :, at], self.across.at[back, :, :, at], item, self.ACROSS, p.a, to, p.c)
             out.append(copy)
         return out
 
     def line_copies(self, item):
-        p = self.place
+        p, at = self.place, self.columns[item]
         out = []
         for k in range(1, p.A):
             to, back = lax.rem(p.a + k, p.A), p.A - 1 - k
-            copy = self.remote(self.sums.at[item, to, p.b], self.line.at[item, back], item, p.B + back, to, p.b, p.c)
+            copy = self.remote(self.sums.at[to, p.b, :, at], self.line.at[back, :, at], item, self.LINE, to, p.b, p.c)
             out.append(copy)
         return out
 
@@ -496,46 +507,44 @@
         self.core_copy(item).start()
 
     def core_step(self, item):
-        p = self.place
+        p, at = self.place, self.columns[item]
         self.core_copy(item).wait()
-        part = self.part(item)
 
         @pl.loop(0, p.A * p.B)
         def _(i):
             a, b = lax.div(i, p.B), lax.rem(i, p.B)
-            total = self.sums[item, a, b].astype(F32) + part[a, b, p.c].astype(F32)
-            self.sums[item, a, b] = total.astype(BF16)
+            total = self.sums[a, b, :, at].astype(F32) + self.part[a, b, p.c, :, at].astype(F32)
+            self.sums[a, b, :, at] = total.astype(BF16)
 
         for copy in self.across_copies(item):
             copy.start()
 
     def across_step(self, item):
-        p = self.place
-        for copy in self.across_copies(item):
-            copy.wait_recv()
+        p, at = self.place, self.columns[item]
+        self.all_of(self.across.at[:, :, :, at], item, self.ACROSS).wait_recv()
 
         @pl.loop(0, p.A)
         def _(a):
-            total = self.sums[item, a, p.b].astype(F32)
+            total = self.sums[a, p.b, :, at].astype(F32)
             for j in range(p.B - 1):
-                total += self.across[item, j, a].astype(F32)
-            self.sums[item, a, p.b] = total.astype(BF16)
+                total += self.across[j, a, :, at].astype(F32)
+            self.sums[a, p.b, :, at] = total.astype(BF16)
 
         for copy in self.line_copies(item):
             copy.start()
 
     def line_step(self, item):
-        p = self.place
-        for copy in self.line_copies(item):
-            copy.wait_recv()
-        total = self.sums[item, p.a, p.b].astype(F32)
+        p, at = self.place, self.columns[item]
+        self.all_of(self.line.at[:, :, at], item, self.LINE).wait_recv()
+        total = self.sums[p.a, p.b, :, at].astype(F32)
         for k in range(p.A - 1):
-            total += self.line[item, k].astype(F32)
+            total += self.line[k, :, at].astype(F32)
         return total
 
     def finish(self, item):
-        for copy in self.across_copies(item) + self.line_copies(item):
-            copy.wait_send()
+        p, at = self.place, self.columns[item]
+        blocks = self.sums.reshape(p.A * p.B, *self.sums.shape[2:])
+        self.all_of(blocks.at[pl.ds(0, (p.B - 1) * p.A + p.A - 1), :, at], item, self.LINE).wait_send()
 
 
 def block_kernel(
@@ -616,16 +625,28 @@
                 with jax.named_scope("_".join(map(str, (name, el, *more)))):
                     actions[name](el, *more)
 
+    inner = jnp.logical_and(place.a > 0, place.a < A - 1)
+
+    def ends(el):
+        for k in range(1, A):
+            for own in (True, False):
+                each("line_step", el, k, own)
+
     actions = {
         "across": lambda el: each("start_across", el),
         "own": lambda el: each("start_own", el),
         "passed": lambda el: each("across_step", el),
-        "relay": lambda *more: each("line_step", *more),
-        "cots": lambda el: cot_swaps(el),
+        "relay": lambda el, k, own: pl.when(inner)(lambda: each("line_step", el, k, own)),
+        "ends": lambda el: pl.when(jnp.logical_not(inner))(lambda: ends(el)),
+        "cots": lambda el: cot_swaps(el, True, True),
+        "cots_across": lambda el: cot_swaps(el, True, False),
+        "cots_along": lambda el: cot_swaps(el, False, True),
         "rows": lambda el: row_swaps(el),
         "sums": lambda el: all_scatters("core_step", el),
+        "outputs": lambda el: outputs(el, True, True),
+        "outputs_across": lambda el: outputs(el, True, False),
+        "outputs_along": lambda el: outputs(el, False, True),
         "sum_relay": lambda el, step: all_scatters("relay_step", el, step),
-        "outputs": lambda el: give_back(2, el),
     }
     params.start()
     do("start", 0)
@@ -660,7 +681,7 @@
             here, there = (sent_ref, rows_ref) if kind == 0 else (cot_sent_ref, grad_ref)
             source, target = here.at[slot_rows(e), :], there.at[source_rows(el, back), :]
         return pltpu.make_async_remote_copy(
-            src_ref=source, dst_ref=target, send_sem=swap_send.at[kind, el, k], recv_sem=swap_recv.at[kind, el, back],
+            src_ref=source, dst_ref=target, send_sem=swap_send.at[kind, el], recv_sem=swap_recv.at[kind, el, back],
             device_id=place.at_peer(peer), device_id_type=MESH,
         )
 
@@ -670,15 +691,27 @@
         else:
             target = (rows_ref if kind == 0 else grad_ref).at[source_rows(el, k), :]
         pltpu.make_async_remote_copy(
-            src_ref=target, dst_ref=target, send_sem=swap_send.at[kind, el, k], recv_sem=swap_recv.at[kind, el, k],
+            src_ref=target, dst_ref=target, send_sem=swap_send.at[kind, el], recv_sem=swap_recv.at[kind, el, k],
             device_id=place.at_peer(place.other_peer(k)), device_id_type=MESH,
         ).wait_recv()
 
-    def cot_swaps(el):
+    def all_of(kind, send, recv):
+        some = gate_ref.at[pl.ds(0, sources - 1)] if kind == 1 else rows_ref.at[pl.ds(0, (sources - 1) * capacity), :]
+        return pltpu.make_async_remote_copy(
+            src_ref=some, dst_ref=some, send_sem=send, recv_sem=recv,
+            device_id=place.at(place.a, place.b, 1 - place.c), device_id_type=MESH,
+        )
+
+    def cot_swaps(el, across, along):
         @pl.loop(1, sources)
         def _(k):
-            swap(2, el, k).start()
-
+            if across and along:
+                swap(2, el, k).start()
+            else:
+                pl.when((lax.rem(k, xs) == 0) == across)(swap(2, el, k).start)
+
+        if not along:
+            return
         grad_ref[source_rows(el, 0), :] = cot_sent_ref[slot_rows(place.peer * count + el), :]
 
     def row_swaps(el):
@@ -693,7 +726,6 @@
     for k in range(1, A):
         params.line_step(k)
         do("start", k)
-        params.across_step(k - 1)
 
         @pl.loop((k - 1) * experts // (A - 1), k * experts // (A - 1))
         def _(e):
@@ -703,6 +735,8 @@
         if k == 1:
             spread(x_raw, x_ref)
             meta_ref[...] = jnp.transpose(meta_row_ref[...])
+        do("after", k)
+        params.across_step(k - 1)
 
     params.across_step(A - 1)
     params.finish_recv()
@@ -711,15 +745,12 @@
     small = params_ref[:, 4 * width :]
     small_rows = jnp.transpose(small.astype(F32))
 
-    def saves(g):
-        rows = rows_of(g)
+    def saves(rows):
         pairs = (
             (act_one, act_one_save), (weights_ref.at[:, pl.ds(0, HEADS * BLOCK)], weights_save), (attended, attended_save),
             (mid_ref, mid_save), (act_two, act_two_save),
         )
-        return [
-            copy_in(here.at[rows, :], there.at[rows, :], save_sem.at[i, g]) for i, (here, there) in enumerate(pairs)
-        ]
+        return [copy_in(here.at[rows, :], there.at[rows, :], save_sem.at[i]) for i, (here, there) in enumerate(pairs)]
 
     @pl.loop(0, groups)
     def _(g):
@@ -764,7 +795,7 @@
         first, second = gates_of(probs, meta_ref[rows, :])
         gate_rows_ref[0:1, rows] = to_row(first)
         gate_rows_ref[1:2, rows] = to_row(second)
-        for copy in saves(g):
+        for copy in saves(rows):
             copy.start()
 
         for i in range(groups):
@@ -795,10 +826,8 @@
         for at in range(8):
             pl.when(i == at)(functools.partial(do, "dispatch", at))
 
-    @pl.loop(0, groups)
-    def _(g):
-        for copy in saves(g):
-            copy.wait()
+    for copy in saves(pl.ds(0, rows_pad)):
+        copy.wait()
 
     part_up = part_up_ref.at[pl.ds(0, count * width), :].reshape(count, A, B, 2, up_in.shape[1], part_up_ref.shape[1])
     part_down = part_down_ref.at[pl.ds(0, count * hidden_width), :].reshape(count, A, B, 2, down_in.shape[1], width)
@@ -816,7 +845,30 @@
         for scatter in scatters:
             getattr(scatter, step)(el, *more)
 
-    par = Scatter(place, lambda e: part_up.at[0], sums_par, across_par, line_par, par_send, par_recv)
+    pairs = HEADS // 2
+    columns = [slice(3 * LANES * p, 3 * LANES * (p + 1)) for p in range(pairs)]
+    columns += [slice(3 * width, 4 * width), slice(4 * width, 4 * width + LANES)]
+    par_out, par_small = pairs, pairs + 1
+    par = Scatter(place, part_up.at[0], sums_par, across_par, line_par, columns, par_send, par_recv)
+
+    def shares(item):
+        at = columns[item]
+        out = []
+        for k in range(1, xs):
+            to, back = lax.rem(place.x + k, xs), xs - 1 - k
+            out.append(
+                pltpu.make_async_remote_copy(
+                    src_ref=swap_ref.at[place.x, :, at], dst_ref=swap_ref.at[place.x, :, at],
+                    send_sem=share_send.at[item, back], recv_sem=share_recv.at[item, back],
+                    device_id=(to, place.me), device_id_type=MESH,
+                )
+            )
+        return out
+
+    def par_last(item):
+        swap_ref[place.x, :, columns[item]] = par.line_step(item).astype(BF16)
+        for copy in shares(item):
+            copy.start()
 
     def returned(kind, el, k):
         e = place.peer * count + el
@@ -827,7 +879,7 @@
             source, target = here.at[source_rows(el, k), :], there.at[slot_rows(e), :]
         return pltpu.make_async_remote_copy(
             src_ref=source, dst_ref=target,
-            send_sem=return_send.at[kind, el, k], recv_sem=return_recv.at[kind, el, place.seen_from(k)],
+            send_sem=return_send.at[kind, el], recv_sem=return_recv.at[kind, el],
             device_id=place.at_peer(place.other_peer(k)), device_id_type=MESH,
         )
 
@@ -836,15 +888,16 @@
         def _(k):
             returned(kind, el, k).start()
 
-    def return_wait(kind, el):
+    def outputs(el, across, along):
         @pl.loop(1, sources)
         def _(k):
-            e = place.other_peer(k) * count + el
-            target = dots_ref.at[e] if kind == 1 else (grad_slots_ref if kind == 0 else back_ref).at[slot_rows(e), :]
-            pltpu.make_async_remote_copy(
-                src_ref=target, dst_ref=target, send_sem=return_send.at[kind, el, k], recv_sem=return_recv.at[kind, el, k],
-                device_id=place.at_peer(place.other_peer(k)), device_id_type=MESH,
-            ).wait_recv()
+            if across and along:
+                returned(2, el, k).start()
+            else:
+                pl.when((lax.rem(k, xs) == 0) == across)(returned(2, el, k).start)
+
+    def return_wait(kind, el):
+        all_of(kind, return_send.at[kind, el], return_recv.at[kind, el]).wait_recv()
 
     def expert(el):
         blocks = expert_rows // row_block
@@ -914,6 +967,7 @@
 
     for el in range(count):
         expert(el)
+        do("after_expert", el)
 
     def late_loads():
         out = [copy_in(weights_save, up_ref.at[pl.ds(0, rows_pad), :], late_sem.at[0])]
@@ -939,8 +993,15 @@
     for kind in range(2):
         for el in range(count):
             return_wait(kind, el)
-    give_back(2, count - 1)
+    for el in range(count):
+        do("returned", el)
     all_scatters("relay_step", count - 1, 0)
+    for el in range(count):
+        for kind in range(3):
+            all_of(kind, swap_send.at[kind, el], return_recv.at[kind, el]).wait_send()
+
+    grad_attended_ref = sent_ref.at[pl.ds(0, rows_pad), :]
+    branch_ref = cot_sent_ref.at[pl.ds(0, rows_pad), :]
     gain_one = small_rows[NORM_LANE : NORM_LANE + 1]
     gain_two = small_rows[NORM_LANE + 2 : NORM_LANE + 3]
     column_ref[...] = jnp.zeros_like(column_ref)
@@ -953,17 +1014,21 @@
 
     def last_sums(g):
         with jax.named_scope("last_sums_%d" % g):
-            if g == 0 and count > 1:
-                all_scatters("line_step", count - 2)
-            if g == 1:
-                all_scatters("relay_step", count - 1, 1)
+            last = count - 1
             if g == 3:
-                all_scatters("relay_step", count - 1, 2)
-
-    def store(i, g):
-        rows = rows_of(g)
+                pl.when(jnp.logical_not(inner))(lambda: all_scatters("relay_step", last, 1))
+                if count > 1:
+                    all_scatters("line_step", last - 1)
+            if g == 4:
+                pl.when(inner)(lambda: all_scatters("relay_step", last, 1))
+            if g == 5:
+                pl.when(jnp.logical_not(inner))(lambda: all_scatters("relay_step", last, 2))
+            if g == 7:
+                pl.when(inner)(lambda: all_scatters("relay_step", last, 2))
+
+    def store(i, rows):
         here, there = ((cot_ref, out_out), (input_grad_ref, input_grad_out))[i]
-        return copy_in(here.at[rows, :], there.at[rows, :], store_sem.at[i, g])
+        return copy_in(here.at[rows, :], there.at[rows, :], store_sem.at[i])
 
     @pl.loop(0, groups)
     def _(g):
@@ -993,48 +1058,82 @@
         column_ref[NORM_LANE + 3 : NORM_LANE + 4, :] += jnp.sum(grad_act, axis=0, keepdims=True)
         grad_mid = cot_ref[rows, :].astype(F32) + denormalize(grad_act, normed, inverse, gain_two)
         input_grad_ref[rows, :] = grad_mid
-        grad_attended = dot_against(grad_mid.astype(BF16), params_ref[:, 3 * width : 4 * width]).astype(BF16)
-        low = lane < HEAD_DIM
-        for pair in range(HEADS // 2):
-            at = pair * LANES
-            q = triple_ref[rows, at : at + LANES] * HEAD_DIM ** (-0.5)
-            k = triple_ref[rows, width + at : width + at + LANES]
-            v = triple_ref[rows, 2 * width + at : 2 * width + at + LANES]
-            upstream = grad_attended[:, at : at + LANES]
-            grad_q = grad_k = grad_v = jnp.zeros((BLOCK, LANES), F32)
-            for half in range(2):
-                mask = low if half == 0 else jnp.logical_not(low)
-                upstream_half = jnp.where(mask, upstream, 0.0).astype(BF16)
-                head = (2 * pair + half) * BLOCK
-                weights = weights_ref[rows, head : head + BLOCK]
-                kept = weights.astype(F32)
-                grad_weights = dot_against(upstream_half, v)
-                inner = jnp.sum(grad_weights * kept, axis=-1, keepdims=True)
-                grad_scores = (kept * (grad_weights - inner)).astype(BF16)
-                grad_q += dot(grad_scores, jnp.where(mask, k, 0.0).astype(BF16))
-                grad_k += dot_rows(grad_scores, jnp.where(mask, q, 0.0).astype(BF16))
-                grad_v += dot_rows(weights, upstream_half)
-            triple_ref[rows, at : at + LANES] = (grad_q * HEAD_DIM ** (-0.5)).astype(BF16)
-            triple_ref[rows, width + at : width + at + LANES] = grad_k.astype(BF16)
-            triple_ref[rows, 2 * width + at : 2 * width + at + LANES] = grad_v.astype(BF16)
+        branch_ref[rows, :] = grad_mid.astype(BF16)
+        grad_attended = dot_against(branch_ref[rows, :], params_ref[:, 3 * width : 4 * width])
+        grad_attended_ref[rows, :] = grad_attended.astype(BF16)
+        for i in range(groups):
+            pl.when(g == i)(functools.partial(last_sums, i))
+
+    split = (A, B, 2, up_in.shape[1])
+
+    def put(item, value):
+        at = columns[item]
+        part_up[0, :, :, :, :, at] = value.astype(BF16).reshape(*split, at.stop - at.start)
+        par.start(item)
+
+    put(par_out, dot_rows(attended[...], branch_ref[...]))
+
+    def attention_backward(pair, g):
+        rows = rows_of(g)
+        at = pair * LANES
+        low = iota((BLOCK, LANES), 1) < HEAD_DIM
+        q = triple_ref[rows, at : at + LANES] * HEAD_DIM ** (-0.5)
+        k = triple_ref[rows, width + at : width + at + LANES]
+        v = triple_ref[rows, 2 * width + at : 2 * width + at + LANES]
+        upstream = grad_attended_ref[rows, at : at + LANES]
+        grad_q = grad_k = grad_v = jnp.zeros((BLOCK, LANES), F32)
+        for half in range(2):
+            mask = low if half == 0 else jnp.logical_not(low)
+            upstream_half = jnp.where(mask, upstream, 0.0).astype(BF16)
+            head = (2 * pair + half) * BLOCK
+            weights = weights_ref[rows, head : head + BLOCK]
+            kept = weights.astype(F32)
+            grad_weights = dot_against(upstream_half, v)
+            inner = jnp.sum(grad_weights * kept, axis=-1, keepdims=True)
+            grad_scores = (kept * (grad_weights - inner)).astype(BF16)
+            grad_q += dot(grad_scores, jnp.where(mask, k, 0.0).astype(BF16))
+            grad_k += dot_rows(grad_scores, jnp.where(mask, q, 0.0).astype(BF16))
+            grad_v += dot_rows(weights, upstream_half)
+        triple_ref[rows, at : at + LANES] = (grad_q * HEAD_DIM ** (-0.5)).astype(BF16)
+        triple_ref[rows, width + at : width + at + LANES] = grad_k.astype(BF16)
+        triple_ref[rows, 2 * width + at : 2 * width + at + LANES] = grad_v.astype(BF16)
+
+    def par_steps(*steps):
+        for name, item in steps:
+            with jax.named_scope("%s_%d" % (name, item)):
+                par_last(item) if name == "last" else getattr(par, name + "_step")(item)
+
+    for pair in range(pairs):
+        pl.loop(0, groups)(functools.partial(attention_backward, pair))
+        if pair == 0:
+            par_steps(("core", par_out))
+        elif pair == 1:
+            par_steps(("core", 0))
+        else:
+            par_steps(("across", par_out if pair == 2 else pair - 3), ("core", pair - 1))
+        last_sums(groups + pair)
+        kinds = [triple_ref[:, kind * width + pair * LANES : kind * width + (pair + 1) * LANES] for kind in range(3)]
+        put(pair, dot_rows(act_one[...], jnp.concatenate(kinds, axis=1)))
+
+    @pl.loop(0, groups)
+    def _(g):
+        rows = rows_of(g)
         grad_act = dot_against(triple_ref[rows, :], params_ref[:, : 3 * width])
         normed, inverse = normalize(x_ref[rows, :].astype(F32))
         column_ref[NORM_LANE : NORM_LANE + 1, :] += jnp.sum(grad_act * normed, axis=0, keepdims=True)
         column_ref[NORM_LANE + 1 : NORM_LANE + 2, :] += jnp.sum(grad_act, axis=0, keepdims=True)
-        grad_mid = input_grad_ref[rows, :]
-        x_ref[rows, :] = grad_mid.astype(BF16)
-        input_grad_ref[rows, :] = grad_mid + denormalize(grad_act, normed, inverse, gain_one)
-        store(1, g).start()
-        for i in range(groups):
-            pl.when(g == i)(functools.partial(last_sums, i))
-
-    size = up_in.shape[1]
-    split = (A, B, 2, size)
-    part_up[0, :, :, :, :, : 3 * width] = dot_rows(act_one[...], triple_ref[...]).astype(BF16).reshape(*split, 3 * width)
-    part_up[0, :, :, :, :, 3 * width : 4 * width] = dot_rows(attended[...], x_ref[...]).astype(BF16).reshape(*split, width)
-    small_part = dot_rows(act_two[...], logit_grad_ref[...]) + jnp.transpose(column_ref[...])
-    part_up[0, :, :, :, :, 4 * width :] = small_part.astype(BF16).reshape(*split, LANES)
-    par.start(0)
+        input_grad_ref[rows, :] += denormalize(grad_act, normed, inverse, gain_one)
+        store(1, rows).start()
+
+        @pl.when(g == 0)
+        def _():
+            par_steps(("core", pairs - 1), ("across", pairs - 3))
+
+        @pl.when(g == 2)
+        def _():
+            par_steps(("across", pairs - 2))
+
+    put(par_small, dot_rows(act_two[...], logit_grad_ref[...]) + jnp.transpose(column_ref[...]))
     for el in range(count):
         return_wait(2, el)
 
@@ -1050,49 +1149,32 @@
             place_ref[:, at : at + LANES] = jnp.where(in_first, gate_first, jnp.where(in_second, gate_second, 0.0)).astype(BF16)
         mid = float_ref[pl.ds(pl.multiple_of(rows_pad + g * BLOCK, BLOCK), BLOCK), :]
         cot_ref[rows, :] = (mid + dot(place_ref[...], back_ref[...])).astype(BF16)
-        store(0, g).start()
-
-    pl.loop(0, groups // 2)(combine)
-    par.core_step(0)
-    pl.loop(groups // 2, groups)(combine)
-    par.across_step(0)
-    all_scatters("line_step", count - 1)
-    swap_ref[place.x] = par.line_step(0).astype(BF16)
-
-    def shares():
-        out = []
-        for k in range(1, xs):
-            to, back = lax.rem(place.x + k, xs), xs - 1 - k
-            out.append(
-                pltpu.make_async_remote_copy(
-                    src_ref=swap_ref.at[place.x], dst_ref=swap_ref.at[place.x],
-                    send_sem=share_send.at[back], recv_sem=share_recv.at[back],
-                    device_id=(to, place.me), device_id_type=MESH,
-                )
-            )
-        return out
-
-    for copy in shares():
-        copy.start()
+        store(0, rows).start()
+
+    steps = (
+        [("across", pairs - 1), ("core", par_small)], [("across", par_small)], [], [("last", item) for item in (par_out, *range(pairs), par_small)],
+    )
 
     @pl.loop(0, groups)
     def _(g):
-        for i in range(2):
-            store(i, g).wait()
+        combine(g)
+        pl.when(g == 2)(lambda: all_scatters("line_step", count - 1))
+        for i in range(groups):
+            pl.when(g == i)(functools.partial(par_steps, *steps[i]))
+
+    for i in range(2):
+        store(i, pl.ds(0, rows_pad)).wait()
 
     params.finish_send()
     for el in range(count):
-
-        @pl.loop(1, sources)
-        def _(k):
-            for kind in range(3):
-                swap(kind, el, k).wait_send()
-                returned(kind, el, k).wait_send()
-
+        for kind in range(3):
+            all_of(kind, return_send.at[kind, el], return_recv.at[kind, el]).wait_send()
         all_scatters("finish", el)
-    par.finish(0)
-    for copy in shares():
-        copy.wait()
+    for item in range(len(columns)):
+        par.finish(item)
+    for item in range(len(columns)):
+        for copy in shares(item):
+            copy.wait()
     total = swap_ref[0].astype(F32)
     for i in range(1, xs):
         total += swap_ref[i].astype(F32)
@@ -1108,7 +1190,10 @@
         here, there = slice(g * BLOCK, g * BLOCK + GROUP_ROWS), slice(g * GROUP_ROWS, (g + 1) * GROUP_ROWS)
         out[there, :] = out_pad[here, :]
         input_grad[there, :] = input_grad_pad[here, :]
-    qkv[...] = share[:, : 3 * width]
+    for pair in range(HEADS // 2):
+        for kind in range(3):
+            here, there = (3 * pair + kind) * LANES, kind * width + pair * LANES
+            qkv[:, there : there + LANES] = share[:, here : here + LANES]
     out_weight[...] = share[:, 3 * width : 4 * width]
     small = jnp.transpose(share[:, 4 * width :])
     router[...] = small[:experts, :]
@@ -1143,6 +1228,7 @@
     up_rows, down_rows = expert_up.shape[1], expert_down.shape[1]
     hidden_width = expert_up.shape[2]
     packed_width = 4 * width + LANES
+    items = HEADS // 2 + 2
     expert_rows = sources * capacity
     row_block = max(n for n in range(capacity, MAX_ROWS + 1, capacity) if expert_rows % n == 0)
     routes_of = 3 + B - 1
@@ -1181,16 +1267,15 @@
             buffer(max(2 * row_block, 2 * rows_pad), width, dtype=F32),
             buffer(count, A, B, up_rows, hidden_width), buffer(count, A, B, down_rows, width),
             buffer(count, 2, A - 1, B, up_rows, hidden_width), buffer(count, 2, A - 1, B, down_rows, width),
-            buffer(1, A, B, up_rows, packed_width), buffer(1, B - 1, A, up_rows, packed_width),
-            buffer(1, A - 1, up_rows, packed_width), buffer(peers, up_rows, packed_width),
+            buffer(A, B, up_rows, packed_width), buffer(B - 1, A, up_rows, packed_width),
+            buffer(A - 1, up_rows, packed_width), buffer(peers, up_rows, packed_width),
             buffer(BLOCK, BLOCK, dtype=F32), buffer(8, rows_pad, dtype=F32), buffer(8, places, dtype=F32),
             buffer(BLOCK, places), buffer(row_block, width), buffer(rows_pad, LANES), buffer(LANES, width, dtype=F32),
-            dma((2,)), dma((5, groups)), dma((6,)), dma((2, groups)),
-            dma((fsdp, routes_of)), dma((fsdp,)), dma,
-            dma((2, count, fsdp, routes_of)), dma((2, count, fsdp)), dma((2, count)),
-            dma((3, count, sources)), dma((3, count, sources)), dma((3, count, sources)), dma((3, count, sources)),
-            dma((2, count, 2 * A + B - 2)), dma((2, count, 2 * A + B - 2)), dma((2, count)),
-            dma((1, A + B - 1)), dma((1, A + B - 1)), dma((peers - 1,)), dma((peers - 1,)),
+            dma((2,)), dma((5,)), dma((6,)), dma((2,)), dma((routes_of,)), dma((A * B + 1,)), dma,
+            dma((2, count, routes_of)), dma((2, count, A * B + 1)), dma((2, count)),
+            dma((3, count)), dma((3, count, sources)), dma((3, count)), dma((3, count)),
+            dma((2, count, 3 + B - 1)), dma((2, count, 2 * A + B - 2)), dma((2, count)),
+            dma((items, 2)), dma((items, 3)), dma((items, peers - 1)), dma((items, peers - 1)),
         ],
         compiler_params=pltpu.CompilerParams(vmem_limit_bytes=VMEM_LIMIT, collective_id=0, has_side_effects=True),
         name="encoder_block",

time: 199 us -> 185 us (0.930)
  Pallas kernels: 196 us -> 182 us
    pallas_call x1, Pallas kernels: 191 us -> 177 us  [on_device(): pl.pallas_call(functools.partial(block_kernel, experts, fsdp, peers, coun...]
where the time goes in v6:
time: 185 us; the launch traced here: 183 us
  Pallas kernels  182 us (98%)
    pallas_call x1, Pallas kernels, on_device(): pl.pallas_call(functools.partial(block_kernel, experts, fsdp, peers, coun...  177 us
    pallas_call x1, Pallas kernels, on_device(): pl.pallas_call(functools.partial(finish_kernel, experts), out_shape=(shap...  4.78 us

profile of v6, /device:TPU:28, one launch (start us, length us, event | category | flops | bytes accessed | tf_op | source)
XLA Modules:
  0.0 182.6 jit_solution(14375167267853951149)
XLA Ops:
  0.6 177.1 %encoder_block.1 = (bf16[1024,512]{1,0:T(8,128)(2,1)}, f32[1024,512]{1,0:T(8,128)}, f32[32,2176]{1,0:T(8,128)}, bf16[4,32,2048]{2,1,0:T(8,128)(2,1)}, bf16[4,128...) custom-call(bf16[980,512]{1,0:T(8,128)(2,1)} %x_in.1, ...), custom_call_target="tpu_custom_call" | custom-call | tf_op jit(solution)/shard_map/encoder_block/pallas_call | solution.py:1240
  177.8 4.8 %results.1 = (bf16[980,512]{1,0:T(8,128)(2,1)}, f32[980,512]{1,0:T(8,128)}, f32[32,1536]{1,0:T(8,128)}, f32[32,512]{1,0:T(8,128)}, f32[8,32]{1,0:T(8,128)}, /*in...) custom-call(bf16[1024,512]{1,0:T(8,128)(2,1)} %get-tuple-element.27., ...), custom_call_target="tpu_custom_call" | custom-call | tf_op jit(solution)/shard_map/results/pallas_call | solution.py:1287

commit v7 on v6

--- a/solution.py
+++ b/solution.py
@@ -29,22 +29,24 @@
     ("start", 1): [("own", 0)],
     ("start", 3): [("passed", 0)],
     ("after", 3): [("relay", 0, 1, True)],
-    ("begin", 0): [("cots", 0)],
+    ("after", 1): [("cots", 0, "x"), ("cots", 1, "x")],
+    ("begin", 0): [("cots", 0, "y", "far")],
     ("end", 0): [("relay", 0, 1, False)],
     ("middle", 1): [("relay", 0, 2, True)],
     ("end", 1): [("across", 1)],
-    ("end", 2): [("relay", 0, 2, False), ("cots_across", 1)],
+    ("end", 2): [("relay", 0, 2, False), ("cots", 1, "y")],
     ("dispatch", 7): [("own", 1), ("passed", 1), ("ends", 0)],
     ("expert", 0, 0): [("relay", 1, 1, True)],
-    ("expert", 0, 1): [("rows", 1), ("relay", 1, 1, False)],
-    ("expert", 0, 3): [("cots_along", 1), ("relay", 1, 2, True)],
+    ("expert", 0, 1): [("relay", 1, 1, False)],
+    ("expert", 0, 2): [("rows", 1)],
+    ("expert", 0, 3): [("cots", 1, "far"), ("relay", 1, 2, True)],
     ("expert", 0, 4): [("relay", 1, 2, False)],
-    ("expert", 0, 7): [("ends", 1)],
-    ("expert", 1, 0): [("sums", 0), ("sum_relay", 0, 0)],
-    ("expert", 1, 4): [("sum_relay", 0, 1)],
-    ("after_expert", 1): [("outputs_across", 0)],
-    ("returned", 0): [("outputs_along", 0)],
-    ("returned", 1): [("outputs", 1)],
+    ("after_expert", 0): [("sums", 0), ("sum_relay", 0, 0), ("ends", 1)],
+    ("expert", 1, 2): [("sum_relay", 0, 1)],
+    ("expert", 1, 7): [("sum_relay", 0, 2)],
+    ("after_expert", 1): [("outputs", 0, "y")],
+    ("returned", 0): [("outputs", 0, "x", "far")],
+    ("returned", 1): [("outputs", 1, "x", "y", "far")],
 }
 F32 = jnp.float32
 BF16 = jnp.bfloat16
@@ -638,14 +640,10 @@
         "passed": lambda el: each("across_step", el),
         "relay": lambda el, k, own: pl.when(inner)(lambda: each("line_step", el, k, own)),
         "ends": lambda el: pl.when(jnp.logical_not(inner))(lambda: ends(el)),
-        "cots": lambda el: cot_swaps(el, True, True),
-        "cots_across": lambda el: cot_swaps(el, True, False),
-        "cots_along": lambda el: cot_swaps(el, False, True),
+        "cots": lambda el, *which: cot_swaps(el, *which),
         "rows": lambda el: row_swaps(el),
         "sums": lambda el: all_scatters("core_step", el),
-        "outputs": lambda el: outputs(el, True, True),
-        "outputs_across": lambda el: outputs(el, True, False),
-        "outputs_along": lambda el: outputs(el, False, True),
+        "outputs": lambda el, *which: outputs(el, *which),
         "sum_relay": lambda el, step: all_scatters("relay_step", el, step),
     }
     params.start()
@@ -702,16 +700,20 @@
             device_id=place.at(place.a, place.b, 1 - place.c), device_id_type=MESH,
         )
 
-    def cot_swaps(el, across, along):
+    def peers_where(which, act):
         @pl.loop(1, sources)
         def _(k):
-            if across and along:
-                swap(2, el, k).start()
-            else:
-                pl.when((lax.rem(k, xs) == 0) == across)(swap(2, el, k).start)
-
-        if not along:
-            return
+            for name, same in (("x", lax.div(k, xs) == 0), ("y", lax.rem(k, xs) == 0)):
+                if which == name:
+                    pl.when(same)(lambda: act(k))
+            if which == "far":
+                pl.when(jnp.logical_and(lax.div(k, xs) > 0, lax.rem(k, xs) > 0))(lambda: act(k))
+
+    def cot_swaps(el, *which):
+        for peers in which:
+            peers_where(peers, lambda k: swap(2, el, k).start())
+
+    def cot_own(el):
         grad_ref[source_rows(el, 0), :] = cot_sent_ref[slot_rows(place.peer * count + el), :]
 
     def row_swaps(el):
@@ -728,7 +730,8 @@
         do("start", k)
 
         @pl.loop((k - 1) * experts // (A - 1), k * experts // (A - 1))
-        def _(e):
+        def _(i):
+            e = place.other_peer(lax.rem(lax.div(i, count) + 1, sources)) * count + lax.rem(i, count)
             _, _, picks = find(e)
             cot_sent_ref[slot_rows(e), :] = dot(picks, cot_ref[...]).astype(BF16)
 
@@ -740,6 +743,8 @@
 
     params.across_step(A - 1)
     params.finish_recv()
+    for el in range(count):
+        cot_own(el)
     do("begin", 0)
 
     small = params_ref[:, 4 * width :]
@@ -888,13 +893,9 @@
         def _(k):
             returned(kind, el, k).start()
 
-    def outputs(el, across, along):
-        @pl.loop(1, sources)
-        def _(k):
-            if across and along:
-                returned(2, el, k).start()
-            else:
-                pl.when((lax.rem(k, xs) == 0) == across)(returned(2, el, k).start)
+    def outputs(el, *which):
+        for peers in which:
+            peers_where(peers, lambda k: returned(2, el, k).start())
 
     def return_wait(kind, el):
         all_of(kind, return_send.at[kind, el], return_recv.at[kind, el]).wait_recv()
@@ -931,8 +932,9 @@
                 spread = 0.5 * (1.0 + lax.erf(hidden * ROOT_HALF))
                 active = (hidden * spread).astype(BF16)
                 slope = spread + hidden * (DENSITY_SCALE * jnp.exp(-0.5 * hidden * hidden))
+                grad_active = dot_against(grads, down_part)
                 float_ref[:row_block, :] += dot(active, down_part)
-                grad_hidden = (dot_against(grads, down_part) * slope).astype(BF16)
+                grad_hidden = (grad_active * slope).astype(BF16)
                 float_ref[row_block : 2 * row_block, :] += dot_against(grad_hidden, up_part)
                 size = up_in.shape[1]
                 up_sum = dot_rows(rows, grad_hidden).reshape(A, B, 2, size, FF_CHUNK)
@@ -986,8 +988,7 @@
     weights_ref = up_ref
     input_grad_ref = float_ref
     all_scatters("core_step", count - 1)
-    if count > 1:
-        all_scatters("relay_step", count - 2, 2)
+    all_scatters("relay_step", count - 1, 0)
     for copy in late_loads():
         copy.wait()
     for kind in range(2):
@@ -995,7 +996,6 @@
             return_wait(kind, el)
     for el in range(count):
         do("returned", el)
-    all_scatters("relay_step", count - 1, 0)
     for el in range(count):
         for kind in range(3):
             all_of(kind, swap_send.at[kind, el], return_recv.at[kind, el]).wait_send()
@@ -1021,7 +1021,7 @@
                     all_scatters("line_step", last - 1)
             if g == 4:
                 pl.when(inner)(lambda: all_scatters("relay_step", last, 1))
-            if g == 5:
+            if g == 6:
                 pl.when(jnp.logical_not(inner))(lambda: all_scatters("relay_step", last, 2))
             if g == 7:
                 pl.when(inner)(lambda: all_scatters("relay_step", last, 2))
@@ -1107,10 +1107,8 @@
         pl.loop(0, groups)(functools.partial(attention_backward, pair))
         if pair == 0:
             par_steps(("core", par_out))
-        elif pair == 1:
-            par_steps(("core", 0))
         else:
-            par_steps(("across", par_out if pair == 2 else pair - 3), ("core", pair - 1))
+            par_steps(("core", pair - 1))
         last_sums(groups + pair)
         kinds = [triple_ref[:, kind * width + pair * LANES : kind * width + (pair + 1) * LANES] for kind in range(3)]
         put(pair, dot_rows(act_one[...], jnp.concatenate(kinds, axis=1)))
@@ -1127,7 +1125,7 @@
 
         @pl.when(g == 0)
         def _():
-            par_steps(("core", pairs - 1), ("across", pairs - 3))
+            par_steps(("core", pairs - 1), ("across", par_out), *[("across", pair) for pair in range(pairs - 2)])
 
         @pl.when(g == 2)
         def _():

time: 185 us -> 178 us (0.962)
  Pallas kernels: 182 us -> 174 us
    pallas_call x1, Pallas kernels: 177 us -> 169 us  [on_device(): pl.pallas_call(functools.partial(block_kernel, experts, fsdp, peers, coun...]
where the time goes in v7:
time: 178 us; the launch traced here: 175 us
  Pallas kernels  174 us (98%)
    pallas_call x1, Pallas kernels, on_device(): pl.pallas_call(functools.partial(block_kernel, experts, fsdp, peers, coun...  169 us
    pallas_call x1, Pallas kernels, on_device(): pl.pallas_call(functools.partial(finish_kernel, experts), out_shape=(shap...  4.78 us

profile of v7, /device:TPU:28, one launch (start us, length us, event | category | flops | bytes accessed | tf_op | source)
XLA Modules:
  0.0 174.9 jit_solution(10743449483803909414)
XLA Ops:
  0.6 169.4 %encoder_block.1 = (bf16[1024,512]{1,0:T(8,128)(2,1)}, f32[1024,512]{1,0:T(8,128)}, f32[32,2176]{1,0:T(8,128)}, bf16[4,32,2048]{2,1,0:T(8,128)(2,1)}, bf16[4,128...) custom-call(bf16[980,512]{1,0:T(8,128)(2,1)} %x_in.1, ...), custom_call_target="tpu_custom_call" | custom-call | tf_op jit(solution)/shard_map/encoder_block/pallas_call | solution.py:1238
  170.1 4.8 %results.1 = (bf16[980,512]{1,0:T(8,128)(2,1)}, f32[980,512]{1,0:T(8,128)}, f32[32,1536]{1,0:T(8,128)}, f32[32,512]{1,0:T(8,128)}, f32[8,32]{1,0:T(8,128)}, /*in...) custom-call(bf16[1024,512]{1,0:T(8,128)(2,1)} %get-tuple-element.27., ...), custom_call_target="tpu_custom_call" | custom-call | tf_op jit(solution)/shard_map/results/pallas_call | solution.py:1285

commit v8 on v7

--- a/solution.py
+++ b/solution.py
@@ -551,16 +551,16 @@
 
 def block_kernel(
     experts, fsdp, xs, count,
-    x_in, cot_in, routes_ref, slots_ref, qkv_ref, out_ref, router_ref, gain_one_ref, shift_one_ref, gain_two_ref, shift_two_ref,
+    x_raw, cot_raw, routes_ref, slots_ref, qkv_ref, out_ref, router_ref, gain_one_ref, shift_one_ref, gain_two_ref, shift_two_ref,
     up_in, down_in,
     out_out, input_grad_out, share_out, up_grad_out, down_grad_out,
     act_one_save, weights_save, attended_save, mid_save, act_two_save,
-    x_raw, cot_raw, shard_ref, meta_row_ref, meta_ref, x_ref, params_ref, triple_ref, probs_ref,
+    shard_ref, meta_row_ref, meta_ref, x_ref, params_ref, triple_ref, probs_ref,
     sent_ref, cot_sent_ref, gate_sent_ref, rows_ref, grad_ref, gate_ref, back_ref, grad_slots_ref, dots_sent_ref, dots_ref,
     up_ref, down_ref, part_up_ref, part_down_ref, float_ref,
     sums_up, sums_down, line_up, line_down, sums_par, across_par, line_par, swap_ref,
     bias_ref, gate_rows_ref, dot_row_ref, place_ref, gated_ref, logit_grad_ref, column_ref,
-    load_sem, save_sem, late_sem, store_sem, par_gather_send, par_gather_recv, par_gather_local,
+    save_sem, late_sem, store_sem, par_gather_send, par_gather_recv, par_gather_local,
     gather_send, gather_recv, gather_local, swap_send, swap_recv, return_send, return_recv,
     scatter_send, scatter_recv, scatter_local, par_send, par_recv, share_send, share_recv,
 ):
@@ -580,10 +580,6 @@
     weights_ref = part_up_ref
     act_one, attended, act_two, cot_ref = (part_down_ref.at[pl.ds(i * rows_pad, rows_pad), :] for i in range(4))
     mid_ref = float_ref
-
-    loads = [copy_in(x_in, x_raw, load_sem.at[0]), copy_in(cot_in, cot_raw, load_sem.at[1])]
-    for copy in loads:
-        copy.start()
 
     def spread(raw, there):
         for g in range(groups):
@@ -722,8 +718,6 @@
             swap(0, el, k).start()
             swap(1, el, k).start()
 
-    for copy in loads:
-        copy.wait()
     spread(cot_raw, cot_ref)
     for k in range(1, A):
         params.line_step(k)
@@ -1015,15 +1009,15 @@
     def last_sums(g):
         with jax.named_scope("last_sums_%d" % g):
             last = count - 1
+            if g == 2:
+                pl.when(jnp.logical_not(inner))(lambda: all_scatters("relay_step", last, 1))
             if g == 3:
-                pl.when(jnp.logical_not(inner))(lambda: all_scatters("relay_step", last, 1))
+                pl.when(inner)(lambda: all_scatters("relay_step", last, 1))
                 if count > 1:
                     all_scatters("line_step", last - 1)
             if g == 4:
-                pl.when(inner)(lambda: all_scatters("relay_step", last, 1))
+                pl.when(jnp.logical_not(inner))(lambda: all_scatters("relay_step", last, 2))
             if g == 6:
-                pl.when(jnp.logical_not(inner))(lambda: all_scatters("relay_step", last, 2))
-            if g == 7:
                 pl.when(inner)(lambda: all_scatters("relay_step", last, 2))
 
     def store(i, rows):
@@ -1156,7 +1150,7 @@
     @pl.loop(0, groups)
     def _(g):
         combine(g)
-        pl.when(g == 2)(lambda: all_scatters("line_step", count - 1))
+        pl.when(g == 1)(lambda: all_scatters("line_step", count - 1))
         for i in range(groups):
             pl.when(g == i)(functools.partial(par_steps, *steps[i]))
 
@@ -1249,10 +1243,10 @@
             shape((rows_pad, width), F32),
             shape((rows_pad, width), BF16),
         ),
-        in_specs=[hbm] * 2 + [vmem] * 9 + [hbm] * 2,
+        in_specs=[vmem] * 11 + [hbm] * 2,
         out_specs=[hbm] * 2 + [vmem] + [hbm] * 7,
         scratch_shapes=[
-            buffer(rows_dev, width), buffer(rows_dev, width), buffer(up_rows, packed_width),
+            buffer(up_rows, packed_width),
             buffer(8, rows_pad, dtype=jnp.int32), buffer(rows_pad, 8, dtype=jnp.int32),
             buffer(rows_pad, width), buffer(fsdp * up_rows, packed_width), buffer(rows_pad, 3 * width),
             buffer(rows_pad, LANES, dtype=F32),
@@ -1269,7 +1263,7 @@
             buffer(A - 1, up_rows, packed_width), buffer(peers, up_rows, packed_width),
             buffer(BLOCK, BLOCK, dtype=F32), buffer(8, rows_pad, dtype=F32), buffer(8, places, dtype=F32),
             buffer(BLOCK, places), buffer(row_block, width), buffer(rows_pad, LANES), buffer(LANES, width, dtype=F32),
-            dma((2,)), dma((5,)), dma((6,)), dma((2,)), dma((routes_of,)), dma((A * B + 1,)), dma,
+            dma((5,)), dma((6,)), dma((2,)), dma((routes_of,)), dma((A * B + 1,)), dma,
             dma((2, count, routes_of)), dma((2, count, A * B + 1)), dma((2, count)),
             dma((3, count)), dma((3, count, sources)), dma((3, count)), dma((3, count)),
             dma((2, count, 3 + B - 1)), dma((2, count, 2 * A + B - 2)), dma((2, count)),

time: 178 us -> 177 us (level)
  no operation moved by 1% of the time
where the time goes in v8:
time: 177 us; the launch traced here: 174 us
  Pallas kernels  173 us (98%)
    pallas_call x1, Pallas kernels, on_device(): pl.pallas_call(functools.partial(block_kernel, experts, fsdp, peers, coun...  168 us
    pallas_call x1, Pallas kernels, on_device(): pl.pallas_call(functools.partial(finish_kernel, experts), out_shape=(shap...  4.78 us

profile of v8, /device:TPU:28, one launch (start us, length us, event | category | flops | bytes accessed | tf_op | source)
XLA Modules:
  0.0 173.9 jit_solution(3753450438432339961)
XLA Ops:
  0.6 168.5 %encoder_block.1 = (bf16[1024,512]{1,0:T(8,128)(2,1)}, f32[1024,512]{1,0:T(8,128)}, f32[32,2176]{1,0:T(8,128)}, bf16[4,32,2048]{2,1,0:T(8,128)(2,1)}, bf16[4,128...) custom-call(bf16[980,512]{1,0:T(8,128)(2,1)} %x_raw.1, ...), custom_call_target="tpu_custom_call" | custom-call | tf_op jit(solution)/shard_map/encoder_block/pallas_call | solution.py:1232
  169.1 4.8 %results.1 = (bf16[980,512]{1,0:T(8,128)(2,1)}, f32[980,512]{1,0:T(8,128)}, f32[32,1536]{1,0:T(8,128)}, f32[32,512]{1,0:T(8,128)}, f32[8,32]{1,0:T(8,128)}, /*in...) custom-call(bf16[1024,512]{1,0:T(8,128)(2,1)} %get-tuple-element.27., ...), custom_call_target="tpu_custom_call" | custom-call | tf_op jit(solution)/shard_map/results/pallas_call | solution.py:1279

commit v9 on v8

--- a/solution.py
+++ b/solution.py
@@ -1032,10 +1032,12 @@
         lane = iota((BLOCK, LANES), 1)
         grad_first = jnp.zeros((BLOCK, LANES), F32)
         grad_second = jnp.zeros((BLOCK, LANES), F32)
+        first_slot = jnp.broadcast_to(meta[:, 0:1], (BLOCK, LANES))
+        second_slot = jnp.broadcast_to(meta[:, 1:2], (BLOCK, LANES))
         for c in range(places // LANES):
             at = c * LANES
-            in_first = lane == meta[:, 0:1] - at
-            in_second = lane == meta[:, 1:2] - at
+            in_first = lane + at == first_slot
+            in_second = lane + at == second_slot
             place_ref[:, at : at + LANES] = jnp.where(jnp.logical_or(in_first, in_second), 1.0, 0.0).astype(BF16)
             dots = dot_row_ref[0:1, at : at + LANES]
             grad_first += jnp.where(in_first, dots, 0.0)
@@ -1134,10 +1136,12 @@
         meta = meta_ref[rows, :]
         gate_first, gate_second = gates_of(probs_ref[rows, :], meta)
         lane = iota((BLOCK, LANES), 1)
+        first_slot = jnp.broadcast_to(meta[:, 0:1], (BLOCK, LANES))
+        second_slot = jnp.broadcast_to(meta[:, 1:2], (BLOCK, LANES))
         for c in range(places // LANES):
             at = c * LANES
-            in_first = lane == meta[:, 0:1] - at
-            in_second = lane == meta[:, 1:2] - at
+            in_first = lane + at == first_slot
+            in_second = lane + at == second_slot
             place_ref[:, at : at + LANES] = jnp.where(in_first, gate_first, jnp.where(in_second, gate_second, 0.0)).astype(BF16)
         mid = float_ref[pl.ds(pl.multiple_of(rows_pad + g * BLOCK, BLOCK), BLOCK), :]
         cot_ref[rows, :] = (mid + dot(place_ref[...], back_ref[...])).astype(BF16)

time: 177 us -> 177 us (level)
  no operation moved by 1% of the time
where the time goes in v9:
time: 177 us; the launch traced here: 174 us
  Pallas kernels  173 us (98%)
    pallas_call x1, Pallas kernels, on_device(): pl.pallas_call(functools.partial(block_kernel, experts, fsdp, peers, coun...  168 us
    pallas_call x1, Pallas kernels, on_device(): pl.pallas_call(functools.partial(finish_kernel, experts), out_shape=(shap...  4.78 us

profile of v9, /device:TPU:28, one launch (start us, length us, event | category | flops | bytes accessed | tf_op | source)
XLA Modules:
  0.0 173.9 jit_solution(7779313236731890922)
XLA Ops:
  0.6 168.5 %encoder_block.1 = (bf16[1024,512]{1,0:T(8,128)(2,1)}, f32[1024,512]{1,0:T(8,128)}, f32[32,2176]{1,0:T(8,128)}, bf16[4,32,2048]{2,1,0:T(8,128)(2,1)}, bf16[4,128...) custom-call(bf16[980,512]{1,0:T(8,128)(2,1)} %x_raw.1, ...), custom_call_target="tpu_custom_call" | custom-call | tf_op jit(solution)/shard_map/encoder_block/pallas_call | solution.py:1236
  169.1 4.8 %results.1 = (bf16[980,512]{1,0:T(8,128)(2,1)}, f32[980,512]{1,0:T(8,128)}, f32[32,1536]{1,0:T(8,128)}, f32[32,512]{1,0:T(8,128)}, f32[8,32]{1,0:T(8,128)}, /*in...) custom-call(bf16[1024,512]{1,0:T(8,128)(2,1)} %get-tuple-element.27., ...), custom_call_target="tpu_custom_call" | custom-call | tf_op jit(solution)/shard_map/results/pallas_call | solution.py:1283
